TPU v7x, 256 devices: a whole 4x4x8 slice. The times are simulated.
256 devices in a mesh: row: 8 (over y, core), col: 32 (over x, z).
Axes of the slice: x: 4, y: 4, z: 8, core: 2. Of those that a mesh axis runs over, the one named last changes fastest.
Arguments:
- gradient: bfloat16 [3584, 12288], P('row', 'col'), may hold values from -54 to 54
- momentum: float32 [3584, 12288], P('row', 'col'), may hold values from -54 to 54
Outputs:
- update_matrix: bfloat16 [3584, 12288], P('row', 'col')
- new_momentum: float32 [3584, 12288], P('row', 'col')
All inputs are finite; a program needn't handle non-finite values.
Results may differ from a plain program's by a relative error of at most 0.013.
Values may be sent and summed in bfloat16 or wider, within the bound.
No kernel may reach another device: no remote copies, remote signals or barrier semaphores. Data moves between devices by JAX's collectives and lax.ppermute only.
A program may use at most 64 MiB of HBM per device.

v0:
```python
import math

import jax
import jax.numpy as jnp
from jax import lax
from jax.sharding import PartitionSpec as P

M = 3584
N = 12288
ITERS = 2


MOMENTUM_DECAY = 0.95
EPSILON = 1e-07
COEF_LINEAR = 3.4445
COEF_CUBIC = -4.775
COEF_QUINTIC = 2.0315


def outer_rows(left, right):
    return lax.dot_general(
        left, right, (((1,), (1,)), ((), ())), preferred_element_type=jnp.float32
    )


def per_device(gradient, momentum):
    grad32 = gradient.astype(jnp.float32)
    buffer = MOMENTUM_DECAY * momentum + grad32
    nesterov = grad32 + MOMENTUM_DECAY * buffer
    iterate = nesterov.astype(jnp.bfloat16)
    combined = iterate.astype(jnp.float32)
    for iteration in range(ITERS):
        panel = lax.all_gather(iterate, "row", axis=0, tiled=True)
        partial_value = outer_rows(iterate, panel)
        shares = lax.psum_scatter(
            partial_value.astype(jnp.bfloat16), "col", scatter_dimension=1, tiled=True
        ).astype(jnp.float32)
        weights = jnp.ones((1, shares.shape[1]), jnp.float32)
        if iteration == 0:
            quartic = lax.psum(jnp.sum(weights * shares * shares), ("row", "col"))
            scale = 1.0 / jnp.sqrt(jnp.sqrt(quartic) + EPSILON)
            shares = shares * (scale * scale)
            iterate = (iterate.astype(jnp.float32) * scale).astype(jnp.bfloat16)
            panel = (panel.astype(jnp.float32) * scale).astype(jnp.bfloat16)
        gram = lax.all_gather(shares.astype(jnp.bfloat16), "col", axis=1, tiled=True)
        product = jnp.dot(gram, panel, preferred_element_type=jnp.float32)
        product_panel = lax.all_gather(product.astype(jnp.bfloat16), "row", axis=0, tiled=True)
        second = jnp.dot(gram, product_panel, preferred_element_type=jnp.float32)
        combined = (
            COEF_LINEAR * iterate.astype(jnp.float32) + COEF_CUBIC * product + COEF_QUINTIC * second
        )
        if iteration + 1 < ITERS:
            iterate = combined.astype(jnp.bfloat16)
    update_matrix = (combined * (0.2 * math.sqrt(max(M, N)))).astype(jnp.bfloat16)
    return (update_matrix, buffer)


def solution(mesh):
    return jax.shard_map(
        per_device,
        mesh=mesh,
        in_specs=(P("row", "col"), P("row", "col")),
        out_specs=(P("row", "col"), P("row", "col")),
        check_vma=False,
    )
```

profile of v0, /device:TPU:1, one launch (start us, length us, event | category | flops | bytes accessed | tf_op | source)
XLA Modules:
  0.0 847.7 jit_solution(8898954018869091649)
XLA Ops:
  7.2 0.0 all-gather.7.cloned.1.call-start
  7.2 2.3 fusion.7
  9.5 0.0 all-gather.7.cloned.1.call-update
  9.5 0.0 reduce-scatter.7.cloned.1.call-start
  9.6 34.0 %all-gather.7.cloned.1.call-done = bf16[3584,384]{1,0:T(8,128)(2,1)} async-done(((bf16[448,384]{1,0:T(8,128)(2,1)}), bf16[3584,384]{1,0:T(8,128)(2,1)}) %all-gather.7.cloned.1.call-update) | async-done | bytes 2752528 | tf_op jit(solution)/shard_map/all_gather | solution.py:33
  43.6 3.8 convolution_convert_fusion.1
  47.4 3.6 copy.6
  51.0 0.0 reduce-scatter.7.cloned.1.call-update
  51.0 0.0 all-gather.9.cloned.1.call-start
  51.1 215.7 %reduce-scatter.7.cloned.1.call-done = bf16[112,448]{1,0:T(8,128)(2,1)} async-done(((bf16[3584,448]{1,0:T(8,128)(2,1)}), bf16[112,448]{1,0:T(8,128)(2,1)}) %reduce-scatter.7.cloned.1.call-update) | async-done | bytes 100368
  266.8 1.0 copy.7
  267.8 0.7 fusion.8
  268.6 79.5 %psum.7 = f32[]{:T(128)} all-reduce(f32[]{:T(128)} %fusion.8), channel_id=1, replica_groups=mesh['row'=8,'col'=32] {'row','col'}, use_global_device_ids=true, to_apply=%region_2.0 | all-reduce | flops 1 | bytes 8 | tf_op jit(solution)/shard_map/psum | solution.py:40
  348.9 0.7 copy.4
  349.6 0.0 all-gather.11.cloned.1.call-start
  349.7 74.5 %all-gather.9.cloned.1.call-done = bf16[448,3584]{0,1:T(8,128)(2,1)} async-done(((bf16[448,112]{0,1:T(8,128)(2,1)}), bf16[448,3584]{0,1:T(8,128)(2,1)}) %all-gather.9.cloned.1.call-update) | async-done | bytes 3211280 | tf_op jit(solution)/shard_map/all_gather | solution.py:45
  424.2 4.8 fusion.10
  429.0 0.0 all-gather.11.cloned.1.call-update
  429.1 0.0 all-gather.13.cloned.1.call-start
  429.1 29.6 %all-gather.11.cloned.1.call-done = bf16[3584,384]{1,0:T(8,128)(2,1)} async-done(((bf16[448,384]{1,0:T(8,128)(2,1)}), bf16[3584,384]{1,0:T(8,128)(2,1)}) %all-gather.11.cloned.1.call-update) | async-done | bytes 2752528 | tf_op jit(solution)/shard_map/all_gather | solution.py:47
  458.7 5.6 fusion.5
  464.3 0.0 reduce-scatter.9.cloned.1.call-start
  464.4 29.6 %all-gather.13.cloned.1.call-done = bf16[3584,384]{1,0:T(8,128)(2,1)} async-done(((bf16[448,384]{1,0:T(8,128)(2,1)}), bf16[3584,384]{1,0:T(8,128)(2,1)}) %all-gather.13.cloned.1.call-update) | async-done | bytes 2752528 | tf_op jit(solution)/shard_map/all_gather | solution.py:33
  494.0 3.8 convolution_convert_fusion
  497.8 3.6 copy.8
  501.4 0.0 all-gather.15.cloned.1.call-start
  501.4 215.8 %reduce-scatter.9.cloned.1.call-done = bf16[112,448]{1,0:T(8,128)(2,1)} async-done(((bf16[3584,448]{1,0:T(8,128)(2,1)}), bf16[112,448]{1,0:T(8,128)(2,1)}) %reduce-scatter.9.cloned.1.call-update) | async-done | bytes 100368
  717.3 0.0 all-gather.17.cloned.1.call-start
  717.3 83.4 %all-gather.15.cloned.1.call-done = bf16[448,3584]{0,1:T(8,128)(2,1)} async-done(((bf16[448,112]{0,1:T(8,128)(2,1)}), bf16[448,3584]{0,1:T(8,128)(2,1)}) %all-gather.15.cloned.1.call-update) | async-done | bytes 3211280 | tf_op jit(solution)/shard_map/all_gather | solution.py:45
  800.8 4.8 fusion.11
  805.6 29.7 %all-gather.17.cloned.1.call-done = bf16[3584,384]{1,0:T(8,128)(2,1)} async-done(((bf16[448,384]{1,0:T(8,128)(2,1)}), bf16[3584,384]{1,0:T(8,128)(2,1)}) %all-gather.17.cloned.1.call-update) | async-done | bytes 2752528 | tf_op jit(solution)/shard_map/all_gather | solution.py:47
  835.3 5.6 fusion.6
  (14 shorter events, 0.1 us)
Async XLA Ops:
  7.2 36.5 %all-gather.7.cloned.1.call-start = ((), (), s32[]{:S(2)}) async-start(), calls=%async_computation.2 | async-start | bytes 3096576 | tf_op jit(solution)/shard_map/all_gather | solution.py:33
  9.5 257.3 %reduce-scatter.7.cloned.1.call-start = ((), (), s32[]{:S(2)}) async-start(), calls=%async_computation.8 | async-start | bytes 3784704
  51.0 373.2 %copy-start.2 = (bf16[3584,384]{1,0:T(8,128)(2,1)S(1)}, bf16[3584,384]{1,0:T(8,128)(2,1)}, u32[]{:S(2)}) copy-start(bf16[3584,384]{1,0:T(8,128)(2,1)} %all-gather.7.cloned.1.call-done) | copy-start | bytes 8257540
  51.0 373.2 %all-gather.9.cloned.1.call-start = ((), (), s32[]{:S(2)}) async-start(), calls=%async_computation.3 | async-start | bytes 3784704 | tf_op jit(solution)/shard_map/all_gather | solution.py:45
  349.6 109.1 %copy-start = (bf16[448,384]{1,0:T(8,128)(2,1)S(1)}, bf16[448,384]{1,0:T(8,128)(2,1)}, u32[]{:S(2)}) copy-start(bf16[448,384]{1,0:T(8,128)(2,1)} %get-tuple-element.2) | copy-start | bytes 1032196
  349.6 109.1 %all-gather.11.cloned.1.call-start = ((), (), s32[]{:S(2)}) async-start(), calls=%async_computation.4 | async-start | bytes 3096576 | tf_op jit(solution)/shard_map/all_gather | solution.py:47
  429.1 64.9 %all-gather.13.cloned.1.call-start = ((), (), s32[]{:S(2)}) async-start(), calls=%async_computation.5 | async-start | bytes 3096576 | tf_op jit(solution)/shard_map/all_gather | solution.py:33
  464.3 252.9 %reduce-scatter.9.cloned.1.call-start = ((), (), s32[]{:S(2)}) async-start(), calls=%async_computation.9 | async-start | bytes 3784704
  501.4 299.4 %copy-start.3 = (bf16[3584,384]{1,0:T(8,128)(2,1)S(1)}, bf16[3584,384]{1,0:T(8,128)(2,1)}, u32[]{:S(2)}) copy-start(bf16[3584,384]{1,0:T(8,128)(2,1)} %all-gather.13.cloned.1.call-done) | copy-start | bytes 8257540
  501.4 299.4 %all-gather.15.cloned.1.call-start = ((), (), s32[]{:S(2)}) async-start(), calls=%async_computation.6 | async-start | bytes 3784704 | tf_op jit(solution)/shard_map/all_gather | solution.py:45
  717.3 118.0 %copy-start.1 = (bf16[448,384]{1,0:T(8,128)(2,1)S(1)}, bf16[448,384]{1,0:T(8,128)(2,1)}, u32[]{:S(2)}) copy-start(bf16[448,384]{1,0:T(8,128)(2,1)} %fusion.5) | copy-start | bytes 1032196
  717.3 118.0 %all-gather.17.cloned.1.call-start = ((), (), s32[]{:S(2)}) async-start(), calls=%async_computation.7 | async-start | bytes 3096576 | tf_op jit(solution)/shard_map/all_gather | solution.py:47
Sparse Core Ops, SparseCore 0:
  10.4 33.1 all-gather.6
  51.1 215.6 reduce-scatter.6
  349.7 74.3 all-gather.8
  429.2 29.4 all-gather.10
  464.4 29.4 all-gather.12
  501.5 215.6 reduce-scatter.8
  719.8 80.9 all-gather.14
  805.8 29.4 all-gather.16
where the time goes:
time: 848 us
  waiting for transfers between devices  713 us (84%)
  blocking collectives  79.5 us (9%)
  matrix products  28.4 us (3%)
  between operations  15 us (2%)
  local copies, waits for them, and re-layouts  9.03 us (1%)
    unnamed x10, waiting for transfers between devices  432 us
    all_gather x2, waiting for transfers between devices, per_device(): lax.all_gather(shares.astype(jnp.bfloat16), 'col', axis=1, tiled=True)  158 us
    psum x1, blocking collectives, per_device(): quartic = lax.psum(jnp.sum(weights * shares * shares), ('row', 'col'))  79.5 us
    all_gather x2, waiting for transfers between devices, per_device(): panel = lax.all_gather(iterate, 'row', axis=0, tiled=True)  63.6 us
    all_gather x2, waiting for transfers between devices, per_device(): lax.all_gather(product.astype(jnp.bfloat16), 'row', axis=0, tiled=True)  59.3 us
  transfers between devices with their start and end apart: 8, of which 8 were waited for; matrix products, arithmetic and copies ran while one was open for 0% of the time, Pallas kernels for 0%

commit v1 on v0

v1 whole, which is shorter than its diff:
```python
import functools
import math

import jax
import jax.numpy as jnp
from jax import lax
from jax.experimental import pallas as pl
from jax.experimental.pallas import tpu as pltpu
from jax.sharding import PartitionSpec as P

M = 3584
N = 12288
ROWS = 8
COLS = 32
X_CHIPS = 4
Z_CHIPS = 8

MOMENTUM_DECAY = 0.95
EPSILON = 1e-07
COEF_LINEAR = 3.4445
COEF_CUBIC = -4.775
COEF_QUINTIC = 2.0315
UPDATE_SCALE = 0.2 * math.sqrt(max(M, N))

BLOCK = 512
BLOCKS = M // BLOCK
KEPT = (BLOCKS + 1) // 2
HALF = BLOCK // 2
UNITS = BLOCKS * KEPT * 2 // ROWS
PANEL_COLS = N // COLS
OWN_COLS = PANEL_COLS // ROWS
OWN_ROWS = M // ROWS

X_GROUPS = [[x * Z_CHIPS + z for x in range(X_CHIPS)] for z in range(Z_CHIPS)]
Z_GROUPS = [[x * Z_CHIPS + z for z in range(Z_CHIPS)] for x in range(X_CHIPS)]


def dot_nt(left, right):
    return lax.dot_general(
        left, right, (((1,), (1,)), ((), ())), preferred_element_type=jnp.float32
    )


def gram_kernel(panel_ref, units_ref, columns_ref):
    row = lax.axis_index("row")
    unit = pl.program_id(0)
    number = row * UNITS + unit
    block, half = number // 2, number % 2
    i, d = block // KEPT, block % KEPT
    j = lax.rem(i + d, BLOCKS)
    left = panel_ref[pl.ds(pl.multiple_of(i * BLOCK + half * HALF, HALF), HALF), :]
    right = panel_ref[pl.ds(pl.multiple_of(j * BLOCK, BLOCK), BLOCK), :]
    units_ref[...] = dot_nt(left, right).astype(units_ref.dtype)
    wanted = row * OWN_COLS + lax.broadcasted_iota(jnp.int32, (OWN_COLS, PANEL_COLS), 0)
    column = lax.broadcasted_iota(jnp.int32, (OWN_COLS, PANEL_COLS), 1)
    pick = jnp.where(wanted == column, 1.0, 0.0).astype(jnp.bfloat16)
    rows = panel_ref[pl.ds(pl.multiple_of(unit * BLOCK, BLOCK), BLOCK), :]
    columns_ref[...] = dot_nt(pick, rows).astype(columns_ref.dtype)


def partial_gram(panel):
    return pl.pallas_call(
        gram_kernel,
        grid=(UNITS,),
        out_shape=(
            jax.ShapeDtypeStruct((UNITS * HALF, BLOCK), jnp.bfloat16),
            jax.ShapeDtypeStruct((OWN_COLS, M), jnp.bfloat16),
        ),
        in_specs=[pl.BlockSpec((M, PANEL_COLS), lambda u: (0, 0))],
        out_specs=(
            pl.BlockSpec((HALF, BLOCK), lambda u: (u, 0)),
            pl.BlockSpec((OWN_COLS, BLOCK), lambda u: (0, u)),
        ),
        compiler_params=pltpu.CompilerParams(vmem_limit_bytes=32 * 2**20),
        name="partial_gram",
    )(panel)


def times_gram(gram_ref, value_ref, write):
    for j in range(BLOCKS):
        total = None
        for d in range(KEPT):
            i = (j - d) % BLOCKS
            term = jnp.dot(
                value_ref[:, i * BLOCK : (i + 1) * BLOCK],
                gram_ref[i * KEPT + d],
                preferred_element_type=jnp.float32,
            )
            total = term if total is None else total + term
        for d in range(1, KEPT):
            i = (j + d) % BLOCKS
            total = total + dot_nt(
                value_ref[:, i * BLOCK : (i + 1) * BLOCK], gram_ref[j * KEPT + d]
            )
        write(j, total)


def newton_schulz_kernel(gram_ref, base_ref, out_ref, value, point, product):
    def square_sum(block):
        rows = jnp.zeros((8, BLOCK), jnp.float32)
        for r in range(0, BLOCK, 64):
            part = gram_ref[block, r : r + 64, :].astype(jnp.float32)
            rows = rows + jnp.sum((part * part).reshape(8, 8, BLOCK), axis=0)
        return rows

    def squares(i, total):
        own = square_sum(i * KEPT)
        others = square_sum(i * KEPT + 1)
        for d in range(2, KEPT):
            others = others + square_sum(i * KEPT + d)
        return total + own + 2.0 * others

    quartic = jnp.sum(lax.fori_loop(0, BLOCKS, squares, jnp.zeros((8, BLOCK), jnp.float32)))
    quartic = jnp.full((1, 1), quartic, jnp.float32)
    scale = 1.0 / jnp.sqrt(jnp.sqrt(quartic) + EPSILON)
    square = scale * scale

    def cut(j):
        return slice(j * BLOCK, (j + 1) * BLOCK)

    def into_product(j, total):
        product[:, cut(j)] = square * total

    def quintic(keep, finish):
        times_gram(gram_ref, value, into_product)
        value[...] = product[...].astype(jnp.bfloat16)
        times_gram(
            gram_ref,
            value,
            lambda j, total: finish(
                j,
                COEF_LINEAR * keep[:, cut(j)]
                + COEF_CUBIC * product[:, cut(j)]
                + COEF_QUINTIC * (square * total),
            ),
        )

    point[...] = base_ref[...].astype(jnp.float32) * scale
    value[...] = point[...].astype(jnp.bfloat16)

    def step(stage, _):
        def finish(j, total):
            point[:, cut(j)] = total

        quintic(point, finish)
        value[...] = point[...].astype(jnp.bfloat16)
        return 0

    step(0, 0)
    first = out_ref
    first[...] = COEF_LINEAR * point[...]

    def gram_of_second(number, _):
        coefficient = jnp.where(number == 0, COEF_CUBIC, COEF_QUINTIC)
        step(0, 0)
        times_gram(gram_ref, value, into_product)
        point[...] = product[...]
        value[...] = point[...].astype(jnp.bfloat16)
        step(0, 0)
        first[...] += coefficient * point[...]
        return 0

    lax.fori_loop(0, 2, gram_of_second, 0)


def newton_schulz(gram, base):
    return pl.pallas_call(
        newton_schulz_kernel,
        out_shape=jax.ShapeDtypeStruct((OWN_COLS, M), jnp.float32),
        in_specs=[pl.BlockSpec(memory_space=pltpu.VMEM)] * 2,
        out_specs=pl.BlockSpec(memory_space=pltpu.VMEM),
        scratch_shapes=[
            pltpu.VMEM((OWN_COLS, M), jnp.bfloat16),
            pltpu.VMEM((OWN_COLS, M), jnp.float32),
            pltpu.VMEM((OWN_COLS, M), jnp.float32),
        ],
        compiler_params=pltpu.CompilerParams(vmem_limit_bytes=48 * 2**20),
        name="newton_schulz",
    )(gram, base)


def per_device(gradient, momentum):
    grad32 = gradient.astype(jnp.float32)
    buffer = MOMENTUM_DECAY * momentum + grad32
    nesterov = grad32 + MOMENTUM_DECAY * buffer
    base = nesterov.astype(jnp.bfloat16)
    panel = lax.all_gather(base, "row", axis=0, tiled=True)
    units, columns = partial_gram(panel)
    shares = lax.psum_scatter(
        units, "col", scatter_dimension=0, axis_index_groups=X_GROUPS, tiled=True
    )
    shares = lax.psum_scatter(
        shares, "col", scatter_dimension=0, axis_index_groups=Z_GROUPS, tiled=True
    )
    gram = lax.all_gather(shares, ("row", "col"), axis=0, tiled=True)
    gram = gram.reshape(BLOCKS * KEPT, BLOCK, BLOCK)
    combined = newton_schulz(gram, columns)
    update = (combined * UPDATE_SCALE).astype(jnp.bfloat16)
    update = update.reshape(OWN_COLS, ROWS, OWN_ROWS).transpose(1, 0, 2)
    update = lax.all_to_all(update, "row", split_axis=0, concat_axis=0)
    update_matrix = update.reshape(PANEL_COLS, OWN_ROWS).T
    return (update_matrix, buffer)


def solution(mesh):
    return jax.shard_map(
        per_device,
        mesh=mesh,
        in_specs=(P("row", "col"), P("row", "col")),
        out_specs=(P("row", "col"), P("row", "col")),
        check_vma=False,
    )
```

time: 848 us -> 344 us (0.41)
  waiting for transfers between devices: 713 us -> 230 us
  Pallas kernels: 0 us -> 81.4 us
  blocking collectives: 79.5 us -> 12.4 us
  matrix products: 28.4 us -> 0 us
    unnamed x10 -> x4, waiting for transfers between devices: 432 us -> 0.07 us
    all_gather x6 -> x2, waiting for transfers between devices: 281 us -> 165 us  [the longest x1 131 us: per_device(): gram = lax.all_gather(shares, ('row', 'col'), axis=0, tiled=True)]
    pallas_call x0 -> x2, Pallas kernels: none -> 81.4 us  [the longest x1 77.3 us: newton_schulz(): pl.pallas_call(newton_schulz_kernel, out_shape=jax.ShapeDtypeStruct((OWN_...]
    psum x1 -> x0, blocking collectives: 79.5 us -> none  [per_device(): quartic = lax.psum(jnp.sum(weights * shares * shares), ('row', 'col'))]
    reduce_scatter x0 -> x2, waiting for transfers between devices: none -> 65 us  [the longest x1 34.7 us: per_device(): lax.psum_scatter(shares, 'col', scatter_dimension=0, axis_index_groups=Z_...]
    dot_general x6 -> x0, matrix products: 28.4 us -> none  [the longest x2 11.2 us: per_device(): second = jnp.dot(gram, product_panel, preferred_element_type=jnp.float32)]
    all_to_all x0 -> x1, blocking collectives: none -> 12.4 us  [per_device(): update = lax.all_to_all(update, 'row', split_axis=0, concat_axis=0)]
  transfers between devices with their start and end apart: 8 -> 4, of which waited for: 8 -> 4; matrix products, arithmetic and copies ran while one was open for 0% -> 0% of each run, Pallas kernels for 0% -> 0%
where the time goes in v1:
time: 344 us
  waiting for transfers between devices  230 us (67%)
  Pallas kernels  81.4 us (24%)
  between operations  13.8 us (4%)
  blocking collectives  12.4 us (4%)
    all_gather x1, waiting for transfers between devices, per_device(): gram = lax.all_gather(shares, ('row', 'col'), axis=0, tiled=True)  131 us
    pallas_call x1, Pallas kernels, newton_schulz(): pl.pallas_call(newton_schulz_kernel, out_shape=jax.ShapeDtypeStruct((OWN_...  77.3 us
    reduce_scatter x1, waiting for transfers between devices, per_device(): lax.psum_scatter(shares, 'col', scatter_dimension=0, axis_index_groups=Z_...  34.7 us
    all_gather x1, waiting for transfers between devices, per_device(): panel = lax.all_gather(base, 'row', axis=0, tiled=True)  34 us
    reduce_scatter x1, waiting for transfers between devices, per_device(): lax.psum_scatter(units, 'col', scatter_dimension=0, axis_index_groups=X_G...  30.3 us
    all_to_all x1, blocking collectives, per_device(): update = lax.all_to_all(update, 'row', split_axis=0, concat_axis=0)  12.4 us
  transfers between devices with their start and end apart: 4, of which 4 were waited for; matrix products, arithmetic and copies ran while one was open for 0% of the time, Pallas kernels for 0%

profile of v1, /device:TPU:1, one launch (start us, length us, event | category | flops | bytes accessed | tf_op | source)
XLA Modules:
  0.0 343.5 jit_solution(8952977083421952389)
XLA Ops:
  7.2 0.0 all-gather.3.cloned.1.call-start
  7.2 2.3 fusion
  9.5 0.0 all-gather.3.cloned.1.call-update
  9.5 0.0 reduce-scatter.3.cloned.1.call-start
  9.6 34.0 %all-gather.3.cloned.1.call-done.panel_ref = bf16[3584,384]{1,0:T(8,128)(2,1)} async-done(((bf16[448,384]{1,0:T(8,128)(2,1)}), bf16[3584,384]{1,0:T(8,128)(2,1)}) %all-gather.3.cloned.1.call-update) | async-done | bytes 2752528 | tf_op jit(solution)/shard_map/all_gather | solution.py:187
  43.6 0.0 copy-start
  43.6 1.8 copy-done
  45.4 4.2 %partial_gram.1 = (bf16[1792,512]{1,0:T(8,128)(2,1)}, bf16[48,3584]{1,0:T(8,128)(2,1)S(1)}) custom-call(bf16[3584,384]{1,0:T(8,128)(2,1)S(1)} %copy-done), custom_call_target="tpu_custom_call" | custom-call | tf_op jit(solution)/shard_map/partial_gram/pallas_call | solution.py:62
  49.6 0.0 reduce-scatter.3.cloned.1.call-update
  49.6 0.0 reduce-scatter.5.cloned.1.call-start
  49.6 30.3 %reduce-scatter.3.cloned.1.call-done = bf16[448,512]{1,0:T(8,128)(2,1)} async-done(((bf16[1792,512]{1,0:T(8,128)(2,1)}), bf16[448,512]{1,0:T(8,128)(2,1)}) %reduce-scatter.3.cloned.1.call-update) | async-done | bytes 458768 | tf_op jit(solution)/shard_map/reduce_scatter | solution.py:189
  80.0 0.0 reduce-scatter.5.cloned.1.call-update
  80.0 0.0 all-gather.5.cloned.1.call-start
  80.0 34.7 %reduce-scatter.5.cloned.1.call-done = bf16[56,512]{1,0:T(8,128)(2,1)} async-done(((bf16[448,512]{1,0:T(8,128)(2,1)}), bf16[56,512]{1,0:T(8,128)(2,1)}) %reduce-scatter.5.cloned.1.call-update) | async-done | bytes 57360 | tf_op jit(solution)/shard_map/reduce_scatter | solution.py:192
  114.7 0.0 all-gather.5.cloned.1.call-update
  114.7 130.9 %all-gather.5.cloned.1.call-done = bf16[14336,512]{1,0:T(8,128)(2,1)} async-done(((bf16[56,512]{1,0:T(8,128)(2,1)}), bf16[14336,512]{1,0:T(8,128)(2,1)}) %all-gather.5.cloned.1.call-update) | async-done | bytes 14680080 | tf_op jit(solution)/shard_map/all_gather | solution.py:195
  245.7 77.3 %newton_schulz.1 = f32[48,3584]{1,0:T(8,128)S(1)} custom-call(bf16[28,512,512]{2,1,0:T(8,128)(2,1)} %bitcast.7, bf16[48,3584]{1,0:T(8,128)(2,1)S(1)} %get-tuple-element.5.base_ref), custom_call_target="tpu_custom_call" | custom-call | tf_op jit(solution)/shard_map/newton_schulz/pallas_call | solution.py:167
  323.0 0.1 multiply_convert_fusion
  323.0 0.5 reshape.14
  323.5 0.1 copy.8
  323.6 12.4 %all_to_all.5 = bf16[8,48,448]{2,1,0:T(8,128)(2,1)S(1)} all-to-all(bf16[8,48,448]{2,1,0:T(8,128)(2,1)S(1)} %bitcast.8), channel_id=1, replica_groups=mesh['row'=8,'col'=32] {'row'}, dimensions={0} | all-to-all | bytes 688128 | tf_op jit(solution)/shard_map/all_to_all | solution.py:200
  336.1 0.9 copy.6
Async XLA Ops:
  7.2 36.5 %all-gather.3.cloned.1.call-start = ((), (), s32[]{:S(2)}) async-start(), calls=%async_computation.3 | async-start | bytes 3096576 | tf_op jit(solution)/shard_map/all_gather | solution.py:187
  9.5 70.4 %reduce-scatter.3.cloned.1.call-start = ((), (), s32[]{:S(2)}) async-start(), calls=%async_computation.4 | async-start | bytes 2293760 | tf_op jit(solution)/shard_map/reduce_scatter | solution.py:189
  43.6 1.8 copy-start
  49.6 65.1 %reduce-scatter.5.cloned.1.call-start = ((), (), s32[]{:S(2)}) async-start(), calls=%async_computation.5 | async-start | bytes 516096 | tf_op jit(solution)/shard_map/reduce_scatter | solution.py:192
  80.0 165.7 %all-gather.5.cloned.1.call-start = ((), (), s32[]{:S(2)}) async-start(), calls=%async_computation.6 | async-start | bytes 14737408 | tf_op jit(solution)/shard_map/all_gather | solution.py:195
Sparse Core Ops, SparseCore 0:
  10.4 33.1 all-gather.2
  49.7 30.2 reduce-scatter.2
  82.5 32.1 reduce-scatter.4
  118.7 126.8 all-gather.4

commit v2 on v0

v2 whole, which is shorter than its diff:
```python
import math

import jax
import jax.numpy as jnp
from jax import lax
from jax.experimental import pallas as pl
from jax.experimental.pallas import tpu as pltpu
from jax.sharding import PartitionSpec as P

M = 3584
N = 12288
ROWS = 8
COLS = 32
X_CHIPS = 4
Y_CHIPS = 4
Z_CHIPS = 8
CORES = 2

MOMENTUM_DECAY = 0.95
EPSILON = 1e-07
COEF_LINEAR = 3.4445
COEF_CUBIC = -4.775
COEF_QUINTIC = 2.0315
UPDATE_SCALE = 0.2 * math.sqrt(max(M, N))

BLOCK = 512
BLOCKS = M // BLOCK
KEPT = (BLOCKS + 1) // 2
TILE = 256
TILES = BLOCKS * KEPT * 4
GRAM_ROWS = TILES * TILE
ROW_TILES = TILES // ROWS
PANEL_COLS = N // COLS
OWN_COLS = PANEL_COLS // ROWS
OWN_ROWS = M // ROWS
CHUNK = GRAM_ROWS // (ROWS * X_CHIPS)
SHARE = CHUNK // Z_CHIPS
HALF_CHUNK = CHUNK // 2
PIECE = TILE // 2
CHUNK_PIECES = CHUNK // PIECE
STEPS = 12

LINES = ((0, (0, 1, 2, 3)), (1, (0, 1, 2, 3)), (3, (0, 1, 2, 3)), (2, (0, 1)), (2, (2, 3)))
PARTS = [
    (half, [(last, k) if half == 0 else (k, last) for k in shifts], other_core)
    for other_core in (False, True)
    for half in (0, 1)
    for last, shifts in LINES
]

Z_GROUPS = [[x * Z_CHIPS + z for z in range(Z_CHIPS)] for x in range(X_CHIPS)]


def dot_nt(left, right):
    return lax.dot_general(
        left, right, (((1,), (1,)), ((), ())), preferred_element_type=jnp.float32
    )


def over_x(value, shift):
    pairs = [
        (x * Z_CHIPS + z, (x + shift) % X_CHIPS * Z_CHIPS + z)
        for x in range(X_CHIPS)
        for z in range(Z_CHIPS)
    ]
    return lax.ppermute(value, "col", pairs)


def over_y(value, shift):
    pairs = [
        (y * CORES + c, (y + shift) % Y_CHIPS * CORES + c)
        for y in range(Y_CHIPS)
        for c in range(CORES)
    ]
    return lax.ppermute(value, "row", pairs)


def over_cores(value):
    pairs = [
        (y * CORES + c, y * CORES + 1 - c) for y in range(Y_CHIPS) for c in range(CORES)
    ]
    return lax.ppermute(value, "row", pairs)


def over_z(value):
    return lax.all_to_all(
        value, "col", split_axis=0, concat_axis=0, axis_index_groups=Z_GROUPS
    )


def gram_kernel(panel_ref, *refs):
    chunk_refs, columns_ref = refs[:X_CHIPS], refs[X_CHIPS]
    row = lax.axis_index("row")
    x = lax.axis_index("col") // Z_CHIPS
    wanted = row * OWN_COLS + lax.broadcasted_iota(jnp.int32, (OWN_COLS, PANEL_COLS), 0)
    column = lax.broadcasted_iota(jnp.int32, (OWN_COLS, PANEL_COLS), 1)
    pick = jnp.where(wanted == column, 1.0, 0.0).astype(jnp.bfloat16)
    for shift in range(X_CHIPS):
        owner = lax.rem(x + shift, X_CHIPS)
        for k in range(CHUNK_PIECES):
            piece = owner * CHUNK_PIECES + k
            tile = row * ROW_TILES + piece // 2
            block = tile // 4
            i, d = block // KEPT, block % KEPT
            j = lax.rem(i + d, BLOCKS)
            top = i * BLOCK + tile % 4 // 2 * TILE + piece % 2 * PIECE
            across = j * BLOCK + tile % 2 * TILE
            left = panel_ref[pl.ds(pl.multiple_of(top, PIECE), PIECE), :]
            right = panel_ref[pl.ds(pl.multiple_of(across, TILE), TILE), :]
            chunk_refs[shift][k * PIECE : (k + 1) * PIECE, :] = dot_nt(left, right).astype(
                jnp.bfloat16
            )
    for b in range(BLOCKS):
        rows = panel_ref[b * BLOCK : (b + 1) * BLOCK, :]
        columns_ref[:, b * BLOCK : (b + 1) * BLOCK] = dot_nt(pick, rows).astype(jnp.bfloat16)


def partial_gram(panel):
    vmem = pl.BlockSpec(memory_space=pltpu.VMEM)
    outs = pl.pallas_call(
        gram_kernel,
        out_shape=[jax.ShapeDtypeStruct((CHUNK, TILE), jnp.bfloat16)] * X_CHIPS
        + [jax.ShapeDtypeStruct((OWN_COLS, M), jnp.bfloat16)],
        in_specs=[vmem],
        out_specs=[vmem] * (X_CHIPS + 1),
        compiler_params=pltpu.CompilerParams(vmem_limit_bytes=32 * 2**20),
        name="partial_gram",
    )(panel)
    return outs[:X_CHIPS], outs[X_CHIPS]


def tile_rows(i, d, half, column_half):
    start = (((i * KEPT + d) * 2 + half) * 2 + column_half) * TILE
    return pl.ds(start, TILE)


def mirror_rows(j, d, half, column_half):
    start = (((j * (KEPT - 1) + d - 1) * 2 + half) * 2 + column_half) * TILE
    return pl.ds(start, TILE)


def newton_schulz_kernel(base_ref, *refs):
    parts = refs[: len(PARTS)]
    out_ref, gram, mirror, value, state, total, sems = refs[len(PARTS) :]
    row = lax.axis_index("row")
    y, core = row // CORES, row % CORES
    x = lax.axis_index("col") // Z_CHIPS
    copies = []
    for part, (half, shifts, other_core) in zip(parts, PARTS):
        for k, (y_shift, x_shift) in enumerate(shifts):
            from_row = lax.rem(y + Y_CHIPS - y_shift, Y_CHIPS) * CORES
            from_row = from_row + (1 - core if other_core else core)
            from_x = lax.rem(x + X_CHIPS - x_shift, X_CHIPS)
            start = (from_row * X_CHIPS + from_x) * CHUNK + half * HALF_CHUNK
            copies.append(
                pltpu.make_async_copy(
                    part.at[k],
                    gram.at[pl.ds(pl.multiple_of(start, HALF_CHUNK), HALF_CHUNK), :],
                    sems.at[len(copies)],
                )
            )
    for copy in copies:
        copy.start()
    for copy in copies:
        copy.wait()

    one = lax.broadcasted_iota(jnp.int32, (TILE, TILE), 0)
    other = lax.broadcasted_iota(jnp.int32, (TILE, TILE), 1)
    identity = jnp.where(one == other, 1.0, 0.0).astype(jnp.bfloat16)

    def square_sum(tile):
        part = tile.astype(jnp.float32)
        return jnp.sum((part * part).reshape(TILE // 8, 8, TILE), axis=0)

    def prepare(i, sums):
        own, others = sums
        for half in range(2):
            for column_half in range(2):
                own = own + square_sum(gram[tile_rows(i, 0, half, column_half), :])
                for d in range(1, KEPT):
                    tile = gram[tile_rows(i, d, half, column_half), :]
                    others = others + square_sum(tile)
                    mirror[mirror_rows(i, d, half, column_half), :] = dot_nt(
                        identity, tile
                    ).astype(jnp.bfloat16)
        return own, others

    zeros = jnp.zeros((8, TILE), jnp.float32)
    own, others = lax.fori_loop(0, BLOCKS, prepare, (zeros, zeros))
    quartic = jnp.full((1, 1), jnp.sum(own + 2.0 * others), jnp.float32)
    scale = 1.0 / jnp.sqrt(jnp.sqrt(quartic) + EPSILON)
    square = scale * scale

    state[...] = base_ref[...].astype(jnp.float32) * scale
    value[0] = state[...].astype(jnp.bfloat16)

    def step(number, _):
        now = lax.rem(number, 2)
        place = jnp.where(number < 2, number, lax.rem(number + 3, 5))
        cubic = (place == 0) | (place == 3)
        quintic = (place == 1) | (place == 4)
        keep = jnp.where(cubic, COEF_LINEAR, jnp.where(quintic, 1.0, 0.0))
        add = jnp.where(cubic, COEF_CUBIC, jnp.where(quintic, COEF_QUINTIC, 1.0))
        from_product = jnp.where(cubic, 1.0, 0.0)
        from_state = jnp.where(cubic, 0.0, 1.0)
        for j in range(BLOCKS):
            for column_half in range(2):
                product = None
                for d in range(KEPT):
                    i = (j - d) % BLOCKS
                    for half in range(2):
                        term = jnp.dot(
                            value[now, :, pl.ds(i * BLOCK + half * TILE, TILE)],
                            gram[tile_rows(i, d, half, column_half), :],
                            preferred_element_type=jnp.float32,
                        )
                        product = term if product is None else product + term
                for d in range(1, KEPT):
                    i = (j + d) % BLOCKS
                    for half in range(2):
                        product = product + jnp.dot(
                            value[now, :, pl.ds(i * BLOCK + half * TILE, TILE)],
                            mirror[mirror_rows(j, d, column_half, half), :],
                            preferred_element_type=jnp.float32,
                        )
                cut = pl.ds(j * BLOCK + column_half * TILE, TILE)
                product = square * product
                result = keep * state[:, cut] + add * product
                state[:, cut] = result
                value[1 - now, :, cut] = (from_product * product + from_state * result).astype(
                    jnp.bfloat16
                )

        @pl.when(number == 1)
        def _():
            total[...] = COEF_LINEAR * state[...]

        @pl.when(number == 6)
        def _():
            total[...] += COEF_CUBIC * state[...]

        return 0

    lax.fori_loop(0, STEPS, step, 0)
    out_ref[...] = (UPDATE_SCALE * (total[...] + COEF_QUINTIC * state[...])).astype(jnp.bfloat16)


def newton_schulz(base, parts):
    mirror_tiles = BLOCKS * (KEPT - 1) * 4
    return pl.pallas_call(
        newton_schulz_kernel,
        out_shape=jax.ShapeDtypeStruct((OWN_COLS, M), jnp.bfloat16),
        in_specs=[pl.BlockSpec(memory_space=pltpu.VMEM)]
        + [pl.BlockSpec(memory_space=pl.ANY)] * len(parts),
        out_specs=pl.BlockSpec(memory_space=pltpu.VMEM),
        scratch_shapes=[
            pltpu.VMEM((GRAM_ROWS, TILE), jnp.bfloat16),
            pltpu.VMEM((mirror_tiles * TILE, TILE), jnp.bfloat16),
            pltpu.VMEM((2, OWN_COLS, M), jnp.bfloat16),
            pltpu.VMEM((OWN_COLS, M), jnp.float32),
            pltpu.VMEM((OWN_COLS, M), jnp.float32),
            pltpu.SemaphoreType.DMA((sum(len(shifts) for _, shifts, _ in PARTS),)),
        ],
        compiler_params=pltpu.CompilerParams(vmem_limit_bytes=48 * 2**20),
        name="newton_schulz",
    )(base, *parts)


def add_up(parts):
    total = parts[0].astype(jnp.float32)
    for part in parts[1:]:
        total = total + part.astype(jnp.float32)
    return total.astype(jnp.bfloat16)


def scattered_sum(chunks):
    received = [chunks[0]] + [over_x(chunks[k], k) for k in (2, 1, 3)]
    shares = over_z(add_up(received).reshape(Z_CHIPS, SHARE, TILE))
    return add_up([shares[z] for z in range(Z_CHIPS)])


def gathered(share):
    chunk = over_z(jnp.broadcast_to(share[None], (Z_CHIPS, SHARE, TILE))).reshape(CHUNK, TILE)
    first, second = chunk[:HALF_CHUNK], chunk[HALF_CHUNK:]
    from_x = {k: over_x(first, k) for k in (1, 3, 2)}
    from_y = {k: over_y(second, k) for k in (1, 3, 2)}
    first = jnp.stack([first] + [from_x[k] for k in (1, 2, 3)])
    second = jnp.stack([second] + [from_y[k] for k in (1, 2, 3)])
    first, second = lax.optimization_barrier((first, second))
    ups, downs = [over_y(first, 1), over_x(second, 1)], [over_y(first, 3), over_x(second, 3)]
    ups, downs = lax.optimization_barrier((ups, downs))
    parts = []
    for own, over, up, down in zip((first, second), (over_y, over_x), ups, downs):
        parts += [own, up, down, over(up[:2], 1), over(down[2:], 3)]
    return parts + [over_cores(part) for part in parts]


def per_device(gradient, momentum):
    grad32 = gradient.astype(jnp.float32)
    buffer = MOMENTUM_DECAY * momentum + grad32
    nesterov = grad32 + MOMENTUM_DECAY * buffer
    base = nesterov.astype(jnp.bfloat16)
    panel = lax.all_gather(base, "row", axis=0, tiled=True)
    chunks, columns = partial_gram(panel)
    parts = gathered(scattered_sum(chunks))
    update = newton_schulz(columns, parts)
    update = update.reshape(OWN_COLS, ROWS, OWN_ROWS).transpose(1, 0, 2)
    update = lax.all_to_all(update, "row", split_axis=0, concat_axis=0)
    update_matrix = update.reshape(PANEL_COLS, OWN_ROWS).T
    return (update_matrix, buffer)


def solution(mesh):
    return jax.shard_map(
        per_device,
        mesh=mesh,
        in_specs=(P("row", "col"), P("row", "col")),
        out_specs=(P("row", "col"), P("row", "col")),
        check_vma=False,
    )
```

time: 848 us -> 298 us (0.35)
  waiting for transfers between devices: 713 us -> 78.9 us
  Pallas kernels: 0 us -> 104 us
  starting transfers between devices: 0.33 us -> 43.9 us
  blocking collectives: 79.5 us -> 48.4 us
  matrix products: 28.4 us -> 0 us
    unnamed x10 -> x1, waiting for transfers between devices: 432 us -> 0.02 us
    all_gather x6 -> x1, waiting for transfers between devices: 281 us -> 34.1 us  [per_device(): panel = lax.all_gather(base, 'row', axis=0, tiled=True)]
    pallas_call x0 -> x2, Pallas kernels: none -> 104 us  [the longest x1 101 us: newton_schulz(): pl.pallas_call(newton_schulz_kernel, out_shape=jax.ShapeDtypeStruct((OWN_...]
    psum x1 -> x0, blocking collectives: 79.5 us -> none  [per_device(): quartic = lax.psum(jnp.sum(weights * shares * shares), ('row', 'col'))]
    all_to_all x0 -> x3, blocking collectives: none -> 48.4 us  [the longest x2 37 us: over_z(): lax.all_to_all(value, 'col', split_axis=0, concat_axis=0, axis_index_grou...]
    ppermute x0 -> x27, waiting for transfers between devices: none -> 44.8 us  [the longest x10 31.1 us: over_x(): return lax.ppermute(value, 'col', pairs)]
    ppermute x0 -> x27, starting transfers between devices: none -> 43.8 us  [the longest x10 21.5 us: over_cores(): return lax.ppermute(value, 'row', pairs)]
    dot_general x6 -> x0, matrix products: 28.4 us -> none  [the longest x2 11.2 us: per_device(): second = jnp.dot(gram, product_panel, preferred_element_type=jnp.float32)]
  transfers between devices with their start and end apart: 8 -> 28, of which waited for: 8 -> 12; matrix products, arithmetic and copies ran while one was open for 0% -> 0% of each run, Pallas kernels for 0% -> 0%
where the time goes in v2:
time: 298 us; the launch traced here: 297 us
  Pallas kernels  104 us (35%)
  waiting for transfers between devices  78.9 us (26%)
  blocking collectives  48.4 us (16%)
  starting transfers between devices  43.9 us (15%)
  between operations  14.2 us (5%)
  local copies, waits for them, and re-layouts  5.34 us (2%)
    pallas_call x1, Pallas kernels, newton_schulz(): pl.pallas_call(newton_schulz_kernel, out_shape=jax.ShapeDtypeStruct((OWN_...  101 us
    all_to_all x2, blocking collectives, over_z(): lax.all_to_all(value, 'col', split_axis=0, concat_axis=0, axis_index_grou...  37 us
    all_gather x1, waiting for transfers between devices, per_device(): panel = lax.all_gather(base, 'row', axis=0, tiled=True)  34.1 us
    ppermute x10, waiting for transfers between devices, over_x(): return lax.ppermute(value, 'col', pairs)  31.1 us
    ppermute x10, starting transfers between devices, over_cores(): return lax.ppermute(value, 'row', pairs)  21.5 us
    ppermute x10, starting transfers between devices, over_x(): return lax.ppermute(value, 'col', pairs)  16.6 us
    all_to_all x1, blocking collectives, per_device(): update = lax.all_to_all(update, 'row', split_axis=0, concat_axis=0)  11.4 us
    ppermute x7, waiting for transfers between devices, over_y(): return lax.ppermute(value, 'row', pairs)  8.79 us
  transfers between devices with their start and end apart: 28, of which 12 were waited for; matrix products, arithmetic and copies ran while one was open for 0% of the time, Pallas kernels for 0%

profile of v2, /device:TPU:1, one launch (start us, length us, event | category | flops | bytes accessed | tf_op | source)
XLA Modules:
  0.0 297.3 jit_solution(10783681653524360056)
XLA Ops:
  7.2 2.3 fusion
  9.5 34.1 %all-gather.2.cloned.1.call-done.panel_ref = bf16[3584,384]{1,0:T(8,128)(2,1)} async-done(((bf16[448,384]{1,0:T(8,128)(2,1)}), bf16[3584,384]{1,0:T(8,128)(2,1)}) %all-gather.2.cloned.1.call-update) | async-done | bytes 2752528 | tf_op jit(solution)/shard_map/all_gather | solution.py:303
  43.6 1.8 copy-done
  45.4 2.4 partial_gram.1
  47.8 2.8 collective-permute-start
  50.9 2.4 collective-permute-start.2
  53.2 8.0 %collective-permute-done = bf16[896,256]{1,0:T(8,128)(2,1)S(1)} collective-permute-done((bf16[896,256]{1,0:T(8,128)(2,1)S(1)}, bf16[896,256]{1,0:T(8,128)(2,1)S(1)}, u32[]{:S(2)}, u32[]{:S(2)}) %collective-permute-start) | collective-permute-done | bytes 458784 | tf_op jit(solution)/shard_map/ppermute | solution.py:66
  61.2 10.4 %collective-permute-done.1 = bf16[896,256]{1,0:T(8,128)(2,1)S(1)} collective-permute-done((bf16[896,256]{1,0:T(8,128)(2,1)S(1)}, bf16[896,256]{1,0:T(8,128)(2,1)S(1)}, u32[]{:S(2)}, u32[]{:S(2)}) %collective-permute-start.1) | collective-permute-done | bytes 458784 | tf_op jit(solution)/shard_map/ppermute | solution.py:66
  71.9 21.5 %all_to_all.15 = bf16[8,112,256]{2,1,0:T(8,128)(2,1)S(1)} all-to-all(bf16[8,112,256]{2,1,0:T(8,128)(2,1)S(1)} %bitcast.19), channel_id=1, replica_groups={{0,1,2,3,4,5,6,7},{8,9,10,11,12,13,14,15},{16,17,18,19,20,21,22,23},{24..., dimensions={0} | all-to-all | bytes 917504 | tf_op jit(solution)/shard_map/all_to_all | solution.py:86
  93.5 15.5 %all_to_all.16 = bf16[8,112,256]{2,1,0:T(8,128)(2,1)S(1)} all-to-all(bf16[8,112,256]{2,1,0:T(8,128)(2,1)S(1)} %broadcast_in_dim.9), channel_id=1, replica_groups={{0,1,2,3,4,5,6,7},{8,9,10,11,12,13,14,15},{16,17,18,19,20,21,22,23},{24..., dimensions={0} | all-to-all | bytes 917504 | tf_op jit(solution)/shard_map/all_to_all | solution.py:86
  109.0 2.6 collective-permute-start.5
  112.3 1.5 collective-permute-start.8
  114.5 3.0 %collective-permute-done.5 = bf16[448,256]{1,0:T(8,128)(2,1)S(1)} collective-permute-done((bf16[448,256]{1,0:T(8,128)(2,1)S(1)}, bf16[448,256]{1,0:T(8,128)(2,1)S(1)}, u32[]{:S(2)}, u32[]{:S(2)}) %collective-permute-start.5) | collective-permute-done | bytes 229408 | tf_op jit(solution)/shard_map/ppermute | solution.py:66
  118.1 2.9 collective-permute-done.3
  121.2 3.3 %collective-permute-done.6 = bf16[448,256]{1,0:T(8,128)(2,1)S(1)} collective-permute-done((bf16[448,256]{1,0:T(8,128)(2,1)S(1)}, bf16[448,256]{1,0:T(8,128)(2,1)S(1)}, u32[]{:S(2)}, u32[]{:S(2)}) %collective-permute-start.6) | collective-permute-done | bytes 229408 | tf_op jit(solution)/shard_map/ppermute | solution.py:75
  125.0 1.2 collective-permute-start.9
  126.1 4.4 %collective-permute-start.12 = (bf16[4,448,256]{2,1,0:T(8,128)(2,1)S(1)}, bf16[4,448,256]{2,1,0:T(8,128)(2,1)S(1)}, u32[]{:S(2)}, u32[]{:S(2)}) collective-permute-start(bf16[4,448,256]{2,1,0:T(8,128)(2,1)S(1)} %pad_maximum_fusion.1.refs_5_), channel_id=1, source_target_pairs={{0,24},{1,25},{2,26},{3,27},{4,28},{5,29},{6,30},{7,31},{8,0},{9,1... | collective-permute-start | bytes 2752520 | tf_op jit(solution)/shard_map/ppermute | solution.py:66
  130.6 5.0 %collective-permute-start.17 = (bf16[4,448,256]{2,1,0:T(8,128)(2,1)S(1)}, bf16[4,448,256]{2,1,0:T(8,128)(2,1)S(1)}, u32[]{:S(2)}, u32[]{:S(2)}) collective-permute-start(bf16[4,448,256]{2,1,0:T(8,128)(2,1)S(1)} %pad_maximum_fusion.refs_0_), channel_id=1, source_target_pairs={{0,32},{32,0},{64,96},{96,64},{128,160},{160,128},{192,224},{224,1... | collective-permute-start | bytes 2752520 | tf_op jit(solution)/shard_map/ppermute | solution.py:82
  135.6 5.5 %collective-permute-done.11.refs_2_ = bf16[4,448,256]{2,1,0:T(8,128)(2,1)S(1)} collective-permute-done((bf16[4,448,256]{2,1,0:T(8,128)(2,1)S(1)}, bf16[4,448,256]{2,1,0:T(8,128)(2,1)S(1)}, u32[]{:S(2)}, u32[]{:S(2)}) %collective-permute-start.11) | collective-permute-done | bytes 917536 | tf_op jit(solution)/shard_map/ppermute | solution.py:75
  141.1 6.4 %collective-permute-start.22 = (bf16[4,448,256]{2,1,0:T(8,128)(2,1)S(1)}, bf16[4,448,256]{2,1,0:T(8,128)(2,1)S(1)}, u32[]{:S(2)}, u32[]{:S(2)}) collective-permute-start(bf16[4,448,256]{2,1,0:T(8,128)(2,1)S(1)} %pad_maximum_fusion.1.refs_5_), channel_id=1, source_target_pairs={{0,32},{32,0},{64,96},{96,64},{128,160},{160,128},{192,224},{224,1... | collective-permute-start | bytes 2752520 | tf_op jit(solution)/shard_map/ppermute | solution.py:82
  147.4 1.2 collective-permute-done.10.refs_6_
  148.7 3.3 %collective-permute-start.16 = (bf16[2,448,256]{2,1,0:T(8,128)(2,1)S(1)}, bf16[2,448,256]{2,1,0:T(8,128)(2,1)S(1)}, u32[]{:S(2)}, u32[]{:S(2)}) collective-permute-start(bf16[2,448,256]{2,1,0:T(8,128)(2,1)S(1)} %slice.63), channel_id=1, source_target_pairs={{0,24},{1,25},{2,26},{3,27},{4,28},{5,29},{6,30},{7,31},{8,0},{9,1... | collective-permute-start | bytes 1376264 | tf_op jit(solution)/shard_map/ppermute | solution.py:66
  152.2 1.6 collective-permute-start.14
  153.8 5.4 %collective-permute-done.16.refs_9_ = bf16[2,448,256]{2,1,0:T(8,128)(2,1)S(1)} collective-permute-done((bf16[2,448,256]{2,1,0:T(8,128)(2,1)S(1)}, bf16[2,448,256]{2,1,0:T(8,128)(2,1)S(1)}, u32[]{:S(2)}, u32[]{:S(2)}) %collective-permute-start.16) | collective-permute-done | bytes 458784 | tf_op jit(solution)/shard_map/ppermute | solution.py:66
  159.2 4.0 %collective-permute-start.26 = (bf16[2,448,256]{2,1,0:T(8,128)(2,1)S(1)}, bf16[2,448,256]{2,1,0:T(8,128)(2,1)S(1)}, u32[]{:S(2)}, u32[]{:S(2)}) collective-permute-start(bf16[2,448,256]{2,1,0:T(8,128)(2,1)S(1)} %collective-permute-done.16.refs_9_), channel_id=1, source_target_pairs={{0,32},{32,0},{64,96},{96,64},{128,160},{160,128},{192,224},{224,1... | collective-permute-start | bytes 1376264 | tf_op jit(solution)/shard_map/ppermute | solution.py:82
  163.1 3.1 %collective-permute-start.25 = (bf16[2,448,256]{2,1,0:T(8,128)(2,1)S(1)}, bf16[2,448,256]{2,1,0:T(8,128)(2,1)S(1)}, u32[]{:S(2)}, u32[]{:S(2)}) collective-permute-start(bf16[2,448,256]{2,1,0:T(8,128)(2,1)S(1)} %collective-permute-done.15.refs_8_), channel_id=1, source_target_pairs={{0,32},{32,0},{64,96},{96,64},{128,160},{160,128},{192,224},{224,1... | collective-permute-start | bytes 1376264 | tf_op jit(solution)/shard_map/ppermute | solution.py:82
  166.8 1.6 collective-permute-start.19
  170.1 4.2 %collective-permute-done.20.refs_13_ = bf16[2,448,256]{2,1,0:T(8,128)(2,1)S(1)} collective-permute-done((bf16[2,448,256]{2,1,0:T(8,128)(2,1)S(1)}, bf16[2,448,256]{2,1,0:T(8,128)(2,1)S(1)}, u32[]{:S(2)}, u32[]{:S(2)}) %collective-permute-start.20) | collective-permute-done | bytes 458784 | tf_op jit(solution)/shard_map/ppermute | solution.py:82
  174.3 1.0 copy-done.10
  176.2 101.3 %newton_schulz.1 = bf16[48,3584]{1,0:T(8,128)(2,1)S(1)} custom-call(bf16[48,3584]{1,0:T(8,128)(2,1)S(1)} %get-tuple-element.13.base_ref, bf16[4,448,256]{2,1,0:T(8,128)(2,1)S(1)} %pad_maximum_fusion.refs_0_, bf16[4,448,256]{2,1,0:T(8,128)(2,1)S(1)} %collective-permute-done.9.refs_1_, bf16[4,448,256]{2,1,0:T(8,128)(2,1)} %copy-done.2, ...), custom_call_target="tpu_custom_call" | custom-call | tf_op jit(solution)/shard_map/newton_schulz/pallas_call | solution.py:250
  278.1 11.4 %all_to_all.17 = bf16[8,48,448]{2,1,0:T(8,128)(2,1)S(1)} all-to-all(bf16[8,48,448]{2,1,0:T(8,128)(2,1)S(1)} %bitcast.20), channel_id=1, replica_groups=mesh['row'=8,'col'=32] {'row'}, dimensions={0} | all-to-all | bytes 688128 | tf_op jit(solution)/shard_map/all_to_all | solution.py:308
  289.5 0.9 copy.6
  (66 shorter events, 7.1 us)
Async XLA Ops:
  7.2 36.5 %all-gather.2.cloned.1.call-start = ((), (), s32[]{:S(2)}) async-start(), calls=%async_computation.3 | async-start | bytes 3096576 | tf_op jit(solution)/shard_map/all_gather | solution.py:303
  47.8 13.5 %collective-permute-start = (bf16[896,256]{1,0:T(8,128)(2,1)S(1)}, bf16[896,256]{1,0:T(8,128)(2,1)S(1)}, u32[]{:S(2)}, u32[]{:S(2)}) collective-permute-start(bf16[896,256]{1,0:T(8,128)(2,1)S(1)} %get-tuple-element.15), channel_id=1, source_target_pairs={{0,16},{1,17},{2,18},{3,19},{4,20},{5,21},{6,22},{7,23},{8,24},{9,... | collective-permute-start | bytes 1376264 | tf_op jit(solution)/shard_map/ppermute | solution.py:66
  50.6 21.1 %collective-permute-start.1 = (bf16[896,256]{1,0:T(8,128)(2,1)S(1)}, bf16[896,256]{1,0:T(8,128)(2,1)S(1)}, u32[]{:S(2)}, u32[]{:S(2)}) collective-permute-start(bf16[896,256]{1,0:T(8,128)(2,1)S(1)} %get-tuple-element.16), channel_id=1, source_target_pairs={{0,8},{1,9},{2,10},{3,11},{4,12},{5,13},{6,14},{7,15},{8,16},{9,17... | collective-permute-start | bytes 1376264 | tf_op jit(solution)/shard_map/ppermute | solution.py:66
  50.9 20.8 %collective-permute-start.2 = (bf16[896,256]{1,0:T(8,128)(2,1)S(1)}, bf16[896,256]{1,0:T(8,128)(2,1)S(1)}, u32[]{:S(2)}, u32[]{:S(2)}) collective-permute-start(bf16[896,256]{1,0:T(8,128)(2,1)S(1)} %get-tuple-element.17), channel_id=1, source_target_pairs={{0,24},{1,25},{2,26},{3,27},{4,28},{5,29},{6,30},{7,31},{8,0},{9,1... | collective-permute-start | bytes 1376264 | tf_op jit(solution)/shard_map/ppermute | solution.py:66
  109.0 8.4 %collective-permute-start.5 = (bf16[448,256]{1,0:T(8,128)(2,1)S(1)}, bf16[448,256]{1,0:T(8,128)(2,1)S(1)}, u32[]{:S(2)}, u32[]{:S(2)}) collective-permute-start(bf16[448,256]{1,0:T(8,128)(2,1)S(1)} %bitcast.26), channel_id=1, source_target_pairs={{0,24},{1,25},{2,26},{3,27},{4,28},{5,29},{6,30},{7,31},{8,0},{9,1... | collective-permute-start | bytes 688136 | tf_op jit(solution)/shard_map/ppermute | solution.py:66
  111.7 6.5 %collective-permute-start.4 = (bf16[448,256]{1,0:T(8,128)(2,1)S(1)}, bf16[448,256]{1,0:T(8,128)(2,1)S(1)}, u32[]{:S(2)}, u32[]{:S(2)}) collective-permute-start(bf16[448,256]{1,0:T(8,128)(2,1)S(1)} %bitcast.27), channel_id=1, source_target_pairs={{0,16},{1,17},{2,18},{3,19},{4,20},{5,21},{6,22},{7,23},{8,24},{9,... | collective-permute-start | bytes 688136 | tf_op jit(solution)/shard_map/ppermute | solution.py:66
  112.1 9.0 %collective-permute-start.3 = (bf16[448,256]{1,0:T(8,128)(2,1)S(1)}, bf16[448,256]{1,0:T(8,128)(2,1)S(1)}, u32[]{:S(2)}, u32[]{:S(2)}) collective-permute-start(bf16[448,256]{1,0:T(8,128)(2,1)S(1)} %bitcast.28), channel_id=1, source_target_pairs={{0,8},{1,9},{2,10},{3,11},{4,12},{5,13},{6,14},{7,15},{8,16},{9,17... | collective-permute-start | bytes 688136 | tf_op jit(solution)/shard_map/ppermute | solution.py:66
  112.3 8.8 %collective-permute-start.8 = (bf16[448,256]{1,0:T(8,128)(2,1)S(1)}, bf16[448,256]{1,0:T(8,128)(2,1)S(1)}, u32[]{:S(2)}, u32[]{:S(2)}) collective-permute-start(bf16[448,256]{1,0:T(8,128)(2,1)S(1)} %bitcast.22), channel_id=1, source_target_pairs={{0,192},{32,224},{64,0},{96,32},{128,64},{160,96},{192,128},{224,1... | collective-permute-start | bytes 688136 | tf_op jit(solution)/shard_map/ppermute | solution.py:75
  113.8 7.3 %collective-permute-start.7 = (bf16[448,256]{1,0:T(8,128)(2,1)S(1)}, bf16[448,256]{1,0:T(8,128)(2,1)S(1)}, u32[]{:S(2)}, u32[]{:S(2)}) collective-permute-start(bf16[448,256]{1,0:T(8,128)(2,1)S(1)} %bitcast.23), channel_id=1, source_target_pairs={{0,128},{32,160},{64,192},{96,224},{128,0},{160,32},{192,64},{224,... | collective-permute-start | bytes 688136 | tf_op jit(solution)/shard_map/ppermute | solution.py:75
  117.5 7.0 %collective-permute-start.6 = (bf16[448,256]{1,0:T(8,128)(2,1)S(1)}, bf16[448,256]{1,0:T(8,128)(2,1)S(1)}, u32[]{:S(2)}, u32[]{:S(2)}) collective-permute-start(bf16[448,256]{1,0:T(8,128)(2,1)S(1)} %bitcast.24), channel_id=1, source_target_pairs={{0,64},{32,96},{64,128},{96,160},{128,192},{160,224},{192,0},{224,... | collective-permute-start | bytes 688136 | tf_op jit(solution)/shard_map/ppermute | solution.py:75
  124.6 50.8 %copy-start.1 = (bf16[4,448,256]{2,1,0:T(8,128)(2,1)}, bf16[4,448,256]{2,1,0:T(8,128)(2,1)S(1)}, u32[]{:S(2)}) copy-start(bf16[4,448,256]{2,1,0:T(8,128)(2,1)S(1)} %pad_maximum_fusion.1.refs_5_) | copy-start | bytes 2752516
  124.6 16.5 %collective-permute-start.11 = (bf16[4,448,256]{2,1,0:T(8,128)(2,1)S(1)}, bf16[4,448,256]{2,1,0:T(8,128)(2,1)S(1)}, u32[]{:S(2)}, u32[]{:S(2)}) collective-permute-start(bf16[4,448,256]{2,1,0:T(8,128)(2,1)S(1)} %pad_maximum_fusion.refs_0_), channel_id=1, source_target_pairs={{0,192},{32,224},{64,0},{96,32},{128,64},{160,96},{192,128},{224,1... | collective-permute-start | bytes 2752520 | tf_op jit(solution)/shard_map/ppermute | solution.py:75
  125.0 22.5 %collective-permute-start.9 = (bf16[4,448,256]{2,1,0:T(8,128)(2,1)S(1)}, bf16[4,448,256]{2,1,0:T(8,128)(2,1)S(1)}, u32[]{:S(2)}, u32[]{:S(2)}) collective-permute-start(bf16[4,448,256]{2,1,0:T(8,128)(2,1)S(1)} %pad_maximum_fusion.refs_0_), channel_id=1, source_target_pairs={{0,64},{32,96},{64,128},{96,160},{128,192},{160,224},{192,0},{224,... | collective-permute-start | bytes 2752520 | tf_op jit(solution)/shard_map/ppermute | solution.py:75
  126.1 21.3 %collective-permute-start.12 = (bf16[4,448,256]{2,1,0:T(8,128)(2,1)S(1)}, bf16[4,448,256]{2,1,0:T(8,128)(2,1)S(1)}, u32[]{:S(2)}, u32[]{:S(2)}) collective-permute-start(bf16[4,448,256]{2,1,0:T(8,128)(2,1)S(1)} %pad_maximum_fusion.1.refs_5_), channel_id=1, source_target_pairs={{0,24},{1,25},{2,26},{3,27},{4,28},{5,29},{6,30},{7,31},{8,0},{9,1... | collective-permute-start | bytes 2752520 | tf_op jit(solution)/shard_map/ppermute | solution.py:66
  130.6 18.1 %collective-permute-start.10 = (bf16[4,448,256]{2,1,0:T(8,128)(2,1)S(1)}, bf16[4,448,256]{2,1,0:T(8,128)(2,1)S(1)}, u32[]{:S(2)}, u32[]{:S(2)}) collective-permute-start(bf16[4,448,256]{2,1,0:T(8,128)(2,1)S(1)} %pad_maximum_fusion.1.refs_5_), channel_id=1, source_target_pairs={{0,8},{1,9},{2,10},{3,11},{4,12},{5,13},{6,14},{7,15},{8,16},{9,17... | collective-permute-start | bytes 2752520 | tf_op jit(solution)/shard_map/ppermute | solution.py:66
  130.6 23.2 %collective-permute-start.17 = (bf16[4,448,256]{2,1,0:T(8,128)(2,1)S(1)}, bf16[4,448,256]{2,1,0:T(8,128)(2,1)S(1)}, u32[]{:S(2)}, u32[]{:S(2)}) collective-permute-start(bf16[4,448,256]{2,1,0:T(8,128)(2,1)S(1)} %pad_maximum_fusion.refs_0_), channel_id=1, source_target_pairs={{0,32},{32,0},{64,96},{96,64},{128,160},{160,128},{192,224},{224,1... | collective-permute-start | bytes 2752520 | tf_op jit(solution)/shard_map/ppermute | solution.py:82
  141.1 34.3 %copy-start.2 = (bf16[4,448,256]{2,1,0:T(8,128)(2,1)}, bf16[4,448,256]{2,1,0:T(8,128)(2,1)S(1)}, u32[]{:S(2)}) copy-start(bf16[4,448,256]{2,1,0:T(8,128)(2,1)S(1)} %collective-permute-done.11.refs_2_) | copy-start | bytes 2752516
  141.1 25.2 %collective-permute-start.22 = (bf16[4,448,256]{2,1,0:T(8,128)(2,1)S(1)}, bf16[4,448,256]{2,1,0:T(8,128)(2,1)S(1)}, u32[]{:S(2)}, u32[]{:S(2)}) collective-permute-start(bf16[4,448,256]{2,1,0:T(8,128)(2,1)S(1)} %pad_maximum_fusion.1.refs_5_), channel_id=1, source_target_pairs={{0,32},{32,0},{64,96},{96,64},{128,160},{160,128},{192,224},{224,1... | collective-permute-start | bytes 2752520 | tf_op jit(solution)/shard_map/ppermute | solution.py:82
  147.4 27.9 %copy-start.3 = (bf16[4,448,256]{2,1,0:T(8,128)(2,1)}, bf16[4,448,256]{2,1,0:T(8,128)(2,1)S(1)}, u32[]{:S(2)}) copy-start(bf16[4,448,256]{2,1,0:T(8,128)(2,1)S(1)} %collective-permute-done.12.refs_7_) | copy-start | bytes 2752516
  148.6 26.8 %copy-start.4 = (bf16[4,448,256]{2,1,0:T(8,128)(2,1)}, bf16[4,448,256]{2,1,0:T(8,128)(2,1)S(1)}, u32[]{:S(2)}) copy-start(bf16[4,448,256]{2,1,0:T(8,128)(2,1)S(1)} %collective-permute-done.10.refs_6_) | copy-start | bytes 2752516
  148.7 10.5 %collective-permute-start.16 = (bf16[2,448,256]{2,1,0:T(8,128)(2,1)S(1)}, bf16[2,448,256]{2,1,0:T(8,128)(2,1)S(1)}, u32[]{:S(2)}, u32[]{:S(2)}) collective-permute-start(bf16[2,448,256]{2,1,0:T(8,128)(2,1)S(1)} %slice.63), channel_id=1, source_target_pairs={{0,24},{1,25},{2,26},{3,27},{4,28},{5,29},{6,30},{7,31},{8,0},{9,1... | collective-permute-start | bytes 1376264 | tf_op jit(solution)/shard_map/ppermute | solution.py:66
  152.0 11.1 %collective-permute-start.15 = (bf16[2,448,256]{2,1,0:T(8,128)(2,1)S(1)}, bf16[2,448,256]{2,1,0:T(8,128)(2,1)S(1)}, u32[]{:S(2)}, u32[]{:S(2)}) collective-permute-start(bf16[2,448,256]{2,1,0:T(8,128)(2,1)S(1)} %slice.62), channel_id=1, source_target_pairs={{0,8},{1,9},{2,10},{3,11},{4,12},{5,13},{6,14},{7,15},{8,16},{9,17... | collective-permute-start | bytes 1376264 | tf_op jit(solution)/shard_map/ppermute | solution.py:66
  152.2 14.2 %collective-permute-start.14 = (bf16[2,448,256]{2,1,0:T(8,128)(2,1)S(1)}, bf16[2,448,256]{2,1,0:T(8,128)(2,1)S(1)}, u32[]{:S(2)}, u32[]{:S(2)}) collective-permute-start(bf16[2,448,256]{2,1,0:T(8,128)(2,1)S(1)} %slice.61), channel_id=1, source_target_pairs={{0,192},{32,224},{64,0},{96,32},{128,64},{160,96},{192,128},{224,1... | collective-permute-start | bytes 1376264 | tf_op jit(solution)/shard_map/ppermute | solution.py:75
  153.8 13.0 %collective-permute-start.13 = (bf16[2,448,256]{2,1,0:T(8,128)(2,1)S(1)}, bf16[2,448,256]{2,1,0:T(8,128)(2,1)S(1)}, u32[]{:S(2)}, u32[]{:S(2)}) collective-permute-start(bf16[2,448,256]{2,1,0:T(8,128)(2,1)S(1)} %slice.60), channel_id=1, source_target_pairs={{0,64},{32,96},{64,128},{96,160},{128,192},{160,224},{192,0},{224,... | collective-permute-start | bytes 1376264 | tf_op jit(solution)/shard_map/ppermute | solution.py:75
  159.2 9.2 %collective-permute-start.26 = (bf16[2,448,256]{2,1,0:T(8,128)(2,1)S(1)}, bf16[2,448,256]{2,1,0:T(8,128)(2,1)S(1)}, u32[]{:S(2)}, u32[]{:S(2)}) collective-permute-start(bf16[2,448,256]{2,1,0:T(8,128)(2,1)S(1)} %collective-permute-done.16.refs_9_), channel_id=1, source_target_pairs={{0,32},{32,0},{64,96},{96,64},{128,160},{160,128},{192,224},{224,1... | collective-permute-start | bytes 1376264 | tf_op jit(solution)/shard_map/ppermute | solution.py:82
  163.1 5.3 %collective-permute-start.25 = (bf16[2,448,256]{2,1,0:T(8,128)(2,1)S(1)}, bf16[2,448,256]{2,1,0:T(8,128)(2,1)S(1)}, u32[]{:S(2)}, u32[]{:S(2)}) collective-permute-start(bf16[2,448,256]{2,1,0:T(8,128)(2,1)S(1)} %collective-permute-done.15.refs_8_), channel_id=1, source_target_pairs={{0,32},{32,0},{64,96},{96,64},{128,160},{160,128},{192,224},{224,1... | collective-permute-start | bytes 1376264 | tf_op jit(solution)/shard_map/ppermute | solution.py:82
  166.3 8.0 %collective-permute-start.18 = (bf16[4,448,256]{2,1,0:T(8,128)(2,1)S(1)}, bf16[4,448,256]{2,1,0:T(8,128)(2,1)S(1)}, u32[]{:S(2)}, u32[]{:S(2)}) collective-permute-start(bf16[4,448,256]{2,1,0:T(8,128)(2,1)S(1)} %collective-permute-done.9.refs_1_), channel_id=1, source_target_pairs={{0,32},{32,0},{64,96},{96,64},{128,160},{160,128},{192,224},{224,1... | collective-permute-start | bytes 2752520 | tf_op jit(solution)/shard_map/ppermute | solution.py:82
  166.4 3.3 %collective-permute-start.21 = (bf16[2,448,256]{2,1,0:T(8,128)(2,1)S(1)}, bf16[2,448,256]{2,1,0:T(8,128)(2,1)S(1)}, u32[]{:S(2)}, u32[]{:S(2)}) collective-permute-start(bf16[2,448,256]{2,1,0:T(8,128)(2,1)S(1)} %collective-permute-done.14.refs_4_), channel_id=1, source_target_pairs={{0,32},{32,0},{64,96},{96,64},{128,160},{160,128},{192,224},{224,1... | collective-permute-start | bytes 1376264 | tf_op jit(solution)/shard_map/ppermute | solution.py:82
  166.8 7.5 %collective-permute-start.19 = (bf16[4,448,256]{2,1,0:T(8,128)(2,1)S(1)}, bf16[4,448,256]{2,1,0:T(8,128)(2,1)S(1)}, u32[]{:S(2)}, u32[]{:S(2)}) collective-permute-start(bf16[4,448,256]{2,1,0:T(8,128)(2,1)S(1)} %collective-permute-done.11.refs_2_), channel_id=1, source_target_pairs={{0,32},{32,0},{64,96},{96,64},{128,160},{160,128},{192,224},{224,1... | collective-permute-start | bytes 2752520 | tf_op jit(solution)/shard_map/ppermute | solution.py:82
  168.4 5.9 %collective-permute-start.23 = (bf16[4,448,256]{2,1,0:T(8,128)(2,1)S(1)}, bf16[4,448,256]{2,1,0:T(8,128)(2,1)S(1)}, u32[]{:S(2)}, u32[]{:S(2)}) collective-permute-start(bf16[4,448,256]{2,1,0:T(8,128)(2,1)S(1)} %collective-permute-done.10.refs_6_), channel_id=1, source_target_pairs={{0,32},{32,0},{64,96},{96,64},{128,160},{160,128},{192,224},{224,1... | collective-permute-start | bytes 2752520 | tf_op jit(solution)/shard_map/ppermute | solution.py:82
  168.4 5.9 %collective-permute-start.24 = (bf16[4,448,256]{2,1,0:T(8,128)(2,1)S(1)}, bf16[4,448,256]{2,1,0:T(8,128)(2,1)S(1)}, u32[]{:S(2)}, u32[]{:S(2)}) collective-permute-start(bf16[4,448,256]{2,1,0:T(8,128)(2,1)S(1)} %collective-permute-done.12.refs_7_), channel_id=1, source_target_pairs={{0,32},{32,0},{64,96},{96,64},{128,160},{160,128},{192,224},{224,1... | collective-permute-start | bytes 2752520 | tf_op jit(solution)/shard_map/ppermute | solution.py:82
  169.7 4.6 %collective-permute-start.20 = (bf16[2,448,256]{2,1,0:T(8,128)(2,1)S(1)}, bf16[2,448,256]{2,1,0:T(8,128)(2,1)S(1)}, u32[]{:S(2)}, u32[]{:S(2)}) collective-permute-start(bf16[2,448,256]{2,1,0:T(8,128)(2,1)S(1)} %collective-permute-done.13.refs_3_), channel_id=1, source_target_pairs={{0,32},{32,0},{64,96},{96,64},{128,160},{160,128},{192,224},{224,1... | collective-permute-start | bytes 1376264 | tf_op jit(solution)/shard_map/ppermute | solution.py:82
  (7 other events, 38.3 us)
Sparse Core Ops, SparseCore 0:
  10.4 33.1 all-gather.1

commit v3 on v2

--- a/solution.py
+++ b/solution.py
@@ -39,6 +39,7 @@
 PIECE = TILE // 2
 CHUNK_PIECES = CHUNK // PIECE
 STEPS = 12
+STRIP = M // 4
 
 LINES = ((0, (0, 1, 2, 3)), (1, (0, 1, 2, 3)), (3, (0, 1, 2, 3)), (2, (0, 1)), (2, (2, 3)))
 PARTS = [
@@ -88,9 +89,26 @@
     )
 
 
-def gram_kernel(panel_ref, *refs):
-    chunk_refs, columns_ref = refs[:X_CHIPS], refs[X_CHIPS]
+def gram_kernel(*refs):
+    row_refs, refs = refs[:ROWS], refs[ROWS:]
+    chunk_refs, (columns_ref, panel_ref, sems) = refs[:X_CHIPS], refs[X_CHIPS:]
     row = lax.axis_index("row")
+    y, core = row // CORES, row % CORES
+    copies = []
+    for number, row_ref in enumerate(row_refs):
+        shift, c = number % Y_CHIPS, core if number < Y_CHIPS else 1 - core
+        owner = lax.rem(y + Y_CHIPS - shift, Y_CHIPS) * CORES + c
+        copies.append(
+            pltpu.make_async_copy(
+                row_ref,
+                panel_ref.at[pl.ds(pl.multiple_of(owner * OWN_ROWS, OWN_ROWS), OWN_ROWS), :],
+                sems.at[number],
+            )
+        )
+    for copy in copies:
+        copy.start()
+    for copy in copies:
+        copy.wait()
     x = lax.axis_index("col") // Z_CHIPS
     wanted = row * OWN_COLS + lax.broadcasted_iota(jnp.int32, (OWN_COLS, PANEL_COLS), 0)
     column = lax.broadcasted_iota(jnp.int32, (OWN_COLS, PANEL_COLS), 1)
@@ -115,17 +133,21 @@
         columns_ref[:, b * BLOCK : (b + 1) * BLOCK] = dot_nt(pick, rows).astype(jnp.bfloat16)
 
 
-def partial_gram(panel):
+def partial_gram(rows):
     vmem = pl.BlockSpec(memory_space=pltpu.VMEM)
     outs = pl.pallas_call(
         gram_kernel,
         out_shape=[jax.ShapeDtypeStruct((CHUNK, TILE), jnp.bfloat16)] * X_CHIPS
         + [jax.ShapeDtypeStruct((OWN_COLS, M), jnp.bfloat16)],
-        in_specs=[vmem],
+        in_specs=[pl.BlockSpec(memory_space=pl.ANY)] * ROWS,
         out_specs=[vmem] * (X_CHIPS + 1),
-        compiler_params=pltpu.CompilerParams(vmem_limit_bytes=32 * 2**20),
+        scratch_shapes=[
+            pltpu.VMEM((M, PANEL_COLS), jnp.bfloat16),
+            pltpu.SemaphoreType.DMA((ROWS,)),
+        ],
+        compiler_params=pltpu.CompilerParams(vmem_limit_bytes=16 * 2**20),
         name="partial_gram",
-    )(panel)
+    )(*rows)
     return outs[:X_CHIPS], outs[X_CHIPS]
 
 
@@ -134,14 +156,9 @@
     return pl.ds(start, TILE)
 
 
-def mirror_rows(j, d, half, column_half):
-    start = (((j * (KEPT - 1) + d - 1) * 2 + half) * 2 + column_half) * TILE
-    return pl.ds(start, TILE)
-
-
 def newton_schulz_kernel(base_ref, *refs):
     parts = refs[: len(PARTS)]
-    out_ref, gram, mirror, value, state, total, sems = refs[len(PARTS) :]
+    out_ref, tiles, gram, value, state, total, sems = refs[len(PARTS) :]
     row = lax.axis_index("row")
     y, core = row // CORES, row % CORES
     x = lax.axis_index("col") // Z_CHIPS
@@ -155,7 +172,7 @@
             copies.append(
                 pltpu.make_async_copy(
                     part.at[k],
-                    gram.at[pl.ds(pl.multiple_of(start, HALF_CHUNK), HALF_CHUNK), :],
+                    tiles.at[pl.ds(pl.multiple_of(start, HALF_CHUNK), HALF_CHUNK), :],
                     sems.at[len(copies)],
                 )
             )
@@ -172,21 +189,21 @@
         part = tile.astype(jnp.float32)
         return jnp.sum((part * part).reshape(TILE // 8, 8, TILE), axis=0)
 
-    def prepare(i, sums):
-        own, others = sums
-        for half in range(2):
-            for column_half in range(2):
-                own = own + square_sum(gram[tile_rows(i, 0, half, column_half), :])
-                for d in range(1, KEPT):
-                    tile = gram[tile_rows(i, d, half, column_half), :]
-                    others = others + square_sum(tile)
-                    mirror[mirror_rows(i, d, half, column_half), :] = dot_nt(
-                        identity, tile
-                    ).astype(jnp.bfloat16)
-        return own, others
-
-    zeros = jnp.zeros((8, TILE), jnp.float32)
-    own, others = lax.fori_loop(0, BLOCKS, prepare, (zeros, zeros))
+    own = others = jnp.zeros((8, TILE), jnp.float32)
+    for i in range(BLOCKS):
+        for d in range(KEPT):
+            j = (i + d) % BLOCKS
+            for half in range(2):
+                down = pl.ds(i * BLOCK + half * TILE, TILE)
+                for column_half in range(2):
+                    across = pl.ds(j * BLOCK + column_half * TILE, TILE)
+                    tile = tiles[tile_rows(i, d, half, column_half), :]
+                    gram[down, across] = tile
+                    if d == 0:
+                        own = own + square_sum(tile)
+                    else:
+                        others = others + square_sum(tile)
+                        gram[across, down] = dot_nt(identity, tile).astype(jnp.bfloat16)
     quartic = jnp.full((1, 1), jnp.sum(own + 2.0 * others), jnp.float32)
     scale = 1.0 / jnp.sqrt(jnp.sqrt(quartic) + EPSILON)
     square = scale * scale
@@ -203,33 +220,16 @@
         add = jnp.where(cubic, COEF_CUBIC, jnp.where(quintic, COEF_QUINTIC, 1.0))
         from_product = jnp.where(cubic, 1.0, 0.0)
         from_state = jnp.where(cubic, 0.0, 1.0)
-        for j in range(BLOCKS):
-            for column_half in range(2):
-                product = None
-                for d in range(KEPT):
-                    i = (j - d) % BLOCKS
-                    for half in range(2):
-                        term = jnp.dot(
-                            value[now, :, pl.ds(i * BLOCK + half * TILE, TILE)],
-                            gram[tile_rows(i, d, half, column_half), :],
-                            preferred_element_type=jnp.float32,
-                        )
-                        product = term if product is None else product + term
-                for d in range(1, KEPT):
-                    i = (j + d) % BLOCKS
-                    for half in range(2):
-                        product = product + jnp.dot(
-                            value[now, :, pl.ds(i * BLOCK + half * TILE, TILE)],
-                            mirror[mirror_rows(j, d, column_half, half), :],
-                            preferred_element_type=jnp.float32,
-                        )
-                cut = pl.ds(j * BLOCK + column_half * TILE, TILE)
-                product = square * product
-                result = keep * state[:, cut] + add * product
-                state[:, cut] = result
-                value[1 - now, :, cut] = (from_product * product + from_state * result).astype(
-                    jnp.bfloat16
-                )
+        for strip in range(M // STRIP):
+            cut = pl.ds(strip * STRIP, STRIP)
+            product = square * jnp.dot(
+                value[now], gram[:, cut], preferred_element_type=jnp.float32
+            )
+            result = keep * state[:, cut] + add * product
+            state[:, cut] = result
+            value[1 - now, :, cut] = (from_product * product + from_state * result).astype(
+                jnp.bfloat16
+            )
 
         @pl.when(number == 1)
         def _():
@@ -246,7 +246,6 @@
 
 
 def newton_schulz(base, parts):
-    mirror_tiles = BLOCKS * (KEPT - 1) * 4
     return pl.pallas_call(
         newton_schulz_kernel,
         out_shape=jax.ShapeDtypeStruct((OWN_COLS, M), jnp.bfloat16),
@@ -255,13 +254,13 @@
         out_specs=pl.BlockSpec(memory_space=pltpu.VMEM),
         scratch_shapes=[
             pltpu.VMEM((GRAM_ROWS, TILE), jnp.bfloat16),
-            pltpu.VMEM((mirror_tiles * TILE, TILE), jnp.bfloat16),
+            pltpu.VMEM((M, M), jnp.bfloat16),
             pltpu.VMEM((2, OWN_COLS, M), jnp.bfloat16),
             pltpu.VMEM((OWN_COLS, M), jnp.float32),
             pltpu.VMEM((OWN_COLS, M), jnp.float32),
             pltpu.SemaphoreType.DMA((sum(len(shifts) for _, shifts, _ in PARTS),)),
         ],
-        compiler_params=pltpu.CompilerParams(vmem_limit_bytes=48 * 2**20),
+        compiler_params=pltpu.CompilerParams(vmem_limit_bytes=43 * 2**20),
         name="newton_schulz",
     )(base, *parts)
 
@@ -300,8 +299,9 @@
     buffer = MOMENTUM_DECAY * momentum + grad32
     nesterov = grad32 + MOMENTUM_DECAY * buffer
     base = nesterov.astype(jnp.bfloat16)
-    panel = lax.all_gather(base, "row", axis=0, tiled=True)
-    chunks, columns = partial_gram(panel)
+    shifted = {k: over_y(base, k) for k in (1, 3, 2)}
+    rows = [base] + [shifted[k] for k in (1, 2, 3)]
+    chunks, columns = partial_gram(rows + [over_cores(part) for part in rows])
     parts = gathered(scattered_sum(chunks))
     update = newton_schulz(columns, parts)
     update = update.reshape(OWN_COLS, ROWS, OWN_ROWS).transpose(1, 0, 2)

time: 298 us -> 252 us (0.85)
  Pallas kernels: 104 us -> 76.8 us
  between operations: 14.2 us -> 0.81 us
  waiting for transfers between devices: 78.9 us -> 67.6 us
  starting transfers between devices: 43.9 us -> 52.8 us
  local copies, waits for them, and re-layouts: 5.34 us -> 1.72 us
    all_gather x1 -> x0, waiting for transfers between devices: 34.1 us -> none  [per_device(): panel = lax.all_gather(base, 'row', axis=0, tiled=True)]
    pallas_call x1, Pallas kernels: 101 us -> 73.3 us  [newton_schulz(): pl.pallas_call(newton_schulz_kernel, out_shape=jax.ShapeDtypeStruct((OWN_...]
    ppermute x7 -> x10, waiting for transfers between devices: 8.79 us -> 36.1 us  [over_y(): return lax.ppermute(value, 'row', pairs)]
    ppermute x10 -> x14, starting transfers between devices: 21.5 us -> 29.3 us  [over_cores(): return lax.ppermute(value, 'row', pairs)]
    unnamed x23 -> x11, local copies, waits for them, and re-layouts: 4.55 us -> 0.94 us
    ppermute x10, waiting for transfers between devices: 31.1 us -> 27.6 us  [over_x(): return lax.ppermute(value, 'col', pairs)]
    ppermute x7 -> x10, starting transfers between devices: 5.75 us -> 8.21 us  [over_y(): return lax.ppermute(value, 'row', pairs)]
  transfers between devices with their start and end apart: 28 -> 34, of which waited for: 12 -> 17; matrix products, arithmetic and copies ran while one was open for 0% -> 0% of each run, Pallas kernels for 0% -> 0%
where the time goes in v3:
time: 252 us; the launch traced here: 251 us
  Pallas kernels  76.8 us (30%)
  waiting for transfers between devices  67.6 us (27%)
  starting transfers between devices  52.8 us (21%)
  blocking collectives  49 us (19%)
  other arithmetic  2.7 us (1%)
    pallas_call x1, Pallas kernels, newton_schulz(): pl.pallas_call(newton_schulz_kernel, out_shape=jax.ShapeDtypeStruct((OWN_...  73.3 us
    all_to_all x2, blocking collectives, over_z(): lax.all_to_all(value, 'col', split_axis=0, concat_axis=0, axis_index_grou...  38.1 us
    ppermute x10, waiting for transfers between devices, over_y(): return lax.ppermute(value, 'row', pairs)  36.1 us
    ppermute x14, starting transfers between devices, over_cores(): return lax.ppermute(value, 'row', pairs)  29.3 us
    ppermute x10, waiting for transfers between devices, over_x(): return lax.ppermute(value, 'col', pairs)  27.6 us
    ppermute x10, starting transfers between devices, over_x(): return lax.ppermute(value, 'col', pairs)  15.4 us
    all_to_all x1, blocking collectives, per_device(): update = lax.all_to_all(update, 'row', split_axis=0, concat_axis=0)  10.9 us
    ppermute x10, starting transfers between devices, over_y(): return lax.ppermute(value, 'row', pairs)  8.21 us
  transfers between devices with their start and end apart: 34, of which 17 were waited for; matrix products, arithmetic and copies ran while one was open for 0% of the time, Pallas kernels for 0%

profile of v3, /device:TPU:1, one launch (start us, length us, event | category | flops | bytes accessed | tf_op | source)
XLA Modules:
  0.0 251.5 jit_solution(14520624310569212724)
XLA Ops:
  0.6 2.2 fusion
  2.8 3.6 %collective-permute-start.2 = (bf16[448,384]{1,0:T(8,128)(2,1)S(1)}, bf16[448,384]{1,0:T(8,128)(2,1)S(1)}, u32[]{:S(2)}, u32[]{:S(2)}) collective-permute-start(bf16[448,384]{1,0:T(8,128)(2,1)S(1)} %get-tuple-element.26.refs_0_), channel_id=1, source_target_pairs={{0,192},{32,224},{64,0},{96,32},{128,64},{160,96},{192,128},{224,1... | collective-permute-start | bytes 1032200 | tf_op jit(solution)/shard_map/ppermute | solution.py:76
  7.4 1.5 collective-permute-start.3
  8.9 11.4 %collective-permute-done.2.refs_3_ = bf16[448,384]{1,0:T(8,128)(2,1)S(1)} collective-permute-done((bf16[448,384]{1,0:T(8,128)(2,1)S(1)}, bf16[448,384]{1,0:T(8,128)(2,1)S(1)}, u32[]{:S(2)}, u32[]{:S(2)}) %collective-permute-start.2) | collective-permute-done | bytes 344096 | tf_op jit(solution)/shard_map/ppermute | solution.py:76
  20.3 1.7 collective-permute-start.6
  22.0 3.2 %collective-permute-done.refs_1_ = bf16[448,384]{1,0:T(8,128)(2,1)S(1)} collective-permute-done((bf16[448,384]{1,0:T(8,128)(2,1)S(1)}, bf16[448,384]{1,0:T(8,128)(2,1)S(1)}, u32[]{:S(2)}, u32[]{:S(2)}) %collective-permute-start) | collective-permute-done | bytes 344096 | tf_op jit(solution)/shard_map/ppermute | solution.py:76
  25.7 1.3 collective-permute-done.4.refs_5_
  27.0 3.5 %partial_gram.1 = (bf16[896,256]{1,0:T(8,128)(2,1)S(1)}, bf16[896,256]{1,0:T(8,128)(2,1)S(1)}, bf16[896,256]{1,0:T(8,128)(2,1)S(1)}, bf16[896,256]{1,0:T(8,128)(2,1)S(1)}, bf16[48,3584]{1,0:T(8,128)(2,1)S(1)}) custom-call(bf16[448,384]{1,0:T(8,128)(2,1)S(1)} %get-tuple-element.26.refs_0_, bf16[448,384]{1,0:T(8,128)(2,1)S(1)} %collective-permute-done.refs_1_, ...), custom_call_target="tpu_custom_call" | custom-call | tf_op jit(solution)/shard_map/partial_gram/pallas_call | solution.py:138
  30.5 2.8 %collective-permute-start.7 = (bf16[896,256]{1,0:T(8,128)(2,1)S(1)}, bf16[896,256]{1,0:T(8,128)(2,1)S(1)}, u32[]{:S(2)}, u32[]{:S(2)}) collective-permute-start(bf16[896,256]{1,0:T(8,128)(2,1)S(1)} %get-tuple-element.15), channel_id=1, source_target_pairs={{0,16},{1,17},{2,18},{3,19},{4,20},{5,21},{6,22},{7,23},{8,24},{9,... | collective-permute-start | bytes 1376264 | tf_op jit(solution)/shard_map/ppermute | solution.py:67
  33.7 2.4 collective-permute-start.9
  36.0 7.9 %collective-permute-done.7 = bf16[896,256]{1,0:T(8,128)(2,1)S(1)} collective-permute-done((bf16[896,256]{1,0:T(8,128)(2,1)S(1)}, bf16[896,256]{1,0:T(8,128)(2,1)S(1)}, u32[]{:S(2)}, u32[]{:S(2)}) %collective-permute-start.7) | collective-permute-done | bytes 458784 | tf_op jit(solution)/shard_map/ppermute | solution.py:67
  43.9 10.5 %collective-permute-done.8 = bf16[896,256]{1,0:T(8,128)(2,1)S(1)} collective-permute-done((bf16[896,256]{1,0:T(8,128)(2,1)S(1)}, bf16[896,256]{1,0:T(8,128)(2,1)S(1)}, u32[]{:S(2)}, u32[]{:S(2)}) %collective-permute-start.8) | collective-permute-done | bytes 458784 | tf_op jit(solution)/shard_map/ppermute | solution.py:67
  54.6 22.7 %all_to_all.15 = bf16[8,112,256]{2,1,0:T(8,128)(2,1)S(1)} all-to-all(bf16[8,112,256]{2,1,0:T(8,128)(2,1)S(1)} %bitcast.19), channel_id=1, replica_groups={{0,1,2,3,4,5,6,7},{8,9,10,11,12,13,14,15},{16,17,18,19,20,21,22,23},{24..., dimensions={0} | all-to-all | bytes 917504 | tf_op jit(solution)/shard_map/all_to_all | solution.py:87
  77.4 15.4 %all_to_all.16 = bf16[8,112,256]{2,1,0:T(8,128)(2,1)S(1)} all-to-all(bf16[8,112,256]{2,1,0:T(8,128)(2,1)S(1)} %broadcast_in_dim.9), channel_id=1, replica_groups={{0,1,2,3,4,5,6,7},{8,9,10,11,12,13,14,15},{16,17,18,19,20,21,22,23},{24..., dimensions={0} | all-to-all | bytes 917504 | tf_op jit(solution)/shard_map/all_to_all | solution.py:87
  92.9 3.1 %collective-permute-start.12 = (bf16[448,256]{1,0:T(8,128)(2,1)S(1)}, bf16[448,256]{1,0:T(8,128)(2,1)S(1)}, u32[]{:S(2)}, u32[]{:S(2)}) collective-permute-start(bf16[448,256]{1,0:T(8,128)(2,1)S(1)} %bitcast.26), channel_id=1, source_target_pairs={{0,24},{1,25},{2,26},{3,27},{4,28},{5,29},{6,30},{7,31},{8,0},{9,1... | collective-permute-start | bytes 688136 | tf_op jit(solution)/shard_map/ppermute | solution.py:67
  97.3 4.6 %collective-permute-done.12 = bf16[448,256]{1,0:T(8,128)(2,1)S(1)} collective-permute-done((bf16[448,256]{1,0:T(8,128)(2,1)S(1)}, bf16[448,256]{1,0:T(8,128)(2,1)S(1)}, u32[]{:S(2)}, u32[]{:S(2)}) %collective-permute-start.12) | collective-permute-done | bytes 229408 | tf_op jit(solution)/shard_map/ppermute | solution.py:67
  102.4 2.7 %collective-permute-done.10 = bf16[448,256]{1,0:T(8,128)(2,1)S(1)} collective-permute-done((bf16[448,256]{1,0:T(8,128)(2,1)S(1)}, bf16[448,256]{1,0:T(8,128)(2,1)S(1)}, u32[]{:S(2)}, u32[]{:S(2)}) %collective-permute-start.10) | collective-permute-done | bytes 229408 | tf_op jit(solution)/shard_map/ppermute | solution.py:67
  105.2 5.2 %collective-permute-done.13 = bf16[448,256]{1,0:T(8,128)(2,1)S(1)} collective-permute-done((bf16[448,256]{1,0:T(8,128)(2,1)S(1)}, bf16[448,256]{1,0:T(8,128)(2,1)S(1)}, u32[]{:S(2)}, u32[]{:S(2)}) %collective-permute-start.13) | collective-permute-done | bytes 229408 | tf_op jit(solution)/shard_map/ppermute | solution.py:76
  110.6 1.5 collective-permute-start.16
  112.1 3.4 %collective-permute-start.19 = (bf16[4,448,256]{2,1,0:T(8,128)(2,1)S(1)}, bf16[4,448,256]{2,1,0:T(8,128)(2,1)S(1)}, u32[]{:S(2)}, u32[]{:S(2)}) collective-permute-start(bf16[4,448,256]{2,1,0:T(8,128)(2,1)S(1)} %pad_maximum_fusion.1.refs_5_), channel_id=1, source_target_pairs={{0,24},{1,25},{2,26},{3,27},{4,28},{5,29},{6,30},{7,31},{8,0},{9,1... | collective-permute-start | bytes 2752520 | tf_op jit(solution)/shard_map/ppermute | solution.py:67
  115.5 4.3 %collective-permute-start.24 = (bf16[4,448,256]{2,1,0:T(8,128)(2,1)S(1)}, bf16[4,448,256]{2,1,0:T(8,128)(2,1)S(1)}, u32[]{:S(2)}, u32[]{:S(2)}) collective-permute-start(bf16[4,448,256]{2,1,0:T(8,128)(2,1)S(1)} %pad_maximum_fusion.refs_0_), channel_id=1, source_target_pairs={{0,32},{32,0},{64,96},{96,64},{128,160},{160,128},{192,224},{224,1... | collective-permute-start | bytes 2752520 | tf_op jit(solution)/shard_map/ppermute | solution.py:83
  119.8 9.2 %collective-permute-done.18.refs_2_ = bf16[4,448,256]{2,1,0:T(8,128)(2,1)S(1)} collective-permute-done((bf16[4,448,256]{2,1,0:T(8,128)(2,1)S(1)}, bf16[4,448,256]{2,1,0:T(8,128)(2,1)S(1)}, u32[]{:S(2)}, u32[]{:S(2)}) %collective-permute-start.18) | collective-permute-done | bytes 917536 | tf_op jit(solution)/shard_map/ppermute | solution.py:76
  129.0 4.4 %collective-permute-start.29 = (bf16[4,448,256]{2,1,0:T(8,128)(2,1)S(1)}, bf16[4,448,256]{2,1,0:T(8,128)(2,1)S(1)}, u32[]{:S(2)}, u32[]{:S(2)}) collective-permute-start(bf16[4,448,256]{2,1,0:T(8,128)(2,1)S(1)} %pad_maximum_fusion.1.refs_5_), channel_id=1, source_target_pairs={{0,32},{32,0},{64,96},{96,64},{128,160},{160,128},{192,224},{224,1... | collective-permute-start | bytes 2752520 | tf_op jit(solution)/shard_map/ppermute | solution.py:83
  134.3 2.6 %collective-permute-start.23 = (bf16[2,448,256]{2,1,0:T(8,128)(2,1)S(1)}, bf16[2,448,256]{2,1,0:T(8,128)(2,1)S(1)}, u32[]{:S(2)}, u32[]{:S(2)}) collective-permute-start(bf16[2,448,256]{2,1,0:T(8,128)(2,1)S(1)} %slice.63), channel_id=1, source_target_pairs={{0,24},{1,25},{2,26},{3,27},{4,28},{5,29},{6,30},{7,31},{8,0},{9,1... | collective-permute-start | bytes 1376264 | tf_op jit(solution)/shard_map/ppermute | solution.py:67
  137.1 1.3 collective-permute-start.21
  138.4 5.0 %collective-permute-start.25 = (bf16[4,448,256]{2,1,0:T(8,128)(2,1)S(1)}, bf16[4,448,256]{2,1,0:T(8,128)(2,1)S(1)}, u32[]{:S(2)}, u32[]{:S(2)}) collective-permute-start(bf16[4,448,256]{2,1,0:T(8,128)(2,1)S(1)} %collective-permute-done.16.refs_1_), channel_id=1, source_target_pairs={{0,32},{32,0},{64,96},{96,64},{128,160},{160,128},{192,224},{224,1... | collective-permute-start | bytes 2752520 | tf_op jit(solution)/shard_map/ppermute | solution.py:83
  144.1 4.0 %collective-permute-start.30 = (bf16[4,448,256]{2,1,0:T(8,128)(2,1)S(1)}, bf16[4,448,256]{2,1,0:T(8,128)(2,1)S(1)}, u32[]{:S(2)}, u32[]{:S(2)}) collective-permute-start(bf16[4,448,256]{2,1,0:T(8,128)(2,1)S(1)} %collective-permute-done.17.refs_6_), channel_id=1, source_target_pairs={{0,32},{32,0},{64,96},{96,64},{128,160},{160,128},{192,224},{224,1... | collective-permute-start | bytes 2752520 | tf_op jit(solution)/shard_map/ppermute | solution.py:83
  148.2 3.0 %collective-permute-start.31 = (bf16[4,448,256]{2,1,0:T(8,128)(2,1)S(1)}, bf16[4,448,256]{2,1,0:T(8,128)(2,1)S(1)}, u32[]{:S(2)}, u32[]{:S(2)}) collective-permute-start(bf16[4,448,256]{2,1,0:T(8,128)(2,1)S(1)} %collective-permute-done.19.refs_7_), channel_id=1, source_target_pairs={{0,32},{32,0},{64,96},{96,64},{128,160},{160,128},{192,224},{224,1... | collective-permute-start | bytes 2752520 | tf_op jit(solution)/shard_map/ppermute | solution.py:83
  151.2 7.1 %collective-permute-done.20.refs_3_ = bf16[2,448,256]{2,1,0:T(8,128)(2,1)S(1)} collective-permute-done((bf16[2,448,256]{2,1,0:T(8,128)(2,1)S(1)}, bf16[2,448,256]{2,1,0:T(8,128)(2,1)S(1)}, u32[]{:S(2)}, u32[]{:S(2)}) %collective-permute-start.20) | collective-permute-done | bytes 458784 | tf_op jit(solution)/shard_map/ppermute | solution.py:76
  158.4 4.0 %collective-permute-start.33 = (bf16[2,448,256]{2,1,0:T(8,128)(2,1)S(1)}, bf16[2,448,256]{2,1,0:T(8,128)(2,1)S(1)}, u32[]{:S(2)}, u32[]{:S(2)}) collective-permute-start(bf16[2,448,256]{2,1,0:T(8,128)(2,1)S(1)} %collective-permute-done.23.refs_9_), channel_id=1, source_target_pairs={{0,32},{32,0},{64,96},{96,64},{128,160},{160,128},{192,224},{224,1... | collective-permute-start | bytes 1376264 | tf_op jit(solution)/shard_map/ppermute | solution.py:83
  165.8 73.3 %newton_schulz.1 = bf16[48,3584]{1,0:T(8,128)(2,1)S(1)} custom-call(bf16[48,3584]{1,0:T(8,128)(2,1)S(1)} %get-tuple-element.13.base_ref, bf16[4,448,256]{2,1,0:T(8,128)(2,1)S(1)} %pad_maximum_fusion.refs_0_, bf16[4,448,256]{2,1,0:T(8,128)(2,1)S(1)} %collective-permute-done.16.refs_1_, bf16[4,448,256]{2,1,0:T(8,128)(2,1)S(1)} %collective-permute-done.18.refs_2_, ...), custom_call_target="tpu_custom_call" | custom-call | tf_op jit(solution)/shard_map/newton_schulz/pallas_call | solution.py:249
  239.7 10.9 %all_to_all.17 = bf16[8,48,448]{2,1,0:T(8,128)(2,1)S(1)} all-to-all(bf16[8,48,448]{2,1,0:T(8,128)(2,1)S(1)} %bitcast.20), channel_id=1, replica_groups=mesh['row'=8,'col'=32] {'row'}, dimensions={0} | all-to-all | bytes 688128 | tf_op jit(solution)/shard_map/all_to_all | solution.py:308
  (65 shorter events, 11.2 us)
Async XLA Ops:
  2.8 17.5 %collective-permute-start.2 = (bf16[448,384]{1,0:T(8,128)(2,1)S(1)}, bf16[448,384]{1,0:T(8,128)(2,1)S(1)}, u32[]{:S(2)}, u32[]{:S(2)}) collective-permute-start(bf16[448,384]{1,0:T(8,128)(2,1)S(1)} %get-tuple-element.26.refs_0_), channel_id=1, source_target_pairs={{0,192},{32,224},{64,0},{96,32},{128,64},{160,96},{192,128},{224,1... | collective-permute-start | bytes 1032200 | tf_op jit(solution)/shard_map/ppermute | solution.py:76
  6.4 15.7 %collective-permute-start.1 = (bf16[448,384]{1,0:T(8,128)(2,1)S(1)}, bf16[448,384]{1,0:T(8,128)(2,1)S(1)}, u32[]{:S(2)}, u32[]{:S(2)}) collective-permute-start(bf16[448,384]{1,0:T(8,128)(2,1)S(1)} %get-tuple-element.26.refs_0_), channel_id=1, source_target_pairs={{0,128},{32,160},{64,192},{96,224},{128,0},{160,32},{192,64},{224,... | collective-permute-start | bytes 1032200 | tf_op jit(solution)/shard_map/ppermute | solution.py:76
  6.7 18.5 %collective-permute-start = (bf16[448,384]{1,0:T(8,128)(2,1)S(1)}, bf16[448,384]{1,0:T(8,128)(2,1)S(1)}, u32[]{:S(2)}, u32[]{:S(2)}) collective-permute-start(bf16[448,384]{1,0:T(8,128)(2,1)S(1)} %get-tuple-element.26.refs_0_), channel_id=1, source_target_pairs={{0,64},{32,96},{64,128},{96,160},{128,192},{160,224},{192,0},{224,... | collective-permute-start | bytes 1032200 | tf_op jit(solution)/shard_map/ppermute | solution.py:76
  7.4 18.3 %collective-permute-start.3 = (bf16[448,384]{1,0:T(8,128)(2,1)S(1)}, bf16[448,384]{1,0:T(8,128)(2,1)S(1)}, u32[]{:S(2)}, u32[]{:S(2)}) collective-permute-start(bf16[448,384]{1,0:T(8,128)(2,1)S(1)} %get-tuple-element.26.refs_0_), channel_id=1, source_target_pairs={{0,32},{32,0},{64,96},{96,64},{128,160},{160,128},{192,224},{224,1... | collective-permute-start | bytes 1032200 | tf_op jit(solution)/shard_map/ppermute | solution.py:83
  20.3 5.4 %collective-permute-start.6 = (bf16[448,384]{1,0:T(8,128)(2,1)S(1)}, bf16[448,384]{1,0:T(8,128)(2,1)S(1)}, u32[]{:S(2)}, u32[]{:S(2)}) collective-permute-start(bf16[448,384]{1,0:T(8,128)(2,1)S(1)} %collective-permute-done.2.refs_3_), channel_id=1, source_target_pairs={{0,32},{32,0},{64,96},{96,64},{128,160},{160,128},{192,224},{224,1... | collective-permute-start | bytes 1032200 | tf_op jit(solution)/shard_map/ppermute | solution.py:83
  22.0 3.7 %collective-permute-start.5 = (bf16[448,384]{1,0:T(8,128)(2,1)S(1)}, bf16[448,384]{1,0:T(8,128)(2,1)S(1)}, u32[]{:S(2)}, u32[]{:S(2)}) collective-permute-start(bf16[448,384]{1,0:T(8,128)(2,1)S(1)} %collective-permute-done.1.refs_2_), channel_id=1, source_target_pairs={{0,32},{32,0},{64,96},{96,64},{128,160},{160,128},{192,224},{224,1... | collective-permute-start | bytes 1032200 | tf_op jit(solution)/shard_map/ppermute | solution.py:83
  30.5 13.4 %collective-permute-start.7 = (bf16[896,256]{1,0:T(8,128)(2,1)S(1)}, bf16[896,256]{1,0:T(8,128)(2,1)S(1)}, u32[]{:S(2)}, u32[]{:S(2)}) collective-permute-start(bf16[896,256]{1,0:T(8,128)(2,1)S(1)} %get-tuple-element.15), channel_id=1, source_target_pairs={{0,16},{1,17},{2,18},{3,19},{4,20},{5,21},{6,22},{7,23},{8,24},{9,... | collective-permute-start | bytes 1376264 | tf_op jit(solution)/shard_map/ppermute | solution.py:67
  33.3 21.0 %collective-permute-start.8 = (bf16[896,256]{1,0:T(8,128)(2,1)S(1)}, bf16[896,256]{1,0:T(8,128)(2,1)S(1)}, u32[]{:S(2)}, u32[]{:S(2)}) collective-permute-start(bf16[896,256]{1,0:T(8,128)(2,1)S(1)} %get-tuple-element.16), channel_id=1, source_target_pairs={{0,8},{1,9},{2,10},{3,11},{4,12},{5,13},{6,14},{7,15},{8,16},{9,17... | collective-permute-start | bytes 1376264 | tf_op jit(solution)/shard_map/ppermute | solution.py:67
  33.7 20.7 %collective-permute-start.9 = (bf16[896,256]{1,0:T(8,128)(2,1)S(1)}, bf16[896,256]{1,0:T(8,128)(2,1)S(1)}, u32[]{:S(2)}, u32[]{:S(2)}) collective-permute-start(bf16[896,256]{1,0:T(8,128)(2,1)S(1)} %get-tuple-element.17), channel_id=1, source_target_pairs={{0,24},{1,25},{2,26},{3,27},{4,28},{5,29},{6,30},{7,31},{8,0},{9,1... | collective-permute-start | bytes 1376264 | tf_op jit(solution)/shard_map/ppermute | solution.py:67
  92.9 9.0 %collective-permute-start.12 = (bf16[448,256]{1,0:T(8,128)(2,1)S(1)}, bf16[448,256]{1,0:T(8,128)(2,1)S(1)}, u32[]{:S(2)}, u32[]{:S(2)}) collective-permute-start(bf16[448,256]{1,0:T(8,128)(2,1)S(1)} %bitcast.26), channel_id=1, source_target_pairs={{0,24},{1,25},{2,26},{3,27},{4,28},{5,29},{6,30},{7,31},{8,0},{9,1... | collective-permute-start | bytes 688136 | tf_op jit(solution)/shard_map/ppermute | solution.py:67
  95.9 6.5 %collective-permute-start.11 = (bf16[448,256]{1,0:T(8,128)(2,1)S(1)}, bf16[448,256]{1,0:T(8,128)(2,1)S(1)}, u32[]{:S(2)}, u32[]{:S(2)}) collective-permute-start(bf16[448,256]{1,0:T(8,128)(2,1)S(1)} %bitcast.27), channel_id=1, source_target_pairs={{0,16},{1,17},{2,18},{3,19},{4,20},{5,21},{6,22},{7,23},{8,24},{9,... | collective-permute-start | bytes 688136 | tf_op jit(solution)/shard_map/ppermute | solution.py:67
  96.1 9.0 %collective-permute-start.10 = (bf16[448,256]{1,0:T(8,128)(2,1)S(1)}, bf16[448,256]{1,0:T(8,128)(2,1)S(1)}, u32[]{:S(2)}, u32[]{:S(2)}) collective-permute-start(bf16[448,256]{1,0:T(8,128)(2,1)S(1)} %bitcast.28), channel_id=1, source_target_pairs={{0,8},{1,9},{2,10},{3,11},{4,12},{5,13},{6,14},{7,15},{8,16},{9,17... | collective-permute-start | bytes 688136 | tf_op jit(solution)/shard_map/ppermute | solution.py:67
  96.6 8.6 %collective-permute-start.15 = (bf16[448,256]{1,0:T(8,128)(2,1)S(1)}, bf16[448,256]{1,0:T(8,128)(2,1)S(1)}, u32[]{:S(2)}, u32[]{:S(2)}) collective-permute-start(bf16[448,256]{1,0:T(8,128)(2,1)S(1)} %bitcast.22), channel_id=1, source_target_pairs={{0,192},{32,224},{64,0},{96,32},{128,64},{160,96},{192,128},{224,1... | collective-permute-start | bytes 688136 | tf_op jit(solution)/shard_map/ppermute | solution.py:76
  97.3 7.9 %collective-permute-start.14 = (bf16[448,256]{1,0:T(8,128)(2,1)S(1)}, bf16[448,256]{1,0:T(8,128)(2,1)S(1)}, u32[]{:S(2)}, u32[]{:S(2)}) collective-permute-start(bf16[448,256]{1,0:T(8,128)(2,1)S(1)} %bitcast.23), channel_id=1, source_target_pairs={{0,128},{32,160},{64,192},{96,224},{128,0},{160,32},{192,64},{224,... | collective-permute-start | bytes 688136 | tf_op jit(solution)/shard_map/ppermute | solution.py:76
  101.9 8.5 %collective-permute-start.13 = (bf16[448,256]{1,0:T(8,128)(2,1)S(1)}, bf16[448,256]{1,0:T(8,128)(2,1)S(1)}, u32[]{:S(2)}, u32[]{:S(2)}) collective-permute-start(bf16[448,256]{1,0:T(8,128)(2,1)S(1)} %bitcast.24), channel_id=1, source_target_pairs={{0,64},{32,96},{64,128},{96,160},{128,192},{160,224},{192,0},{224,... | collective-permute-start | bytes 688136 | tf_op jit(solution)/shard_map/ppermute | solution.py:76
  110.6 18.5 %collective-permute-start.18 = (bf16[4,448,256]{2,1,0:T(8,128)(2,1)S(1)}, bf16[4,448,256]{2,1,0:T(8,128)(2,1)S(1)}, u32[]{:S(2)}, u32[]{:S(2)}) collective-permute-start(bf16[4,448,256]{2,1,0:T(8,128)(2,1)S(1)} %pad_maximum_fusion.refs_0_), channel_id=1, source_target_pairs={{0,192},{32,224},{64,0},{96,32},{128,64},{160,96},{192,128},{224,1... | collective-permute-start | bytes 2752520 | tf_op jit(solution)/shard_map/ppermute | solution.py:76
  110.6 22.8 %collective-permute-start.16 = (bf16[4,448,256]{2,1,0:T(8,128)(2,1)S(1)}, bf16[4,448,256]{2,1,0:T(8,128)(2,1)S(1)}, u32[]{:S(2)}, u32[]{:S(2)}) collective-permute-start(bf16[4,448,256]{2,1,0:T(8,128)(2,1)S(1)} %pad_maximum_fusion.refs_0_), channel_id=1, source_target_pairs={{0,64},{32,96},{64,128},{96,160},{128,192},{160,224},{192,0},{224,... | collective-permute-start | bytes 2752520 | tf_op jit(solution)/shard_map/ppermute | solution.py:76
  112.1 21.3 %collective-permute-start.19 = (bf16[4,448,256]{2,1,0:T(8,128)(2,1)S(1)}, bf16[4,448,256]{2,1,0:T(8,128)(2,1)S(1)}, u32[]{:S(2)}, u32[]{:S(2)}) collective-permute-start(bf16[4,448,256]{2,1,0:T(8,128)(2,1)S(1)} %pad_maximum_fusion.1.refs_5_), channel_id=1, source_target_pairs={{0,24},{1,25},{2,26},{3,27},{4,28},{5,29},{6,30},{7,31},{8,0},{9,1... | collective-permute-start | bytes 2752520 | tf_op jit(solution)/shard_map/ppermute | solution.py:67
  115.5 18.8 %collective-permute-start.17 = (bf16[4,448,256]{2,1,0:T(8,128)(2,1)S(1)}, bf16[4,448,256]{2,1,0:T(8,128)(2,1)S(1)}, u32[]{:S(2)}, u32[]{:S(2)}) collective-permute-start(bf16[4,448,256]{2,1,0:T(8,128)(2,1)S(1)} %pad_maximum_fusion.1.refs_5_), channel_id=1, source_target_pairs={{0,8},{1,9},{2,10},{3,11},{4,12},{5,13},{6,14},{7,15},{8,16},{9,17... | collective-permute-start | bytes 2752520 | tf_op jit(solution)/shard_map/ppermute | solution.py:67
  115.5 22.9 %collective-permute-start.24 = (bf16[4,448,256]{2,1,0:T(8,128)(2,1)S(1)}, bf16[4,448,256]{2,1,0:T(8,128)(2,1)S(1)}, u32[]{:S(2)}, u32[]{:S(2)}) collective-permute-start(bf16[4,448,256]{2,1,0:T(8,128)(2,1)S(1)} %pad_maximum_fusion.refs_0_), channel_id=1, source_target_pairs={{0,32},{32,0},{64,96},{96,64},{128,160},{160,128},{192,224},{224,1... | collective-permute-start | bytes 2752520 | tf_op jit(solution)/shard_map/ppermute | solution.py:83
  129.0 14.3 %collective-permute-start.29 = (bf16[4,448,256]{2,1,0:T(8,128)(2,1)S(1)}, bf16[4,448,256]{2,1,0:T(8,128)(2,1)S(1)}, u32[]{:S(2)}, u32[]{:S(2)}) collective-permute-start(bf16[4,448,256]{2,1,0:T(8,128)(2,1)S(1)} %pad_maximum_fusion.1.refs_5_), channel_id=1, source_target_pairs={{0,32},{32,0},{64,96},{96,64},{128,160},{160,128},{192,224},{224,1... | collective-permute-start | bytes 2752520 | tf_op jit(solution)/shard_map/ppermute | solution.py:83
  134.3 9.8 %collective-permute-start.23 = (bf16[2,448,256]{2,1,0:T(8,128)(2,1)S(1)}, bf16[2,448,256]{2,1,0:T(8,128)(2,1)S(1)}, u32[]{:S(2)}, u32[]{:S(2)}) collective-permute-start(bf16[2,448,256]{2,1,0:T(8,128)(2,1)S(1)} %slice.63), channel_id=1, source_target_pairs={{0,24},{1,25},{2,26},{3,27},{4,28},{5,29},{6,30},{7,31},{8,0},{9,1... | collective-permute-start | bytes 1376264 | tf_op jit(solution)/shard_map/ppermute | solution.py:67
  137.0 11.1 %collective-permute-start.22 = (bf16[2,448,256]{2,1,0:T(8,128)(2,1)S(1)}, bf16[2,448,256]{2,1,0:T(8,128)(2,1)S(1)}, u32[]{:S(2)}, u32[]{:S(2)}) collective-permute-start(bf16[2,448,256]{2,1,0:T(8,128)(2,1)S(1)} %slice.62), channel_id=1, source_target_pairs={{0,8},{1,9},{2,10},{3,11},{4,12},{5,13},{6,14},{7,15},{8,16},{9,17... | collective-permute-start | bytes 1376264 | tf_op jit(solution)/shard_map/ppermute | solution.py:67
  137.1 11.1 %collective-permute-start.21 = (bf16[2,448,256]{2,1,0:T(8,128)(2,1)S(1)}, bf16[2,448,256]{2,1,0:T(8,128)(2,1)S(1)}, u32[]{:S(2)}, u32[]{:S(2)}) collective-permute-start(bf16[2,448,256]{2,1,0:T(8,128)(2,1)S(1)} %slice.61), channel_id=1, source_target_pairs={{0,192},{32,224},{64,0},{96,32},{128,64},{160,96},{192,128},{224,1... | collective-permute-start | bytes 1376264 | tf_op jit(solution)/shard_map/ppermute | solution.py:76
  138.4 23.9 %collective-permute-start.25 = (bf16[4,448,256]{2,1,0:T(8,128)(2,1)S(1)}, bf16[4,448,256]{2,1,0:T(8,128)(2,1)S(1)}, u32[]{:S(2)}, u32[]{:S(2)}) collective-permute-start(bf16[4,448,256]{2,1,0:T(8,128)(2,1)S(1)} %collective-permute-done.16.refs_1_), channel_id=1, source_target_pairs={{0,32},{32,0},{64,96},{96,64},{128,160},{160,128},{192,224},{224,1... | collective-permute-start | bytes 2752520 | tf_op jit(solution)/shard_map/ppermute | solution.py:83
  143.4 19.1 %collective-permute-start.26 = (bf16[4,448,256]{2,1,0:T(8,128)(2,1)S(1)}, bf16[4,448,256]{2,1,0:T(8,128)(2,1)S(1)}, u32[]{:S(2)}, u32[]{:S(2)}) collective-permute-start(bf16[4,448,256]{2,1,0:T(8,128)(2,1)S(1)} %collective-permute-done.18.refs_2_), channel_id=1, source_target_pairs={{0,32},{32,0},{64,96},{96,64},{128,160},{160,128},{192,224},{224,1... | collective-permute-start | bytes 2752520 | tf_op jit(solution)/shard_map/ppermute | solution.py:83
  144.1 18.8 %collective-permute-start.30 = (bf16[4,448,256]{2,1,0:T(8,128)(2,1)S(1)}, bf16[4,448,256]{2,1,0:T(8,128)(2,1)S(1)}, u32[]{:S(2)}, u32[]{:S(2)}) collective-permute-start(bf16[4,448,256]{2,1,0:T(8,128)(2,1)S(1)} %collective-permute-done.17.refs_6_), channel_id=1, source_target_pairs={{0,32},{32,0},{64,96},{96,64},{128,160},{160,128},{192,224},{224,1... | collective-permute-start | bytes 2752520 | tf_op jit(solution)/shard_map/ppermute | solution.py:83
  148.1 10.3 %collective-permute-start.20 = (bf16[2,448,256]{2,1,0:T(8,128)(2,1)S(1)}, bf16[2,448,256]{2,1,0:T(8,128)(2,1)S(1)}, u32[]{:S(2)}, u32[]{:S(2)}) collective-permute-start(bf16[2,448,256]{2,1,0:T(8,128)(2,1)S(1)} %slice.60), channel_id=1, source_target_pairs={{0,64},{32,96},{64,128},{96,160},{128,192},{160,224},{192,0},{224,... | collective-permute-start | bytes 1376264 | tf_op jit(solution)/shard_map/ppermute | solution.py:76
  148.2 15.0 %collective-permute-start.31 = (bf16[4,448,256]{2,1,0:T(8,128)(2,1)S(1)}, bf16[4,448,256]{2,1,0:T(8,128)(2,1)S(1)}, u32[]{:S(2)}, u32[]{:S(2)}) collective-permute-start(bf16[4,448,256]{2,1,0:T(8,128)(2,1)S(1)} %collective-permute-done.19.refs_7_), channel_id=1, source_target_pairs={{0,32},{32,0},{64,96},{96,64},{128,160},{160,128},{192,224},{224,1... | collective-permute-start | bytes 2752520 | tf_op jit(solution)/shard_map/ppermute | solution.py:83
  158.4 5.4 %collective-permute-start.33 = (bf16[2,448,256]{2,1,0:T(8,128)(2,1)S(1)}, bf16[2,448,256]{2,1,0:T(8,128)(2,1)S(1)}, u32[]{:S(2)}, u32[]{:S(2)}) collective-permute-start(bf16[2,448,256]{2,1,0:T(8,128)(2,1)S(1)} %collective-permute-done.23.refs_9_), channel_id=1, source_target_pairs={{0,32},{32,0},{64,96},{96,64},{128,160},{160,128},{192,224},{224,1... | collective-permute-start | bytes 1376264 | tf_op jit(solution)/shard_map/ppermute | solution.py:83
  162.4 2.7 %collective-permute-start.28 = (bf16[2,448,256]{2,1,0:T(8,128)(2,1)S(1)}, bf16[2,448,256]{2,1,0:T(8,128)(2,1)S(1)}, u32[]{:S(2)}, u32[]{:S(2)}) collective-permute-start(bf16[2,448,256]{2,1,0:T(8,128)(2,1)S(1)} %collective-permute-done.21.refs_4_), channel_id=1, source_target_pairs={{0,32},{32,0},{64,96},{96,64},{128,160},{160,128},{192,224},{224,1... | collective-permute-start | bytes 1376264 | tf_op jit(solution)/shard_map/ppermute | solution.py:83
  162.9 2.9 %collective-permute-start.27 = (bf16[2,448,256]{2,1,0:T(8,128)(2,1)S(1)}, bf16[2,448,256]{2,1,0:T(8,128)(2,1)S(1)}, u32[]{:S(2)}, u32[]{:S(2)}) collective-permute-start(bf16[2,448,256]{2,1,0:T(8,128)(2,1)S(1)} %collective-permute-done.20.refs_3_), channel_id=1, source_target_pairs={{0,32},{32,0},{64,96},{96,64},{128,160},{160,128},{192,224},{224,1... | collective-permute-start | bytes 1376264 | tf_op jit(solution)/shard_map/ppermute | solution.py:83
  (7 other events, 38.5 us)

commit v4 on v3

--- a/solution.py
+++ b/solution.py
@@ -260,7 +260,7 @@
             pltpu.VMEM((OWN_COLS, M), jnp.float32),
             pltpu.SemaphoreType.DMA((sum(len(shifts) for _, shifts, _ in PARTS),)),
         ],
-        compiler_params=pltpu.CompilerParams(vmem_limit_bytes=43 * 2**20),
+        compiler_params=pltpu.CompilerParams(vmem_limit_bytes=58 * 2**20),
         name="newton_schulz",
     )(base, *parts)
 
@@ -287,11 +287,15 @@
     second = jnp.stack([second] + [from_y[k] for k in (1, 2, 3)])
     first, second = lax.optimization_barrier((first, second))
     ups, downs = [over_y(first, 1), over_x(second, 1)], [over_y(first, 3), over_x(second, 3)]
-    ups, downs = lax.optimization_barrier((ups, downs))
-    parts = []
-    for own, over, up, down in zip((first, second), (over_y, over_x), ups, downs):
-        parts += [own, up, down, over(up[:2], 1), over(down[2:], 3)]
-    return parts + [over_cores(part) for part in parts]
+    swapped = [over_cores(first), over_cores(second)]
+    onward = [up[:2] for up in ups], [down[2:] for down in downs]
+    ups, downs, onward, swapped = lax.optimization_barrier((ups, downs, onward, swapped))
+    own_core, other_core = [], []
+    far = [[over(up, 1), over(down, 3)] for over, up, down in zip((over_y, over_x), *onward)]
+    for own, swap, up, down, rest in zip((first, second), swapped, ups, downs, far):
+        own_core += [own, up, down] + rest
+        other_core += [swap] + [over_cores(part) for part in [up, down] + rest]
+    return own_core + other_core
 
 
 def per_device(gradient, momentum):

time: 252 us -> 246 us (0.976)
  Pallas kernels: 76.8 us -> 67.7 us
  waiting for transfers between devices: 67.6 us -> 70.9 us
  local copies, waits for them, and re-layouts: 1.72 us -> 4.69 us
  starting transfers between devices: 52.8 us -> 50 us
    pallas_call x1, Pallas kernels: 73.3 us -> 64.2 us  [newton_schulz(): pl.pallas_call(newton_schulz_kernel, out_shape=jax.ShapeDtypeStruct((OWN_...]
    ppermute x10, waiting for transfers between devices: 27.6 us -> 36.4 us  [over_x(): return lax.ppermute(value, 'col', pairs)]
    ppermute x10, waiting for transfers between devices: 36.1 us -> 30.5 us  [over_y(): return lax.ppermute(value, 'row', pairs)]
    ppermute x14, starting transfers between devices: 29.3 us -> 24.4 us  [over_cores(): return lax.ppermute(value, 'row', pairs)]
where the time goes in v4:
time: 246 us
  waiting for transfers between devices  70.9 us (29%)
  Pallas kernels  67.7 us (28%)
  starting transfers between devices  50 us (20%)
  blocking collectives  48.9 us (20%)
  local copies, waits for them, and re-layouts  4.69 us (2%)
  other arithmetic  2.7 us (1%)
    pallas_call x1, Pallas kernels, newton_schulz(): pl.pallas_call(newton_schulz_kernel, out_shape=jax.ShapeDtypeStruct((OWN_...  64.2 us
    all_to_all x2, blocking collectives, over_z(): lax.all_to_all(value, 'col', split_axis=0, concat_axis=0, axis_index_grou...  38.1 us
    ppermute x10, waiting for transfers between devices, over_x(): return lax.ppermute(value, 'col', pairs)  36.4 us
    ppermute x10, waiting for transfers between devices, over_y(): return lax.ppermute(value, 'row', pairs)  30.5 us
    ppermute x14, starting transfers between devices, over_cores(): return lax.ppermute(value, 'row', pairs)  24.4 us
    ppermute x10, starting transfers between devices, over_x(): return lax.ppermute(value, 'col', pairs)  16.1 us
    all_to_all x1, blocking collectives, per_device(): update = lax.all_to_all(update, 'row', split_axis=0, concat_axis=0)  10.8 us
    ppermute x10, starting transfers between devices, over_y(): return lax.ppermute(value, 'row', pairs)  9.51 us
  transfers between devices with their start and end apart: 34, of which 17 were waited for; matrix products, arithmetic and copies ran while one was open for 0% of the time, Pallas kernels for 0%

profile of v4, /device:TPU:1, one launch (start us, length us, event | category | flops | bytes accessed | tf_op | source)
XLA Modules:
  0.0 245.7 jit_solution(2001891585010525246)
XLA Ops:
  0.6 2.2 fusion
  2.8 3.6 %collective-permute-start.2 = (bf16[448,384]{1,0:T(8,128)(2,1)S(1)}, bf16[448,384]{1,0:T(8,128)(2,1)S(1)}, u32[]{:S(2)}, u32[]{:S(2)}) collective-permute-start(bf16[448,384]{1,0:T(8,128)(2,1)S(1)} %get-tuple-element.38.refs_0_), channel_id=1, source_target_pairs={{0,192},{32,224},{64,0},{96,32},{128,64},{160,96},{192,128},{224,1... | collective-permute-start | bytes 1032200 | tf_op jit(solution)/shard_map/ppermute | solution.py:76
  7.4 1.5 collective-permute-start.3
  8.9 11.4 %collective-permute-done.2.refs_3_ = bf16[448,384]{1,0:T(8,128)(2,1)S(1)} collective-permute-done((bf16[448,384]{1,0:T(8,128)(2,1)S(1)}, bf16[448,384]{1,0:T(8,128)(2,1)S(1)}, u32[]{:S(2)}, u32[]{:S(2)}) %collective-permute-start.2) | collective-permute-done | bytes 344096 | tf_op jit(solution)/shard_map/ppermute | solution.py:76
  20.3 1.7 collective-permute-start.6
  22.0 3.2 %collective-permute-done.refs_1_ = bf16[448,384]{1,0:T(8,128)(2,1)S(1)} collective-permute-done((bf16[448,384]{1,0:T(8,128)(2,1)S(1)}, bf16[448,384]{1,0:T(8,128)(2,1)S(1)}, u32[]{:S(2)}, u32[]{:S(2)}) %collective-permute-start) | collective-permute-done | bytes 344096 | tf_op jit(solution)/shard_map/ppermute | solution.py:76
  25.7 1.3 collective-permute-done.4.refs_5_
  27.0 3.5 %partial_gram.1 = (bf16[896,256]{1,0:T(8,128)(2,1)S(1)}, bf16[896,256]{1,0:T(8,128)(2,1)S(1)}, bf16[896,256]{1,0:T(8,128)(2,1)S(1)}, bf16[896,256]{1,0:T(8,128)(2,1)S(1)}, bf16[48,3584]{1,0:T(8,128)(2,1)S(1)}) custom-call(bf16[448,384]{1,0:T(8,128)(2,1)S(1)} %get-tuple-element.38.refs_0_, bf16[448,384]{1,0:T(8,128)(2,1)S(1)} %collective-permute-done.refs_1_, ...), custom_call_target="tpu_custom_call" | custom-call | tf_op jit(solution)/shard_map/partial_gram/pallas_call | solution.py:138
  30.5 2.8 %collective-permute-start.7 = (bf16[896,256]{1,0:T(8,128)(2,1)S(1)}, bf16[896,256]{1,0:T(8,128)(2,1)S(1)}, u32[]{:S(2)}, u32[]{:S(2)}) collective-permute-start(bf16[896,256]{1,0:T(8,128)(2,1)S(1)} %get-tuple-element.21), channel_id=1, source_target_pairs={{0,16},{1,17},{2,18},{3,19},{4,20},{5,21},{6,22},{7,23},{8,24},{9,... | collective-permute-start | bytes 1376264 | tf_op jit(solution)/shard_map/ppermute | solution.py:67
  33.7 2.4 collective-permute-start.9
  36.0 7.9 %collective-permute-done.7 = bf16[896,256]{1,0:T(8,128)(2,1)S(1)} collective-permute-done((bf16[896,256]{1,0:T(8,128)(2,1)S(1)}, bf16[896,256]{1,0:T(8,128)(2,1)S(1)}, u32[]{:S(2)}, u32[]{:S(2)}) %collective-permute-start.7) | collective-permute-done | bytes 458784 | tf_op jit(solution)/shard_map/ppermute | solution.py:67
  43.9 10.5 %collective-permute-done.8 = bf16[896,256]{1,0:T(8,128)(2,1)S(1)} collective-permute-done((bf16[896,256]{1,0:T(8,128)(2,1)S(1)}, bf16[896,256]{1,0:T(8,128)(2,1)S(1)}, u32[]{:S(2)}, u32[]{:S(2)}) %collective-permute-start.8) | collective-permute-done | bytes 458784 | tf_op jit(solution)/shard_map/ppermute | solution.py:67
  54.6 22.7 %all_to_all.15 = bf16[8,112,256]{2,1,0:T(8,128)(2,1)S(1)} all-to-all(bf16[8,112,256]{2,1,0:T(8,128)(2,1)S(1)} %bitcast.19), channel_id=1, replica_groups={{0,1,2,3,4,5,6,7},{8,9,10,11,12,13,14,15},{16,17,18,19,20,21,22,23},{24..., dimensions={0} | all-to-all | bytes 917504 | tf_op jit(solution)/shard_map/all_to_all | solution.py:87
  77.4 15.4 %all_to_all.16 = bf16[8,112,256]{2,1,0:T(8,128)(2,1)S(1)} all-to-all(bf16[8,112,256]{2,1,0:T(8,128)(2,1)S(1)} %broadcast_in_dim.9), channel_id=1, replica_groups={{0,1,2,3,4,5,6,7},{8,9,10,11,12,13,14,15},{16,17,18,19,20,21,22,23},{24..., dimensions={0} | all-to-all | bytes 917504 | tf_op jit(solution)/shard_map/all_to_all | solution.py:87
  92.9 3.1 %collective-permute-start.12 = (bf16[448,256]{1,0:T(8,128)(2,1)S(1)}, bf16[448,256]{1,0:T(8,128)(2,1)S(1)}, u32[]{:S(2)}, u32[]{:S(2)}) collective-permute-start(bf16[448,256]{1,0:T(8,128)(2,1)S(1)} %bitcast.26), channel_id=1, source_target_pairs={{0,24},{1,25},{2,26},{3,27},{4,28},{5,29},{6,30},{7,31},{8,0},{9,1... | collective-permute-start | bytes 688136 | tf_op jit(solution)/shard_map/ppermute | solution.py:67
  97.3 4.6 %collective-permute-done.12 = bf16[448,256]{1,0:T(8,128)(2,1)S(1)} collective-permute-done((bf16[448,256]{1,0:T(8,128)(2,1)S(1)}, bf16[448,256]{1,0:T(8,128)(2,1)S(1)}, u32[]{:S(2)}, u32[]{:S(2)}) %collective-permute-start.12) | collective-permute-done | bytes 229408 | tf_op jit(solution)/shard_map/ppermute | solution.py:67
  102.4 2.8 %collective-permute-done.10 = bf16[448,256]{1,0:T(8,128)(2,1)S(1)} collective-permute-done((bf16[448,256]{1,0:T(8,128)(2,1)S(1)}, bf16[448,256]{1,0:T(8,128)(2,1)S(1)}, u32[]{:S(2)}, u32[]{:S(2)}) %collective-permute-start.10) | collective-permute-done | bytes 229408 | tf_op jit(solution)/shard_map/ppermute | solution.py:67
  105.4 5.1 %collective-permute-done.13 = bf16[448,256]{1,0:T(8,128)(2,1)S(1)} collective-permute-done((bf16[448,256]{1,0:T(8,128)(2,1)S(1)}, bf16[448,256]{1,0:T(8,128)(2,1)S(1)}, u32[]{:S(2)}, u32[]{:S(2)}) %collective-permute-start.13) | collective-permute-done | bytes 229408 | tf_op jit(solution)/shard_map/ppermute | solution.py:76
  110.7 1.5 collective-permute-start.16
  112.1 3.4 %collective-permute-start.19 = (bf16[4,448,256]{2,1,0:T(8,128)(2,1)S(1)}, bf16[4,448,256]{2,1,0:T(8,128)(2,1)S(1)}, u32[]{:S(2)}, u32[]{:S(2)}) collective-permute-start(bf16[4,448,256]{2,1,0:T(8,128)(2,1)S(1)} %pad_maximum_fusion.1.refs_5_), channel_id=1, source_target_pairs={{0,24},{1,25},{2,26},{3,27},{4,28},{5,29},{6,30},{7,31},{8,0},{9,1... | collective-permute-start | bytes 2752520 | tf_op jit(solution)/shard_map/ppermute | solution.py:67
  115.5 4.3 %collective-permute-start.20 = (bf16[4,448,256]{2,1,0:T(8,128)(2,1)S(1)}, bf16[4,448,256]{2,1,0:T(8,128)(2,1)S(1)}, u32[]{:S(2)}, u32[]{:S(2)}) collective-permute-start(bf16[4,448,256]{2,1,0:T(8,128)(2,1)S(1)} %pad_maximum_fusion.refs_0_), channel_id=1, source_target_pairs={{0,32},{32,0},{64,96},{96,64},{128,160},{160,128},{192,224},{224,1... | collective-permute-start | bytes 2752520 | tf_op jit(solution)/shard_map/ppermute | solution.py:83
  119.8 9.2 %collective-permute-done.18.refs_2_ = bf16[4,448,256]{2,1,0:T(8,128)(2,1)S(1)} collective-permute-done((bf16[4,448,256]{2,1,0:T(8,128)(2,1)S(1)}, bf16[4,448,256]{2,1,0:T(8,128)(2,1)S(1)}, u32[]{:S(2)}, u32[]{:S(2)}) %collective-permute-start.18) | collective-permute-done | bytes 917536 | tf_op jit(solution)/shard_map/ppermute | solution.py:76
  129.0 4.4 %collective-permute-start.21 = (bf16[4,448,256]{2,1,0:T(8,128)(2,1)S(1)}, bf16[4,448,256]{2,1,0:T(8,128)(2,1)S(1)}, u32[]{:S(2)}, u32[]{:S(2)}) collective-permute-start(bf16[4,448,256]{2,1,0:T(8,128)(2,1)S(1)} %pad_maximum_fusion.1.refs_5_), channel_id=1, source_target_pairs={{0,32},{32,0},{64,96},{96,64},{128,160},{160,128},{192,224},{224,1... | collective-permute-start | bytes 2752520 | tf_op jit(solution)/shard_map/ppermute | solution.py:83
  135.5 2.7 %collective-permute-start.23 = (bf16[2,448,256]{2,1,0:T(8,128)(2,1)S(1)}, bf16[2,448,256]{2,1,0:T(8,128)(2,1)S(1)}, u32[]{:S(2)}, u32[]{:S(2)}) collective-permute-start(bf16[2,448,256]{2,1,0:T(8,128)(2,1)S(1)} %slice.76), channel_id=1, source_target_pairs={{0,192},{32,224},{64,0},{96,32},{128,64},{160,96},{192,128},{224,1... | collective-permute-start | bytes 1376264 | tf_op jit(solution)/shard_map/ppermute | solution.py:76
  138.2 4.7 %collective-permute-start.26 = (bf16[4,448,256]{2,1,0:T(8,128)(2,1)S(1)}, bf16[4,448,256]{2,1,0:T(8,128)(2,1)S(1)}, u32[]{:S(2)}, u32[]{:S(2)}) collective-permute-start(bf16[4,448,256]{2,1,0:T(8,128)(2,1)S(1)} %collective-permute-done.16.refs_1_), channel_id=1, source_target_pairs={{0,32},{32,0},{64,96},{96,64},{128,160},{160,128},{192,224},{224,1... | collective-permute-start | bytes 2752520 | tf_op jit(solution)/shard_map/ppermute | solution.py:83
  143.0 1.6 collective-permute-done.22.refs_3_
  144.6 5.1 %collective-permute-start.30 = (bf16[4,448,256]{2,1,0:T(8,128)(2,1)S(1)}, bf16[4,448,256]{2,1,0:T(8,128)(2,1)S(1)}, u32[]{:S(2)}, u32[]{:S(2)}) collective-permute-start(bf16[4,448,256]{2,1,0:T(8,128)(2,1)S(1)} %collective-permute-done.17.refs_6_), channel_id=1, source_target_pairs={{0,32},{32,0},{64,96},{96,64},{128,160},{160,128},{192,224},{224,1... | collective-permute-start | bytes 2752520 | tf_op jit(solution)/shard_map/ppermute | solution.py:83
  149.7 3.4 %collective-permute-start.25 = (bf16[2,448,256]{2,1,0:T(8,128)(2,1)S(1)}, bf16[2,448,256]{2,1,0:T(8,128)(2,1)S(1)}, u32[]{:S(2)}, u32[]{:S(2)}) collective-permute-start(bf16[2,448,256]{2,1,0:T(8,128)(2,1)S(1)} %slice.77), channel_id=1, source_target_pairs={{0,24},{1,25},{2,26},{3,27},{4,28},{5,29},{6,30},{7,31},{8,0},{9,1... | collective-permute-start | bytes 1376264 | tf_op jit(solution)/shard_map/ppermute | solution.py:67
  153.6 9.4 %collective-permute-done.25.refs_9_ = bf16[2,448,256]{2,1,0:T(8,128)(2,1)S(1)} collective-permute-done((bf16[2,448,256]{2,1,0:T(8,128)(2,1)S(1)}, bf16[2,448,256]{2,1,0:T(8,128)(2,1)S(1)}, u32[]{:S(2)}, u32[]{:S(2)}) %collective-permute-start.25) | collective-permute-done | bytes 458784 | tf_op jit(solution)/shard_map/ppermute | solution.py:67
  168.2 64.2 %newton_schulz.1 = bf16[48,3584]{1,0:T(8,128)(2,1)} custom-call(bf16[48,3584]{1,0:T(8,128)(2,1)} %copy-done, bf16[4,448,256]{2,1,0:T(8,128)(2,1)} %copy-done.1, bf16[4,448,256]{2,1,0:T(8,128)(2,1)} %copy-done.4, bf16[4,448,256]{2,1,0:T(8,128)(2,1)} %copy-done.3, bf16[2,448,256]{2,1,0:T(8,128)(2,1)} %copy-done.13, bf16[2,448,256]{2,1,0:T(8,128)(2,1)} %copy-done.14, ...), custom_call_target="tpu_custom_call" | custom-call | tf_op jit(solution)/shard_map/newton_schulz/pallas_call | solution.py:249
  232.4 1.5 reshape.19
  234.0 10.8 %all_to_all.17 = bf16[8,48,448]{2,1,0:T(8,128)(2,1)S(1)} all-to-all(bf16[8,48,448]{2,1,0:T(8,128)(2,1)S(1)} %bitcast.20), channel_id=1, replica_groups=mesh['row'=8,'col'=32] {'row'}, dimensions={0} | all-to-all | bytes 688128 | tf_op jit(solution)/shard_map/all_to_all | solution.py:312
  (97 shorter events, 13.2 us)
Async XLA Ops:
  2.8 17.5 %collective-permute-start.2 = (bf16[448,384]{1,0:T(8,128)(2,1)S(1)}, bf16[448,384]{1,0:T(8,128)(2,1)S(1)}, u32[]{:S(2)}, u32[]{:S(2)}) collective-permute-start(bf16[448,384]{1,0:T(8,128)(2,1)S(1)} %get-tuple-element.38.refs_0_), channel_id=1, source_target_pairs={{0,192},{32,224},{64,0},{96,32},{128,64},{160,96},{192,128},{224,1... | collective-permute-start | bytes 1032200 | tf_op jit(solution)/shard_map/ppermute | solution.py:76
  6.4 15.7 %collective-permute-start.1 = (bf16[448,384]{1,0:T(8,128)(2,1)S(1)}, bf16[448,384]{1,0:T(8,128)(2,1)S(1)}, u32[]{:S(2)}, u32[]{:S(2)}) collective-permute-start(bf16[448,384]{1,0:T(8,128)(2,1)S(1)} %get-tuple-element.38.refs_0_), channel_id=1, source_target_pairs={{0,128},{32,160},{64,192},{96,224},{128,0},{160,32},{192,64},{224,... | collective-permute-start | bytes 1032200 | tf_op jit(solution)/shard_map/ppermute | solution.py:76
  6.7 18.5 %collective-permute-start = (bf16[448,384]{1,0:T(8,128)(2,1)S(1)}, bf16[448,384]{1,0:T(8,128)(2,1)S(1)}, u32[]{:S(2)}, u32[]{:S(2)}) collective-permute-start(bf16[448,384]{1,0:T(8,128)(2,1)S(1)} %get-tuple-element.38.refs_0_), channel_id=1, source_target_pairs={{0,64},{32,96},{64,128},{96,160},{128,192},{160,224},{192,0},{224,... | collective-permute-start | bytes 1032200 | tf_op jit(solution)/shard_map/ppermute | solution.py:76
  7.4 18.3 %collective-permute-start.3 = (bf16[448,384]{1,0:T(8,128)(2,1)S(1)}, bf16[448,384]{1,0:T(8,128)(2,1)S(1)}, u32[]{:S(2)}, u32[]{:S(2)}) collective-permute-start(bf16[448,384]{1,0:T(8,128)(2,1)S(1)} %get-tuple-element.38.refs_0_), channel_id=1, source_target_pairs={{0,32},{32,0},{64,96},{96,64},{128,160},{160,128},{192,224},{224,1... | collective-permute-start | bytes 1032200 | tf_op jit(solution)/shard_map/ppermute | solution.py:83
  20.3 5.4 %collective-permute-start.6 = (bf16[448,384]{1,0:T(8,128)(2,1)S(1)}, bf16[448,384]{1,0:T(8,128)(2,1)S(1)}, u32[]{:S(2)}, u32[]{:S(2)}) collective-permute-start(bf16[448,384]{1,0:T(8,128)(2,1)S(1)} %collective-permute-done.2.refs_3_), channel_id=1, source_target_pairs={{0,32},{32,0},{64,96},{96,64},{128,160},{160,128},{192,224},{224,1... | collective-permute-start | bytes 1032200 | tf_op jit(solution)/shard_map/ppermute | solution.py:83
  22.0 3.7 %collective-permute-start.5 = (bf16[448,384]{1,0:T(8,128)(2,1)S(1)}, bf16[448,384]{1,0:T(8,128)(2,1)S(1)}, u32[]{:S(2)}, u32[]{:S(2)}) collective-permute-start(bf16[448,384]{1,0:T(8,128)(2,1)S(1)} %collective-permute-done.1.refs_2_), channel_id=1, source_target_pairs={{0,32},{32,0},{64,96},{96,64},{128,160},{160,128},{192,224},{224,1... | collective-permute-start | bytes 1032200 | tf_op jit(solution)/shard_map/ppermute | solution.py:83
  30.5 13.4 %collective-permute-start.7 = (bf16[896,256]{1,0:T(8,128)(2,1)S(1)}, bf16[896,256]{1,0:T(8,128)(2,1)S(1)}, u32[]{:S(2)}, u32[]{:S(2)}) collective-permute-start(bf16[896,256]{1,0:T(8,128)(2,1)S(1)} %get-tuple-element.21), channel_id=1, source_target_pairs={{0,16},{1,17},{2,18},{3,19},{4,20},{5,21},{6,22},{7,23},{8,24},{9,... | collective-permute-start | bytes 1376264 | tf_op jit(solution)/shard_map/ppermute | solution.py:67
  33.4 21.0 %collective-permute-start.8 = (bf16[896,256]{1,0:T(8,128)(2,1)S(1)}, bf16[896,256]{1,0:T(8,128)(2,1)S(1)}, u32[]{:S(2)}, u32[]{:S(2)}) collective-permute-start(bf16[896,256]{1,0:T(8,128)(2,1)S(1)} %get-tuple-element.22), channel_id=1, source_target_pairs={{0,8},{1,9},{2,10},{3,11},{4,12},{5,13},{6,14},{7,15},{8,16},{9,17... | collective-permute-start | bytes 1376264 | tf_op jit(solution)/shard_map/ppermute | solution.py:67
  33.7 20.7 %collective-permute-start.9 = (bf16[896,256]{1,0:T(8,128)(2,1)S(1)}, bf16[896,256]{1,0:T(8,128)(2,1)S(1)}, u32[]{:S(2)}, u32[]{:S(2)}) collective-permute-start(bf16[896,256]{1,0:T(8,128)(2,1)S(1)} %get-tuple-element.23), channel_id=1, source_target_pairs={{0,24},{1,25},{2,26},{3,27},{4,28},{5,29},{6,30},{7,31},{8,0},{9,1... | collective-permute-start | bytes 1376264 | tf_op jit(solution)/shard_map/ppermute | solution.py:67
  92.9 9.0 %collective-permute-start.12 = (bf16[448,256]{1,0:T(8,128)(2,1)S(1)}, bf16[448,256]{1,0:T(8,128)(2,1)S(1)}, u32[]{:S(2)}, u32[]{:S(2)}) collective-permute-start(bf16[448,256]{1,0:T(8,128)(2,1)S(1)} %bitcast.26), channel_id=1, source_target_pairs={{0,24},{1,25},{2,26},{3,27},{4,28},{5,29},{6,30},{7,31},{8,0},{9,1... | collective-permute-start | bytes 688136 | tf_op jit(solution)/shard_map/ppermute | solution.py:67
  95.9 6.5 %collective-permute-start.11 = (bf16[448,256]{1,0:T(8,128)(2,1)S(1)}, bf16[448,256]{1,0:T(8,128)(2,1)S(1)}, u32[]{:S(2)}, u32[]{:S(2)}) collective-permute-start(bf16[448,256]{1,0:T(8,128)(2,1)S(1)} %bitcast.27), channel_id=1, source_target_pairs={{0,16},{1,17},{2,18},{3,19},{4,20},{5,21},{6,22},{7,23},{8,24},{9,... | collective-permute-start | bytes 688136 | tf_op jit(solution)/shard_map/ppermute | solution.py:67
  96.2 9.0 %collective-permute-start.10 = (bf16[448,256]{1,0:T(8,128)(2,1)S(1)}, bf16[448,256]{1,0:T(8,128)(2,1)S(1)}, u32[]{:S(2)}, u32[]{:S(2)}) collective-permute-start(bf16[448,256]{1,0:T(8,128)(2,1)S(1)} %bitcast.28), channel_id=1, source_target_pairs={{0,8},{1,9},{2,10},{3,11},{4,12},{5,13},{6,14},{7,15},{8,16},{9,17... | collective-permute-start | bytes 688136 | tf_op jit(solution)/shard_map/ppermute | solution.py:67
  96.6 8.7 %collective-permute-start.15 = (bf16[448,256]{1,0:T(8,128)(2,1)S(1)}, bf16[448,256]{1,0:T(8,128)(2,1)S(1)}, u32[]{:S(2)}, u32[]{:S(2)}) collective-permute-start(bf16[448,256]{1,0:T(8,128)(2,1)S(1)} %bitcast.22), channel_id=1, source_target_pairs={{0,192},{32,224},{64,0},{96,32},{128,64},{160,96},{192,128},{224,1... | collective-permute-start | bytes 688136 | tf_op jit(solution)/shard_map/ppermute | solution.py:76
  97.3 8.1 %collective-permute-start.14 = (bf16[448,256]{1,0:T(8,128)(2,1)S(1)}, bf16[448,256]{1,0:T(8,128)(2,1)S(1)}, u32[]{:S(2)}, u32[]{:S(2)}) collective-permute-start(bf16[448,256]{1,0:T(8,128)(2,1)S(1)} %bitcast.23), channel_id=1, source_target_pairs={{0,128},{32,160},{64,192},{96,224},{128,0},{160,32},{192,64},{224,... | collective-permute-start | bytes 688136 | tf_op jit(solution)/shard_map/ppermute | solution.py:76
  101.9 8.5 %collective-permute-start.13 = (bf16[448,256]{1,0:T(8,128)(2,1)S(1)}, bf16[448,256]{1,0:T(8,128)(2,1)S(1)}, u32[]{:S(2)}, u32[]{:S(2)}) collective-permute-start(bf16[448,256]{1,0:T(8,128)(2,1)S(1)} %bitcast.24), channel_id=1, source_target_pairs={{0,64},{32,96},{64,128},{96,160},{128,192},{160,224},{192,0},{224,... | collective-permute-start | bytes 688136 | tf_op jit(solution)/shard_map/ppermute | solution.py:76
  110.6 18.5 %collective-permute-start.18 = (bf16[4,448,256]{2,1,0:T(8,128)(2,1)S(1)}, bf16[4,448,256]{2,1,0:T(8,128)(2,1)S(1)}, u32[]{:S(2)}, u32[]{:S(2)}) collective-permute-start(bf16[4,448,256]{2,1,0:T(8,128)(2,1)S(1)} %pad_maximum_fusion.refs_0_), channel_id=1, source_target_pairs={{0,192},{32,224},{64,0},{96,32},{128,64},{160,96},{192,128},{224,1... | collective-permute-start | bytes 2752520 | tf_op jit(solution)/shard_map/ppermute | solution.py:76
  110.7 22.8 %collective-permute-start.16 = (bf16[4,448,256]{2,1,0:T(8,128)(2,1)S(1)}, bf16[4,448,256]{2,1,0:T(8,128)(2,1)S(1)}, u32[]{:S(2)}, u32[]{:S(2)}) collective-permute-start(bf16[4,448,256]{2,1,0:T(8,128)(2,1)S(1)} %pad_maximum_fusion.refs_0_), channel_id=1, source_target_pairs={{0,64},{32,96},{64,128},{96,160},{128,192},{160,224},{192,0},{224,... | collective-permute-start | bytes 2752520 | tf_op jit(solution)/shard_map/ppermute | solution.py:76
  112.1 21.4 %collective-permute-start.19 = (bf16[4,448,256]{2,1,0:T(8,128)(2,1)S(1)}, bf16[4,448,256]{2,1,0:T(8,128)(2,1)S(1)}, u32[]{:S(2)}, u32[]{:S(2)}) collective-permute-start(bf16[4,448,256]{2,1,0:T(8,128)(2,1)S(1)} %pad_maximum_fusion.1.refs_5_), channel_id=1, source_target_pairs={{0,24},{1,25},{2,26},{3,27},{4,28},{5,29},{6,30},{7,31},{8,0},{9,1... | collective-permute-start | bytes 2752520 | tf_op jit(solution)/shard_map/ppermute | solution.py:67
  115.5 18.8 %collective-permute-start.17 = (bf16[4,448,256]{2,1,0:T(8,128)(2,1)S(1)}, bf16[4,448,256]{2,1,0:T(8,128)(2,1)S(1)}, u32[]{:S(2)}, u32[]{:S(2)}) collective-permute-start(bf16[4,448,256]{2,1,0:T(8,128)(2,1)S(1)} %pad_maximum_fusion.1.refs_5_), channel_id=1, source_target_pairs={{0,8},{1,9},{2,10},{3,11},{4,12},{5,13},{6,14},{7,15},{8,16},{9,17... | collective-permute-start | bytes 2752520 | tf_op jit(solution)/shard_map/ppermute | solution.py:67
  115.5 18.8 %collective-permute-start.20 = (bf16[4,448,256]{2,1,0:T(8,128)(2,1)S(1)}, bf16[4,448,256]{2,1,0:T(8,128)(2,1)S(1)}, u32[]{:S(2)}, u32[]{:S(2)}) collective-permute-start(bf16[4,448,256]{2,1,0:T(8,128)(2,1)S(1)} %pad_maximum_fusion.refs_0_), channel_id=1, source_target_pairs={{0,32},{32,0},{64,96},{96,64},{128,160},{160,128},{192,224},{224,1... | collective-permute-start | bytes 2752520 | tf_op jit(solution)/shard_map/ppermute | solution.py:83
  129.0 6.5 %collective-permute-start.21 = (bf16[4,448,256]{2,1,0:T(8,128)(2,1)S(1)}, bf16[4,448,256]{2,1,0:T(8,128)(2,1)S(1)}, u32[]{:S(2)}, u32[]{:S(2)}) collective-permute-start(bf16[4,448,256]{2,1,0:T(8,128)(2,1)S(1)} %pad_maximum_fusion.1.refs_5_), channel_id=1, source_target_pairs={{0,32},{32,0},{64,96},{96,64},{128,160},{160,128},{192,224},{224,1... | collective-permute-start | bytes 2752520 | tf_op jit(solution)/shard_map/ppermute | solution.py:83
  135.5 9.1 %collective-permute-start.22 = (bf16[2,448,256]{2,1,0:T(8,128)(2,1)S(1)}, bf16[2,448,256]{2,1,0:T(8,128)(2,1)S(1)}, u32[]{:S(2)}, u32[]{:S(2)}) collective-permute-start(bf16[2,448,256]{2,1,0:T(8,128)(2,1)S(1)} %slice.74), channel_id=1, source_target_pairs={{0,64},{32,96},{64,128},{96,160},{128,192},{160,224},{192,0},{224,... | collective-permute-start | bytes 1376264 | tf_op jit(solution)/shard_map/ppermute | solution.py:76
  135.5 14.1 %collective-permute-start.23 = (bf16[2,448,256]{2,1,0:T(8,128)(2,1)S(1)}, bf16[2,448,256]{2,1,0:T(8,128)(2,1)S(1)}, u32[]{:S(2)}, u32[]{:S(2)}) collective-permute-start(bf16[2,448,256]{2,1,0:T(8,128)(2,1)S(1)} %slice.76), channel_id=1, source_target_pairs={{0,192},{32,224},{64,0},{96,32},{128,64},{160,96},{192,128},{224,1... | collective-permute-start | bytes 1376264 | tf_op jit(solution)/shard_map/ppermute | solution.py:76
  138.2 14.9 %collective-permute-start.24 = (bf16[2,448,256]{2,1,0:T(8,128)(2,1)S(1)}, bf16[2,448,256]{2,1,0:T(8,128)(2,1)S(1)}, u32[]{:S(2)}, u32[]{:S(2)}) collective-permute-start(bf16[2,448,256]{2,1,0:T(8,128)(2,1)S(1)} %slice.75), channel_id=1, source_target_pairs={{0,8},{1,9},{2,10},{3,11},{4,12},{5,13},{6,14},{7,15},{8,16},{9,17... | collective-permute-start | bytes 1376264 | tf_op jit(solution)/shard_map/ppermute | solution.py:67
  138.2 25.6 %collective-permute-start.26 = (bf16[4,448,256]{2,1,0:T(8,128)(2,1)S(1)}, bf16[4,448,256]{2,1,0:T(8,128)(2,1)S(1)}, u32[]{:S(2)}, u32[]{:S(2)}) collective-permute-start(bf16[4,448,256]{2,1,0:T(8,128)(2,1)S(1)} %collective-permute-done.16.refs_1_), channel_id=1, source_target_pairs={{0,32},{32,0},{64,96},{96,64},{128,160},{160,128},{192,224},{224,1... | collective-permute-start | bytes 2752520 | tf_op jit(solution)/shard_map/ppermute | solution.py:83
  142.9 21.3 %collective-permute-start.27 = (bf16[4,448,256]{2,1,0:T(8,128)(2,1)S(1)}, bf16[4,448,256]{2,1,0:T(8,128)(2,1)S(1)}, u32[]{:S(2)}, u32[]{:S(2)}) collective-permute-start(bf16[4,448,256]{2,1,0:T(8,128)(2,1)S(1)} %collective-permute-done.18.refs_2_), channel_id=1, source_target_pairs={{0,32},{32,0},{64,96},{96,64},{128,160},{160,128},{192,224},{224,1... | collective-permute-start | bytes 2752520 | tf_op jit(solution)/shard_map/ppermute | solution.py:83
  144.6 19.8 %collective-permute-start.30 = (bf16[4,448,256]{2,1,0:T(8,128)(2,1)S(1)}, bf16[4,448,256]{2,1,0:T(8,128)(2,1)S(1)}, u32[]{:S(2)}, u32[]{:S(2)}) collective-permute-start(bf16[4,448,256]{2,1,0:T(8,128)(2,1)S(1)} %collective-permute-done.17.refs_6_), channel_id=1, source_target_pairs={{0,32},{32,0},{64,96},{96,64},{128,160},{160,128},{192,224},{224,1... | collective-permute-start | bytes 2752520 | tf_op jit(solution)/shard_map/ppermute | solution.py:83
  149.7 13.3 %collective-permute-start.25 = (bf16[2,448,256]{2,1,0:T(8,128)(2,1)S(1)}, bf16[2,448,256]{2,1,0:T(8,128)(2,1)S(1)}, u32[]{:S(2)}, u32[]{:S(2)}) collective-permute-start(bf16[2,448,256]{2,1,0:T(8,128)(2,1)S(1)} %slice.77), channel_id=1, source_target_pairs={{0,24},{1,25},{2,26},{3,27},{4,28},{5,29},{6,30},{7,31},{8,0},{9,1... | collective-permute-start | bytes 1376264 | tf_op jit(solution)/shard_map/ppermute | solution.py:67
  153.1 11.6 %collective-permute-start.31 = (bf16[4,448,256]{2,1,0:T(8,128)(2,1)S(1)}, bf16[4,448,256]{2,1,0:T(8,128)(2,1)S(1)}, u32[]{:S(2)}, u32[]{:S(2)}) collective-permute-start(bf16[4,448,256]{2,1,0:T(8,128)(2,1)S(1)} %collective-permute-done.19.refs_7_), channel_id=1, source_target_pairs={{0,32},{32,0},{64,96},{96,64},{128,160},{160,128},{192,224},{224,1... | collective-permute-start | bytes 2752520 | tf_op jit(solution)/shard_map/ppermute | solution.py:83
  163.0 2.8 %collective-permute-start.28 = (bf16[2,448,256]{2,1,0:T(8,128)(2,1)S(1)}, bf16[2,448,256]{2,1,0:T(8,128)(2,1)S(1)}, u32[]{:S(2)}, u32[]{:S(2)}) collective-permute-start(bf16[2,448,256]{2,1,0:T(8,128)(2,1)S(1)} %collective-permute-done.22.refs_3_), channel_id=1, source_target_pairs={{0,32},{32,0},{64,96},{96,64},{128,160},{160,128},{192,224},{224,1... | collective-permute-start | bytes 1376264 | tf_op jit(solution)/shard_map/ppermute | solution.py:83
  164.2 2.4 collective-permute-start.32
  164.4 2.9 %collective-permute-start.33 = (bf16[2,448,256]{2,1,0:T(8,128)(2,1)S(1)}, bf16[2,448,256]{2,1,0:T(8,128)(2,1)S(1)}, u32[]{:S(2)}, u32[]{:S(2)}) collective-permute-start(bf16[2,448,256]{2,1,0:T(8,128)(2,1)S(1)} %collective-permute-done.25.refs_9_), channel_id=1, source_target_pairs={{0,32},{32,0},{64,96},{96,64},{128,160},{160,128},{192,224},{224,1... | collective-permute-start | bytes 1376264 | tf_op jit(solution)/shard_map/ppermute | solution.py:83
  (23 other events, 273.3 us)

commit v5 on v4

--- a/solution.py
+++ b/solution.py
@@ -41,13 +41,17 @@
 STEPS = 12
 STRIP = M // 4
 
-LINES = ((0, (0, 1, 2, 3)), (1, (0, 1, 2, 3)), (3, (0, 1, 2, 3)), (2, (0, 1)), (2, (2, 3)))
-PARTS = [
-    (half, [(last, k) if half == 0 else (k, last) for k in shifts], other_core)
-    for other_core in (False, True)
-    for half in (0, 1)
-    for last, shifts in LINES
-]
+ALL_FOUR = (0, 1, 2, 3)
+
+
+def line(half, last, others):
+    return [(half, last, k) if half == 0 else (half, k, last) for k in others]
+
+
+NEAR = [line(half, last, ALL_FOUR) for last in (0, 1, 3) for half in (0, 1)]
+FAR = [line(half, 2, others) for half in (0, 1) for others in ((0, 1), (2, 3))]
+OWN_PARTS = len(NEAR) + len(FAR)
+PARTS = NEAR + FAR + [sum(NEAR[:2], []), sum(NEAR[2:], [])] + FAR
 
 Z_GROUPS = [[x * Z_CHIPS + z for z in range(Z_CHIPS)] for x in range(X_CHIPS)]
 
@@ -163,10 +167,10 @@
     y, core = row // CORES, row % CORES
     x = lax.axis_index("col") // Z_CHIPS
     copies = []
-    for part, (half, shifts, other_core) in zip(parts, PARTS):
-        for k, (y_shift, x_shift) in enumerate(shifts):
-            from_row = lax.rem(y + Y_CHIPS - y_shift, Y_CHIPS) * CORES
-            from_row = from_row + (1 - core if other_core else core)
+    for number, (part, places) in enumerate(zip(parts, PARTS)):
+        from_core = core if number < OWN_PARTS else 1 - core
+        for k, (half, y_shift, x_shift) in enumerate(places):
+            from_row = lax.rem(y + Y_CHIPS - y_shift, Y_CHIPS) * CORES + from_core
             from_x = lax.rem(x + X_CHIPS - x_shift, X_CHIPS)
             start = (from_row * X_CHIPS + from_x) * CHUNK + half * HALF_CHUNK
             copies.append(
@@ -242,13 +246,15 @@
         return 0
 
     lax.fori_loop(0, STEPS, step, 0)
-    out_ref[...] = (UPDATE_SCALE * (total[...] + COEF_QUINTIC * state[...])).astype(jnp.bfloat16)
+    update = (UPDATE_SCALE * (total[...] + COEF_QUINTIC * state[...])).astype(jnp.bfloat16)
+    for r in range(ROWS):
+        out_ref[r] = update[:, r * OWN_ROWS : (r + 1) * OWN_ROWS]
 
 
 def newton_schulz(base, parts):
     return pl.pallas_call(
         newton_schulz_kernel,
-        out_shape=jax.ShapeDtypeStruct((OWN_COLS, M), jnp.bfloat16),
+        out_shape=jax.ShapeDtypeStruct((ROWS, OWN_COLS, OWN_ROWS), jnp.bfloat16),
         in_specs=[pl.BlockSpec(memory_space=pltpu.VMEM)]
         + [pl.BlockSpec(memory_space=pl.ANY)] * len(parts),
         out_specs=pl.BlockSpec(memory_space=pltpu.VMEM),
@@ -258,7 +264,7 @@
             pltpu.VMEM((2, OWN_COLS, M), jnp.bfloat16),
             pltpu.VMEM((OWN_COLS, M), jnp.float32),
             pltpu.VMEM((OWN_COLS, M), jnp.float32),
-            pltpu.SemaphoreType.DMA((sum(len(shifts) for _, shifts, _ in PARTS),)),
+            pltpu.SemaphoreType.DMA((sum(len(places) for places in PARTS),)),
         ],
         compiler_params=pltpu.CompilerParams(vmem_limit_bytes=58 * 2**20),
         name="newton_schulz",
@@ -287,15 +293,15 @@
     second = jnp.stack([second] + [from_y[k] for k in (1, 2, 3)])
     first, second = lax.optimization_barrier((first, second))
     ups, downs = [over_y(first, 1), over_x(second, 1)], [over_y(first, 3), over_x(second, 3)]
-    swapped = [over_cores(first), over_cores(second)]
+    swapped = over_cores(jnp.concatenate([first, second]))
     onward = [up[:2] for up in ups], [down[2:] for down in downs]
     ups, downs, onward, swapped = lax.optimization_barrier((ups, downs, onward, swapped))
-    own_core, other_core = [], []
-    far = [[over(up, 1), over(down, 3)] for over, up, down in zip((over_y, over_x), *onward)]
-    for own, swap, up, down, rest in zip((first, second), swapped, ups, downs, far):
-        own_core += [own, up, down] + rest
-        other_core += [swap] + [over_cores(part) for part in [up, down] + rest]
-    return own_core + other_core
+    far = []
+    for over, up, down in zip((over_y, over_x), *onward):
+        far += [over(up, 1), over(down, 3)]
+    near = over_cores(jnp.concatenate(ups + downs))
+    own_core = [first, second] + ups + downs + far
+    return own_core + [swapped, near] + [over_cores(part) for part in far]
 
 
 def per_device(gradient, momentum):
@@ -308,7 +314,6 @@
     chunks, columns = partial_gram(rows + [over_cores(part) for part in rows])
     parts = gathered(scattered_sum(chunks))
     update = newton_schulz(columns, parts)
-    update = update.reshape(OWN_COLS, ROWS, OWN_ROWS).transpose(1, 0, 2)
     update = lax.all_to_all(update, "row", split_axis=0, concat_axis=0)
     update_matrix = update.reshape(PANEL_COLS, OWN_ROWS).T
     return (update_matrix, buffer)

time: 246 us -> 237 us (0.963)
  starting transfers between devices: 50 us -> 44.7 us
    ppermute x14 -> x10, starting transfers between devices: 24.4 us -> 16.7 us  [over_cores(): return lax.ppermute(value, 'row', pairs)]
    ppermute x10, waiting for transfers between devices: 36.4 us -> 28.8 us  [over_x(): return lax.ppermute(value, 'col', pairs)]
    ppermute x10, waiting for transfers between devices: 30.5 us -> 36.4 us  [over_y(): return lax.ppermute(value, 'row', pairs)]
    ppermute x10, starting transfers between devices: 9.51 us -> 13.7 us  [over_y(): return lax.ppermute(value, 'row', pairs)]
  transfers between devices with their start and end apart: 34 -> 30, of which waited for: 17 -> 17; matrix products, arithmetic and copies ran while one was open for 0% -> 0% of each run, Pallas kernels for 0% -> 0%
where the time goes in v5:
time: 237 us
  waiting for transfers between devices  68.7 us (29%)
  Pallas kernels  67.7 us (29%)
  blocking collectives  48.2 us (20%)
  starting transfers between devices  44.7 us (19%)
  other arithmetic  3.38 us (1%)
  local copies, waits for them, and re-layouts  3.38 us (1%)
    pallas_call x1, Pallas kernels, newton_schulz(): pl.pallas_call(newton_schulz_kernel, out_shape=jax.ShapeDtypeStruct((ROWS...  64.2 us
    all_to_all x2, blocking collectives, over_z(): lax.all_to_all(value, 'col', split_axis=0, concat_axis=0, axis_index_grou...  36.4 us
    ppermute x10, waiting for transfers between devices, over_y(): return lax.ppermute(value, 'row', pairs)  36.4 us
    ppermute x10, waiting for transfers between devices, over_x(): return lax.ppermute(value, 'col', pairs)  28.8 us
    ppermute x10, starting transfers between devices, over_cores(): return lax.ppermute(value, 'row', pairs)  16.7 us
    ppermute x10, starting transfers between devices, over_x(): return lax.ppermute(value, 'col', pairs)  14.3 us
    ppermute x10, starting transfers between devices, over_y(): return lax.ppermute(value, 'row', pairs)  13.7 us
    all_to_all x1, blocking collectives, per_device(): update = lax.all_to_all(update, 'row', split_axis=0, concat_axis=0)  11.8 us
  transfers between devices with their start and end apart: 30, of which 17 were waited for; matrix products, arithmetic and copies ran while one was open for 0% of the time, Pallas kernels for 0%

profile of v5, /device:TPU:1, one launch (start us, length us, event | category | flops | bytes accessed | tf_op | source)
XLA Modules:
  0.0 236.9 jit_solution(17982055936938400165)
XLA Ops:
  0.6 2.2 fusion
  2.8 2.1 collective-permute-start
  4.9 2.6 %collective-permute-start.1 = (bf16[448,384]{1,0:T(8,128)(2,1)S(1)}, bf16[448,384]{1,0:T(8,128)(2,1)S(1)}, u32[]{:S(2)}, u32[]{:S(2)}) collective-permute-start(bf16[448,384]{1,0:T(8,128)(2,1)S(1)} %get-tuple-element.34.refs_0_), channel_id=1, source_target_pairs={{0,128},{32,160},{64,192},{96,224},{128,0},{160,32},{192,64},{224,... | collective-permute-start | bytes 1032200 | tf_op jit(solution)/shard_map/ppermute | solution.py:80
  8.6 1.5 collective-permute-start.3
  10.1 2.0 collective-permute-done.refs_1_
  12.1 3.3 %collective-permute-start.4 = (bf16[448,384]{1,0:T(8,128)(2,1)S(1)}, bf16[448,384]{1,0:T(8,128)(2,1)S(1)}, u32[]{:S(2)}, u32[]{:S(2)}) collective-permute-start(bf16[448,384]{1,0:T(8,128)(2,1)S(1)} %collective-permute-done.refs_1_), channel_id=1, source_target_pairs={{0,32},{32,0},{64,96},{96,64},{128,160},{160,128},{192,224},{224,1... | collective-permute-start | bytes 1032200 | tf_op jit(solution)/shard_map/ppermute | solution.py:87
  15.4 7.0 %collective-permute-done.1.refs_2_ = bf16[448,384]{1,0:T(8,128)(2,1)S(1)} collective-permute-done((bf16[448,384]{1,0:T(8,128)(2,1)S(1)}, bf16[448,384]{1,0:T(8,128)(2,1)S(1)}, u32[]{:S(2)}, u32[]{:S(2)}) %collective-permute-start.1) | collective-permute-done | bytes 344096 | tf_op jit(solution)/shard_map/ppermute | solution.py:80
  22.4 1.5 collective-permute-start.5
  25.7 3.5 %partial_gram.1 = (bf16[896,256]{1,0:T(8,128)(2,1)S(1)}, bf16[896,256]{1,0:T(8,128)(2,1)S(1)}, bf16[896,256]{1,0:T(8,128)(2,1)S(1)}, bf16[896,256]{1,0:T(8,128)(2,1)S(1)}, bf16[48,3584]{1,0:T(8,128)(2,1)S(1)}) custom-call(bf16[448,384]{1,0:T(8,128)(2,1)S(1)} %get-tuple-element.34.refs_0_, bf16[448,384]{1,0:T(8,128)(2,1)S(1)} %collective-permute-done.refs_1_, ...), custom_call_target="tpu_custom_call" | custom-call | tf_op jit(solution)/shard_map/partial_gram/pallas_call | solution.py:142
  29.2 2.5 %collective-permute-start.9 = (bf16[896,256]{1,0:T(8,128)(2,1)S(1)}, bf16[896,256]{1,0:T(8,128)(2,1)S(1)}, u32[]{:S(2)}, u32[]{:S(2)}) collective-permute-start(bf16[896,256]{1,0:T(8,128)(2,1)S(1)} %get-tuple-element.22), channel_id=1, source_target_pairs={{0,24},{1,25},{2,26},{3,27},{4,28},{5,29},{6,30},{7,31},{8,0},{9,1... | collective-permute-start | bytes 1376264 | tf_op jit(solution)/shard_map/ppermute | solution.py:71
  31.8 1.7 collective-permute-start.7
  33.5 17.5 %collective-permute-done.9 = bf16[896,256]{1,0:T(8,128)(2,1)S(1)} collective-permute-done((bf16[896,256]{1,0:T(8,128)(2,1)S(1)}, bf16[896,256]{1,0:T(8,128)(2,1)S(1)}, u32[]{:S(2)}, u32[]{:S(2)}) %collective-permute-start.9) | collective-permute-done | bytes 458784 | tf_op jit(solution)/shard_map/ppermute | solution.py:71
  51.0 2.3 collective-permute-done.7
  53.6 20.6 %all_to_all.15 = bf16[8,112,256]{2,1,0:T(8,128)(2,1)S(1)} all-to-all(bf16[8,112,256]{2,1,0:T(8,128)(2,1)S(1)} %bitcast.15), channel_id=1, replica_groups={{0,1,2,3,4,5,6,7},{8,9,10,11,12,13,14,15},{16,17,18,19,20,21,22,23},{24..., dimensions={0} | all-to-all | bytes 917504 | tf_op jit(solution)/shard_map/all_to_all | solution.py:91
  74.3 15.9 %all_to_all.16 = bf16[8,112,256]{2,1,0:T(8,128)(2,1)S(1)} all-to-all(bf16[8,112,256]{2,1,0:T(8,128)(2,1)S(1)} %broadcast_in_dim.9), channel_id=1, replica_groups={{0,1,2,3,4,5,6,7},{8,9,10,11,12,13,14,15},{16,17,18,19,20,21,22,23},{24..., dimensions={0} | all-to-all | bytes 917504 | tf_op jit(solution)/shard_map/all_to_all | solution.py:91
  90.2 2.3 collective-permute-start.12
  95.8 2.1 collective-permute-done.12
  98.9 2.4 collective-permute-done.10
  101.5 2.8 %collective-permute-done.13 = bf16[448,256]{1,0:T(8,128)(2,1)S(1)} collective-permute-done((bf16[448,256]{1,0:T(8,128)(2,1)S(1)}, bf16[448,256]{1,0:T(8,128)(2,1)S(1)}, u32[]{:S(2)}, u32[]{:S(2)}) %collective-permute-start.13) | collective-permute-done | bytes 229408 | tf_op jit(solution)/shard_map/ppermute | solution.py:80
  104.6 6.3 %collective-permute-start.20 = (bf16[8,448,256]{2,1,0:T(8,128)(2,1)S(1)}, bf16[8,448,256]{2,1,0:T(8,128)(2,1)}, u32[]{:S(2)}, u32[]{:S(2)}) collective-permute-start(bf16[8,448,256]{2,1,0:T(8,128)(2,1)S(1)} %pad_maximum_fusion.1), channel_id=1, source_target_pairs={{0,32},{32,0},{64,96},{96,64},{128,160},{160,128},{192,224},{224,1... | collective-permute-start | bytes 5505032 | tf_op jit(solution)/shard_map/ppermute | solution.py:87
  110.9 1.5 collective-permute-start.17
  112.3 2.7 %collective-permute-start.18 = (bf16[4,448,256]{2,1,0:T(8,128)(2,1)S(1)}, bf16[4,448,256]{2,1,0:T(8,128)(2,1)S(1)}, u32[]{:S(2)}, u32[]{:S(2)}) collective-permute-start(bf16[4,448,256]{2,1,0:T(8,128)(2,1)S(1)} %pad_maximum_fusion.2.refs_0_), channel_id=1, source_target_pairs={{0,192},{32,224},{64,0},{96,32},{128,64},{160,96},{192,128},{224,1... | collective-permute-start | bytes 2752520 | tf_op jit(solution)/shard_map/ppermute | solution.py:80
  115.0 1.9 collective-permute-start.19
  116.9 17.1 %collective-permute-done.16.refs_2_ = bf16[4,448,256]{2,1,0:T(8,128)(2,1)S(1)} collective-permute-done((bf16[4,448,256]{2,1,0:T(8,128)(2,1)S(1)}, bf16[4,448,256]{2,1,0:T(8,128)(2,1)S(1)}, u32[]{:S(2)}, u32[]{:S(2)}) %collective-permute-start.16) | collective-permute-done | bytes 917536 | tf_op jit(solution)/shard_map/ppermute | solution.py:80
  136.9 1.8 collective-permute-start.25
  138.7 2.7 %collective-permute-start.22 = (bf16[2,448,256]{2,1,0:T(8,128)(2,1)S(1)}, bf16[2,448,256]{2,1,0:T(8,128)(2,1)S(1)}, u32[]{:S(2)}, u32[]{:S(2)}) collective-permute-start(bf16[2,448,256]{2,1,0:T(8,128)(2,1)S(1)} %slice.76), channel_id=1, source_target_pairs={{0,192},{32,224},{64,0},{96,32},{128,64},{160,96},{192,128},{224,1... | collective-permute-start | bytes 1376264 | tf_op jit(solution)/shard_map/ppermute | solution.py:80
  142.7 1.8 collective-permute-start.24
  144.5 7.5 %collective-permute-done.21.refs_6_ = bf16[2,448,256]{2,1,0:T(8,128)(2,1)S(1)} collective-permute-done((bf16[2,448,256]{2,1,0:T(8,128)(2,1)S(1)}, bf16[2,448,256]{2,1,0:T(8,128)(2,1)S(1)}, u32[]{:S(2)}, u32[]{:S(2)}) %collective-permute-start.21) | collective-permute-done | bytes 458784 | tf_op jit(solution)/shard_map/ppermute | solution.py:80
  153.0 1.9 collective-permute-done.23.refs_8_
  158.1 1.8 copy-done.7
  160.0 64.2 %newton_schulz.1 = bf16[8,48,448]{2,1,0:T(8,128)(2,1)} custom-call(bf16[48,3584]{1,0:T(8,128)(2,1)} %copy-done, bf16[4,448,256]{2,1,0:T(8,128)(2,1)} %copy-done.1, bf16[4,448,256]{2,1,0:T(8,128)(2,1)} %copy-done.2, bf16[4,448,256]{2,1,0:T(8,128)(2,1)} %copy-done.3, bf16[4,448,256]{2,1,0:T(8,128)(2,1)} %copy-done.4, bf16[4,448,256]{2,1,0:T(8,128)(2,1)} %copy-done.5, ...), custom_call_target="tpu_custom_call" | custom-call | tf_op jit(solution)/shard_map/newton_schulz/pallas_call | solution.py:255
  224.2 11.8 %all_to_all.17 = bf16[8,48,448]{2,1,0:T(8,128)(2,1)S(1)} all-to-all(bf16[8,48,448]{2,1,0:T(8,128)(2,1)} %newton_schulz.1), channel_id=1, replica_groups=mesh['row'=8,'col'=32] {'row'}, dimensions={0} | all-to-all | bytes 688128 | tf_op jit(solution)/shard_map/all_to_all | solution.py:317
  (79 shorter events, 17.2 us)
Async XLA Ops:
  2.8 9.3 %collective-permute-start = (bf16[448,384]{1,0:T(8,128)(2,1)S(1)}, bf16[448,384]{1,0:T(8,128)(2,1)S(1)}, u32[]{:S(2)}, u32[]{:S(2)}) collective-permute-start(bf16[448,384]{1,0:T(8,128)(2,1)S(1)} %get-tuple-element.34.refs_0_), channel_id=1, source_target_pairs={{0,64},{32,96},{64,128},{96,160},{128,192},{160,224},{192,0},{224,... | collective-permute-start | bytes 1032200 | tf_op jit(solution)/shard_map/ppermute | solution.py:80
  4.9 17.5 %collective-permute-start.1 = (bf16[448,384]{1,0:T(8,128)(2,1)S(1)}, bf16[448,384]{1,0:T(8,128)(2,1)S(1)}, u32[]{:S(2)}, u32[]{:S(2)}) collective-permute-start(bf16[448,384]{1,0:T(8,128)(2,1)S(1)} %get-tuple-element.34.refs_0_), channel_id=1, source_target_pairs={{0,128},{32,160},{64,192},{96,224},{128,0},{160,32},{192,64},{224,... | collective-permute-start | bytes 1032200 | tf_op jit(solution)/shard_map/ppermute | solution.py:80
  7.6 16.4 %collective-permute-start.2 = (bf16[448,384]{1,0:T(8,128)(2,1)S(1)}, bf16[448,384]{1,0:T(8,128)(2,1)S(1)}, u32[]{:S(2)}, u32[]{:S(2)}) collective-permute-start(bf16[448,384]{1,0:T(8,128)(2,1)S(1)} %get-tuple-element.34.refs_0_), channel_id=1, source_target_pairs={{0,192},{32,224},{64,0},{96,32},{128,64},{160,96},{192,128},{224,1... | collective-permute-start | bytes 1032200 | tf_op jit(solution)/shard_map/ppermute | solution.py:80
  8.6 15.3 %collective-permute-start.3 = (bf16[448,384]{1,0:T(8,128)(2,1)S(1)}, bf16[448,384]{1,0:T(8,128)(2,1)S(1)}, u32[]{:S(2)}, u32[]{:S(2)}) collective-permute-start(bf16[448,384]{1,0:T(8,128)(2,1)S(1)} %get-tuple-element.34.refs_0_), channel_id=1, source_target_pairs={{0,32},{32,0},{64,96},{96,64},{128,160},{160,128},{192,224},{224,1... | collective-permute-start | bytes 1032200 | tf_op jit(solution)/shard_map/ppermute | solution.py:87
  12.1 11.8 %collective-permute-start.4 = (bf16[448,384]{1,0:T(8,128)(2,1)S(1)}, bf16[448,384]{1,0:T(8,128)(2,1)S(1)}, u32[]{:S(2)}, u32[]{:S(2)}) collective-permute-start(bf16[448,384]{1,0:T(8,128)(2,1)S(1)} %collective-permute-done.refs_1_), channel_id=1, source_target_pairs={{0,32},{32,0},{64,96},{96,64},{128,160},{160,128},{192,224},{224,1... | collective-permute-start | bytes 1032200 | tf_op jit(solution)/shard_map/ppermute | solution.py:87
  22.4 2.8 %collective-permute-start.5 = (bf16[448,384]{1,0:T(8,128)(2,1)S(1)}, bf16[448,384]{1,0:T(8,128)(2,1)S(1)}, u32[]{:S(2)}, u32[]{:S(2)}) collective-permute-start(bf16[448,384]{1,0:T(8,128)(2,1)S(1)} %collective-permute-done.1.refs_2_), channel_id=1, source_target_pairs={{0,32},{32,0},{64,96},{96,64},{128,160},{160,128},{192,224},{224,1... | collective-permute-start | bytes 1032200 | tf_op jit(solution)/shard_map/ppermute | solution.py:87
  23.9 1.8 collective-permute-start.6
  29.2 72.2 %copy-start = (bf16[48,3584]{1,0:T(8,128)(2,1)}, bf16[48,3584]{1,0:T(8,128)(2,1)S(1)}, u32[]{:S(2)}) copy-start(bf16[48,3584]{1,0:T(8,128)(2,1)S(1)} %get-tuple-element.18.base_ref) | copy-start | bytes 1032196
  29.2 21.8 %collective-permute-start.9 = (bf16[896,256]{1,0:T(8,128)(2,1)S(1)}, bf16[896,256]{1,0:T(8,128)(2,1)S(1)}, u32[]{:S(2)}, u32[]{:S(2)}) collective-permute-start(bf16[896,256]{1,0:T(8,128)(2,1)S(1)} %get-tuple-element.22), channel_id=1, source_target_pairs={{0,24},{1,25},{2,26},{3,27},{4,28},{5,29},{6,30},{7,31},{8,0},{9,1... | collective-permute-start | bytes 1376264 | tf_op jit(solution)/shard_map/ppermute | solution.py:71
  31.8 19.2 %collective-permute-start.8 = (bf16[896,256]{1,0:T(8,128)(2,1)S(1)}, bf16[896,256]{1,0:T(8,128)(2,1)S(1)}, u32[]{:S(2)}, u32[]{:S(2)}) collective-permute-start(bf16[896,256]{1,0:T(8,128)(2,1)S(1)} %get-tuple-element.21), channel_id=1, source_target_pairs={{0,8},{1,9},{2,10},{3,11},{4,12},{5,13},{6,14},{7,15},{8,16},{9,17... | collective-permute-start | bytes 1376264 | tf_op jit(solution)/shard_map/ppermute | solution.py:71
  31.8 21.6 %collective-permute-start.7 = (bf16[896,256]{1,0:T(8,128)(2,1)S(1)}, bf16[896,256]{1,0:T(8,128)(2,1)S(1)}, u32[]{:S(2)}, u32[]{:S(2)}) collective-permute-start(bf16[896,256]{1,0:T(8,128)(2,1)S(1)} %get-tuple-element.20), channel_id=1, source_target_pairs={{0,16},{1,17},{2,18},{3,19},{4,20},{5,21},{6,22},{7,23},{8,24},{9,... | collective-permute-start | bytes 1376264 | tf_op jit(solution)/shard_map/ppermute | solution.py:71
  90.2 7.7 %collective-permute-start.12 = (bf16[448,256]{1,0:T(8,128)(2,1)S(1)}, bf16[448,256]{1,0:T(8,128)(2,1)S(1)}, u32[]{:S(2)}, u32[]{:S(2)}) collective-permute-start(bf16[448,256]{1,0:T(8,128)(2,1)S(1)} %bitcast.21), channel_id=1, source_target_pairs={{0,24},{1,25},{2,26},{3,27},{4,28},{5,29},{6,30},{7,31},{8,0},{9,1... | collective-permute-start | bytes 688136 | tf_op jit(solution)/shard_map/ppermute | solution.py:71
  92.5 6.5 %collective-permute-start.11 = (bf16[448,256]{1,0:T(8,128)(2,1)S(1)}, bf16[448,256]{1,0:T(8,128)(2,1)S(1)}, u32[]{:S(2)}, u32[]{:S(2)}) collective-permute-start(bf16[448,256]{1,0:T(8,128)(2,1)S(1)} %bitcast.22), channel_id=1, source_target_pairs={{0,16},{1,17},{2,18},{3,19},{4,20},{5,21},{6,22},{7,23},{8,24},{9,... | collective-permute-start | bytes 688136 | tf_op jit(solution)/shard_map/ppermute | solution.py:71
  92.9 8.4 %collective-permute-start.10 = (bf16[448,256]{1,0:T(8,128)(2,1)S(1)}, bf16[448,256]{1,0:T(8,128)(2,1)S(1)}, u32[]{:S(2)}, u32[]{:S(2)}) collective-permute-start(bf16[448,256]{1,0:T(8,128)(2,1)S(1)} %bitcast.23), channel_id=1, source_target_pairs={{0,8},{1,9},{2,10},{3,11},{4,12},{5,13},{6,14},{7,15},{8,16},{9,17... | collective-permute-start | bytes 688136 | tf_op jit(solution)/shard_map/ppermute | solution.py:71
  93.6 7.8 %collective-permute-start.15 = (bf16[448,256]{1,0:T(8,128)(2,1)S(1)}, bf16[448,256]{1,0:T(8,128)(2,1)S(1)}, u32[]{:S(2)}, u32[]{:S(2)}) collective-permute-start(bf16[448,256]{1,0:T(8,128)(2,1)S(1)} %bitcast.17), channel_id=1, source_target_pairs={{0,192},{32,224},{64,0},{96,32},{128,64},{160,96},{192,128},{224,1... | collective-permute-start | bytes 688136 | tf_op jit(solution)/shard_map/ppermute | solution.py:80
  94.9 6.5 %collective-permute-start.14 = (bf16[448,256]{1,0:T(8,128)(2,1)S(1)}, bf16[448,256]{1,0:T(8,128)(2,1)S(1)}, u32[]{:S(2)}, u32[]{:S(2)}) collective-permute-start(bf16[448,256]{1,0:T(8,128)(2,1)S(1)} %bitcast.18), channel_id=1, source_target_pairs={{0,128},{32,160},{64,192},{96,224},{128,0},{160,32},{192,64},{224,... | collective-permute-start | bytes 688136 | tf_op jit(solution)/shard_map/ppermute | solution.py:80
  97.9 6.4 %collective-permute-start.13 = (bf16[448,256]{1,0:T(8,128)(2,1)S(1)}, bf16[448,256]{1,0:T(8,128)(2,1)S(1)}, u32[]{:S(2)}, u32[]{:S(2)}) collective-permute-start(bf16[448,256]{1,0:T(8,128)(2,1)S(1)} %bitcast.19), channel_id=1, source_target_pairs={{0,64},{32,96},{64,128},{96,160},{128,192},{160,224},{192,0},{224,... | collective-permute-start | bytes 688136 | tf_op jit(solution)/shard_map/ppermute | solution.py:80
  101.4 33.5 %copy-start.1 = (bf16[4,448,256]{2,1,0:T(8,128)(2,1)}, bf16[4,448,256]{2,1,0:T(8,128)(2,1)S(1)}, u32[]{:S(2)}) copy-start(bf16[4,448,256]{2,1,0:T(8,128)(2,1)S(1)} %pad_maximum_fusion.2.refs_0_) | copy-start | bytes 2752516
  104.6 31.5 %collective-permute-start.20 = (bf16[8,448,256]{2,1,0:T(8,128)(2,1)S(1)}, bf16[8,448,256]{2,1,0:T(8,128)(2,1)}, u32[]{:S(2)}, u32[]{:S(2)}) collective-permute-start(bf16[8,448,256]{2,1,0:T(8,128)(2,1)S(1)} %pad_maximum_fusion.1), channel_id=1, source_target_pairs={{0,32},{32,0},{64,96},{96,64},{128,160},{160,128},{192,224},{224,1... | collective-permute-start | bytes 5505032 | tf_op jit(solution)/shard_map/ppermute | solution.py:87
  110.9 23.1 %collective-permute-start.16 = (bf16[4,448,256]{2,1,0:T(8,128)(2,1)S(1)}, bf16[4,448,256]{2,1,0:T(8,128)(2,1)S(1)}, u32[]{:S(2)}, u32[]{:S(2)}) collective-permute-start(bf16[4,448,256]{2,1,0:T(8,128)(2,1)S(1)} %pad_maximum_fusion.2.refs_0_), channel_id=1, source_target_pairs={{0,64},{32,96},{64,128},{96,160},{128,192},{160,224},{192,0},{224,... | collective-permute-start | bytes 2752520 | tf_op jit(solution)/shard_map/ppermute | solution.py:80
  110.9 24.0 %collective-permute-start.17 = (bf16[4,448,256]{2,1,0:T(8,128)(2,1)S(1)}, bf16[4,448,256]{2,1,0:T(8,128)(2,1)S(1)}, u32[]{:S(2)}, u32[]{:S(2)}) collective-permute-start(bf16[4,448,256]{2,1,0:T(8,128)(2,1)S(1)} %pad_maximum_fusion.3.refs_1_), channel_id=1, source_target_pairs={{0,8},{1,9},{2,10},{3,11},{4,12},{5,13},{6,14},{7,15},{8,16},{9,17... | collective-permute-start | bytes 2752520 | tf_op jit(solution)/shard_map/ppermute | solution.py:71
  112.3 22.6 %collective-permute-start.18 = (bf16[4,448,256]{2,1,0:T(8,128)(2,1)S(1)}, bf16[4,448,256]{2,1,0:T(8,128)(2,1)S(1)}, u32[]{:S(2)}, u32[]{:S(2)}) collective-permute-start(bf16[4,448,256]{2,1,0:T(8,128)(2,1)S(1)} %pad_maximum_fusion.2.refs_0_), channel_id=1, source_target_pairs={{0,192},{32,224},{64,0},{96,32},{128,64},{160,96},{192,128},{224,1... | collective-permute-start | bytes 2752520 | tf_op jit(solution)/shard_map/ppermute | solution.py:80
  115.0 21.0 %collective-permute-start.19 = (bf16[4,448,256]{2,1,0:T(8,128)(2,1)S(1)}, bf16[4,448,256]{2,1,0:T(8,128)(2,1)S(1)}, u32[]{:S(2)}, u32[]{:S(2)}) collective-permute-start(bf16[4,448,256]{2,1,0:T(8,128)(2,1)S(1)} %pad_maximum_fusion.3.refs_1_), channel_id=1, source_target_pairs={{0,24},{1,25},{2,26},{3,27},{4,28},{5,29},{6,30},{7,31},{8,0},{9,1... | collective-permute-start | bytes 2752520 | tf_op jit(solution)/shard_map/ppermute | solution.py:71
  136.9 21.2 %collective-permute-start.25 = (bf16[16,448,256]{2,1,0:T(8,128)(2,1)S(1)}, bf16[16,448,256]{2,1,0:T(8,128)(2,1)S(1)}, u32[]{:S(2)}, u32[]{:S(2)}) collective-permute-start(bf16[16,448,256]{2,1,0:T(8,128)(2,1)S(1)} %pad_maximum_fusion), channel_id=1, source_target_pairs={{0,32},{32,0},{64,96},{96,64},{128,160},{160,128},{192,224},{224,1... | collective-permute-start | bytes 11010056 | tf_op jit(solution)/shard_map/ppermute | solution.py:87
  138.7 13.4 %collective-permute-start.21 = (bf16[2,448,256]{2,1,0:T(8,128)(2,1)S(1)}, bf16[2,448,256]{2,1,0:T(8,128)(2,1)S(1)}, u32[]{:S(2)}, u32[]{:S(2)}) collective-permute-start(bf16[2,448,256]{2,1,0:T(8,128)(2,1)S(1)} %slice.74), channel_id=1, source_target_pairs={{0,64},{32,96},{64,128},{96,160},{128,192},{160,224},{192,0},{224,... | collective-permute-start | bytes 1376264 | tf_op jit(solution)/shard_map/ppermute | solution.py:80
  138.7 14.1 %collective-permute-start.22 = (bf16[2,448,256]{2,1,0:T(8,128)(2,1)S(1)}, bf16[2,448,256]{2,1,0:T(8,128)(2,1)S(1)}, u32[]{:S(2)}, u32[]{:S(2)}) collective-permute-start(bf16[2,448,256]{2,1,0:T(8,128)(2,1)S(1)} %slice.76), channel_id=1, source_target_pairs={{0,192},{32,224},{64,0},{96,32},{128,64},{160,96},{192,128},{224,1... | collective-permute-start | bytes 1376264 | tf_op jit(solution)/shard_map/ppermute | solution.py:80
  141.4 13.5 %collective-permute-start.23 = (bf16[2,448,256]{2,1,0:T(8,128)(2,1)S(1)}, bf16[2,448,256]{2,1,0:T(8,128)(2,1)S(1)}, u32[]{:S(2)}, u32[]{:S(2)}) collective-permute-start(bf16[2,448,256]{2,1,0:T(8,128)(2,1)S(1)} %slice.75), channel_id=1, source_target_pairs={{0,8},{1,9},{2,10},{3,11},{4,12},{5,13},{6,14},{7,15},{8,16},{9,17... | collective-permute-start | bytes 1376264 | tf_op jit(solution)/shard_map/ppermute | solution.py:71
  142.7 13.3 %collective-permute-start.24 = (bf16[2,448,256]{2,1,0:T(8,128)(2,1)S(1)}, bf16[2,448,256]{2,1,0:T(8,128)(2,1)S(1)}, u32[]{:S(2)}, u32[]{:S(2)}) collective-permute-start(bf16[2,448,256]{2,1,0:T(8,128)(2,1)S(1)} %slice.77), channel_id=1, source_target_pairs={{0,24},{1,25},{2,26},{3,27},{4,28},{5,29},{6,30},{7,31},{8,0},{9,1... | collective-permute-start | bytes 1376264 | tf_op jit(solution)/shard_map/ppermute | solution.py:71
  152.1 4.3 %collective-permute-start.26 = (bf16[2,448,256]{2,1,0:T(8,128)(2,1)S(1)}, bf16[2,448,256]{2,1,0:T(8,128)(2,1)S(1)}, u32[]{:S(2)}, u32[]{:S(2)}) collective-permute-start(bf16[2,448,256]{2,1,0:T(8,128)(2,1)S(1)} %collective-permute-done.21.refs_6_), channel_id=1, source_target_pairs={{0,32},{32,0},{64,96},{96,64},{128,160},{160,128},{192,224},{224,1... | collective-permute-start | bytes 1376264 | tf_op jit(solution)/shard_map/ppermute | solution.py:87
  152.9 3.5 %collective-permute-start.27 = (bf16[2,448,256]{2,1,0:T(8,128)(2,1)S(1)}, bf16[2,448,256]{2,1,0:T(8,128)(2,1)S(1)}, u32[]{:S(2)}, u32[]{:S(2)}) collective-permute-start(bf16[2,448,256]{2,1,0:T(8,128)(2,1)S(1)} %collective-permute-done.22.refs_7_), channel_id=1, source_target_pairs={{0,32},{32,0},{64,96},{96,64},{128,160},{160,128},{192,224},{224,1... | collective-permute-start | bytes 1376264 | tf_op jit(solution)/shard_map/ppermute | solution.py:87
  154.9 2.5 %collective-permute-start.28 = (bf16[2,448,256]{2,1,0:T(8,128)(2,1)S(1)}, bf16[2,448,256]{2,1,0:T(8,128)(2,1)S(1)}, u32[]{:S(2)}, u32[]{:S(2)}) collective-permute-start(bf16[2,448,256]{2,1,0:T(8,128)(2,1)S(1)} %collective-permute-done.23.refs_8_), channel_id=1, source_target_pairs={{0,32},{32,0},{64,96},{96,64},{128,160},{160,128},{192,224},{224,1... | collective-permute-start | bytes 1376264 | tf_op jit(solution)/shard_map/ppermute | solution.py:87
  156.0 2.1 collective-permute-start.29
  (14 other events, 76.0 us)

commit v6 on v5

--- a/solution.py
+++ b/solution.py
@@ -38,6 +38,9 @@
 HALF_CHUNK = CHUNK // 2
 PIECE = TILE // 2
 CHUNK_PIECES = CHUNK // PIECE
+FIRST_PIECES = 5
+FIRST_SHARE = FIRST_PIECES * PIECE // Z_CHIPS
+OTHER_SHARE = SHARE - FIRST_SHARE
 STEPS = 12
 STRIP = M // 4
 
@@ -95,7 +98,7 @@
 
 def gram_kernel(*refs):
     row_refs, refs = refs[:ROWS], refs[ROWS:]
-    chunk_refs, (columns_ref, panel_ref, sems) = refs[:X_CHIPS], refs[X_CHIPS:]
+    chunk_refs, (others_ref, columns_ref, panel_ref, sems) = refs[:X_CHIPS], refs[X_CHIPS:]
     row = lax.axis_index("row")
     y, core = row // CORES, row % CORES
     copies = []
@@ -129,9 +132,15 @@
             across = j * BLOCK + tile % 2 * TILE
             left = panel_ref[pl.ds(pl.multiple_of(top, PIECE), PIECE), :]
             right = panel_ref[pl.ds(pl.multiple_of(across, TILE), TILE), :]
-            chunk_refs[shift][k * PIECE : (k + 1) * PIECE, :] = dot_nt(left, right).astype(
-                jnp.bfloat16
-            )
+            piece = dot_nt(left, right).astype(jnp.bfloat16)
+            if k < FIRST_PIECES:
+                chunk_refs[shift][k * PIECE : (k + 1) * PIECE, :] = piece
+            else:
+                for part in range(PIECE // OTHER_SHARE):
+                    z = (k - FIRST_PIECES) * (PIECE // OTHER_SHARE) + part
+                    others_ref[z, shift * OTHER_SHARE : (shift + 1) * OTHER_SHARE, :] = piece[
+                        part * OTHER_SHARE : (part + 1) * OTHER_SHARE, :
+                    ]
     for b in range(BLOCKS):
         rows = panel_ref[b * BLOCK : (b + 1) * BLOCK, :]
         columns_ref[:, b * BLOCK : (b + 1) * BLOCK] = dot_nt(pick, rows).astype(jnp.bfloat16)
@@ -141,10 +150,11 @@
     vmem = pl.BlockSpec(memory_space=pltpu.VMEM)
     outs = pl.pallas_call(
         gram_kernel,
-        out_shape=[jax.ShapeDtypeStruct((CHUNK, TILE), jnp.bfloat16)] * X_CHIPS
+        out_shape=[jax.ShapeDtypeStruct((FIRST_PIECES * PIECE, TILE), jnp.bfloat16)] * X_CHIPS
+        + [jax.ShapeDtypeStruct((Z_CHIPS, X_CHIPS * OTHER_SHARE, TILE), jnp.bfloat16)]
         + [jax.ShapeDtypeStruct((OWN_COLS, M), jnp.bfloat16)],
         in_specs=[pl.BlockSpec(memory_space=pl.ANY)] * ROWS,
-        out_specs=[vmem] * (X_CHIPS + 1),
+        out_specs=[vmem] * (X_CHIPS + 2),
         scratch_shapes=[
             pltpu.VMEM((M, PANEL_COLS), jnp.bfloat16),
             pltpu.SemaphoreType.DMA((ROWS,)),
@@ -152,7 +162,7 @@
         compiler_params=pltpu.CompilerParams(vmem_limit_bytes=16 * 2**20),
         name="partial_gram",
     )(*rows)
-    return outs[:X_CHIPS], outs[X_CHIPS]
+    return outs[:X_CHIPS], outs[X_CHIPS], outs[X_CHIPS + 1]
 
 
 def tile_rows(i, d, half, column_half):
@@ -278,14 +288,19 @@
     return total.astype(jnp.bfloat16)
 
 
-def scattered_sum(chunks):
+def scattered_sum(chunks, others):
     received = [chunks[0]] + [over_x(chunks[k], k) for k in (2, 1, 3)]
-    shares = over_z(add_up(received).reshape(Z_CHIPS, SHARE, TILE))
-    return add_up([shares[z] for z in range(Z_CHIPS)])
+    others = over_z(others)
+    others = add_up([others[z] for z in range(Z_CHIPS)]).reshape(X_CHIPS, OTHER_SHARE, TILE)
+    others = [others[0]] + [over_x(others[k], k) for k in (2, 1, 3)]
+    shares = over_z(add_up(received).reshape(Z_CHIPS, FIRST_SHARE, TILE))
+    return jnp.concatenate([add_up([shares[z] for z in range(Z_CHIPS)]), add_up(others)])
 
 
 def gathered(share):
-    chunk = over_z(jnp.broadcast_to(share[None], (Z_CHIPS, SHARE, TILE))).reshape(CHUNK, TILE)
+    chunk = over_z(jnp.broadcast_to(share[None], (Z_CHIPS, SHARE, TILE)))
+    chunk = [chunk[:, :FIRST_SHARE], chunk[:, FIRST_SHARE:]]
+    chunk = jnp.concatenate([part.reshape(-1, TILE) for part in chunk])
     first, second = chunk[:HALF_CHUNK], chunk[HALF_CHUNK:]
     from_x = {k: over_x(first, k) for k in (1, 3, 2)}
     from_y = {k: over_y(second, k) for k in (1, 3, 2)}
@@ -311,8 +326,8 @@
     base = nesterov.astype(jnp.bfloat16)
     shifted = {k: over_y(base, k) for k in (1, 3, 2)}
     rows = [base] + [shifted[k] for k in (1, 2, 3)]
-    chunks, columns = partial_gram(rows + [over_cores(part) for part in rows])
-    parts = gathered(scattered_sum(chunks))
+    chunks, others, columns = partial_gram(rows + [over_cores(part) for part in rows])
+    parts = gathered(scattered_sum(chunks, others))
     update = newton_schulz(columns, parts)
     update = lax.all_to_all(update, "row", split_axis=0, concat_axis=0)
     update_matrix = update.reshape(PANEL_COLS, OWN_ROWS).T

time: 237 us -> 236 us (level)
  blocking collectives: 48.2 us -> 25.7 us
  starting transfers between devices: 44.7 us -> 62.6 us
    all_to_all x2 -> x1, blocking collectives: 36.4 us -> 13.9 us  [over_z(): lax.all_to_all(value, 'col', split_axis=0, concat_axis=0, axis_index_grou...]
    all_to_all x0 -> x2, starting transfers between devices: none -> 14.5 us  [over_z(): lax.all_to_all(value, 'col', split_axis=0, concat_axis=0, axis_index_grou...]
    ppermute x10 -> x13, waiting for transfers between devices: 28.8 us -> 20.3 us  [over_x(): return lax.ppermute(value, 'col', pairs)]
    all_to_all x0 -> x2, waiting for transfers between devices: none -> 7.05 us  [over_z(): lax.all_to_all(value, 'col', split_axis=0, concat_axis=0, axis_index_grou...]
    ppermute x10, waiting for transfers between devices: 36.4 us -> 38.9 us  [over_y(): return lax.ppermute(value, 'row', pairs)]
    ppermute x10 -> x13, starting transfers between devices: 14.3 us -> 16.6 us  [over_x(): return lax.ppermute(value, 'col', pairs)]
  transfers between devices with their start and end apart: 30 -> 35, of which waited for: 17 -> 18; matrix products, arithmetic and copies ran while one was open for 0% -> 1% of each run, Pallas kernels for 0% -> 0%
where the time goes in v6:
time: 236 us; the launch traced here: 235 us
  waiting for transfers between devices  69.9 us (30%)
  Pallas kernels  67.8 us (29%)
  starting transfers between devices  62.6 us (27%)
  blocking collectives  25.7 us (11%)
  other arithmetic  4.17 us (2%)
  local copies, waits for them, and re-layouts  4.13 us (2%)
    pallas_call x1, Pallas kernels, newton_schulz(): pl.pallas_call(newton_schulz_kernel, out_shape=jax.ShapeDtypeStruct((ROWS...  64.2 us
    ppermute x10, waiting for transfers between devices, over_y(): return lax.ppermute(value, 'row', pairs)  38.9 us
    ppermute x13, waiting for transfers between devices, over_x(): return lax.ppermute(value, 'col', pairs)  20.3 us
    ppermute x10, starting transfers between devices, over_cores(): return lax.ppermute(value, 'row', pairs)  17.5 us
    ppermute x13, starting transfers between devices, over_x(): return lax.ppermute(value, 'col', pairs)  16.6 us
    all_to_all x2, starting transfers between devices, over_z(): lax.all_to_all(value, 'col', split_axis=0, concat_axis=0, axis_index_grou...  14.5 us
    all_to_all x1, blocking collectives, over_z(): lax.all_to_all(value, 'col', split_axis=0, concat_axis=0, axis_index_grou...  13.9 us
    ppermute x10, starting transfers between devices, over_y(): return lax.ppermute(value, 'row', pairs)  13.8 us
  transfers between devices with their start and end apart: 35, of which 18 were waited for; matrix products, arithmetic and copies ran while one was open for 1% of the time, Pallas kernels for 0%

profile of v6, /device:TPU:1, one launch (start us, length us, event | category | flops | bytes accessed | tf_op | source)
XLA Modules:
  0.0 235.3 jit_solution(15174092687414561747)
XLA Ops:
  0.6 2.2 fusion
  2.8 2.1 collective-permute-start
  4.9 2.6 %collective-permute-start.1 = (bf16[448,384]{1,0:T(8,128)(2,1)S(1)}, bf16[448,384]{1,0:T(8,128)(2,1)S(1)}, u32[]{:S(2)}, u32[]{:S(2)}) collective-permute-start(bf16[448,384]{1,0:T(8,128)(2,1)S(1)} %get-tuple-element.36.refs_0_), channel_id=1, source_target_pairs={{0,128},{32,160},{64,192},{96,224},{128,0},{160,32},{192,64},{224,... | collective-permute-start | bytes 1032200 | tf_op jit(solution)/shard_map/ppermute | solution.py:83
  8.6 1.5 collective-permute-start.3
  10.1 2.0 collective-permute-done.refs_1_
  12.1 3.3 %collective-permute-start.4 = (bf16[448,384]{1,0:T(8,128)(2,1)S(1)}, bf16[448,384]{1,0:T(8,128)(2,1)S(1)}, u32[]{:S(2)}, u32[]{:S(2)}) collective-permute-start(bf16[448,384]{1,0:T(8,128)(2,1)S(1)} %collective-permute-done.refs_1_), channel_id=1, source_target_pairs={{0,32},{32,0},{64,96},{96,64},{128,160},{160,128},{192,224},{224,1... | collective-permute-start | bytes 1032200 | tf_op jit(solution)/shard_map/ppermute | solution.py:90
  15.4 7.0 %collective-permute-done.1.refs_2_ = bf16[448,384]{1,0:T(8,128)(2,1)S(1)} collective-permute-done((bf16[448,384]{1,0:T(8,128)(2,1)S(1)}, bf16[448,384]{1,0:T(8,128)(2,1)S(1)}, u32[]{:S(2)}, u32[]{:S(2)}) %collective-permute-start.1) | collective-permute-done | bytes 344096 | tf_op jit(solution)/shard_map/ppermute | solution.py:83
  22.4 1.5 collective-permute-start.5
  25.7 3.6 %partial_gram.1 = (bf16[640,256]{1,0:T(8,128)(2,1)S(1)}, bf16[640,256]{1,0:T(8,128)(2,1)S(1)}, bf16[640,256]{1,0:T(8,128)(2,1)S(1)}, bf16[640,256]{1,0:T(8,128)(...) custom-call(bf16[448,384]{1,0:T(8,128)(2,1)S(1)} %get-tuple-element.36.refs_0_, ...), custom_call_target="tpu_custom_call" | custom-call | tf_op jit(solution)/shard_map/partial_gram/pallas_call | solution.py:151
  30.1 8.2 %all-to-all-start.1 = ((bf16[8,128,256]{2,1,0:T(8,128)(2,1)}), bf16[8,128,256]{2,1,0:T(8,128)(2,1)S(1)}, u32[]{:S(2)}, u32[]{:S(2)}) async-start(bf16[8,128,256]{2,1,0:T(8,128)(2,1)} %get-tuple-element.24), calls=%async_computation.1 | async-start | bytes 1048576 | tf_op jit(solution)/shard_map/all_to_all | solution.py:94
  38.3 2.5 %collective-permute-start.9 = (bf16[640,256]{1,0:T(8,128)(2,1)S(1)}, bf16[640,256]{1,0:T(8,128)(2,1)S(1)}, u32[]{:S(2)}, u32[]{:S(2)}) collective-permute-start(bf16[640,256]{1,0:T(8,128)(2,1)S(1)} %get-tuple-element.23), channel_id=1, source_target_pairs={{0,24},{1,25},{2,26},{3,27},{4,28},{5,29},{6,30},{7,31},{8,0},{9,1... | collective-permute-start | bytes 983048 | tf_op jit(solution)/shard_map/ppermute | solution.py:74
  40.7 1.7 collective-permute-start.7
  42.5 5.4 %collective-permute-done.9 = bf16[640,256]{1,0:T(8,128)(2,1)S(1)} collective-permute-done((bf16[640,256]{1,0:T(8,128)(2,1)S(1)}, bf16[640,256]{1,0:T(8,128)(2,1)S(1)}, u32[]{:S(2)}, u32[]{:S(2)}) %collective-permute-start.9) | collective-permute-done | bytes 327712 | tf_op jit(solution)/shard_map/ppermute | solution.py:74
  47.9 3.2 %collective-permute-done.8 = bf16[640,256]{1,0:T(8,128)(2,1)S(1)} collective-permute-done((bf16[640,256]{1,0:T(8,128)(2,1)S(1)}, bf16[640,256]{1,0:T(8,128)(2,1)S(1)}, u32[]{:S(2)}, u32[]{:S(2)}) %collective-permute-start.8) | collective-permute-done | bytes 327712 | tf_op jit(solution)/shard_map/ppermute | solution.py:74
  51.1 5.3 %collective-permute-done.7 = bf16[640,256]{1,0:T(8,128)(2,1)S(1)} collective-permute-done((bf16[640,256]{1,0:T(8,128)(2,1)S(1)}, bf16[640,256]{1,0:T(8,128)(2,1)S(1)}, u32[]{:S(2)}, u32[]{:S(2)}) %collective-permute-start.7) | collective-permute-done | bytes 327712 | tf_op jit(solution)/shard_map/ppermute | solution.py:74
  57.3 6.4 %all-to-all-start = ((bf16[8,80,256]{2,1,0:T(8,128)(2,1)}), bf16[8,80,256]{2,1,0:T(8,128)(2,1)S(1)}, u32[]{:S(2)}, u32[]{:S(2)}) async-start(bf16[8,80,256]{2,1,0:T(8,128)(2,1)} %bitcast), calls=%async_computation | async-start | bytes 655360 | tf_op jit(solution)/shard_map/all_to_all | solution.py:94
  66.7 7.0 %all-to-all-done = bf16[8,80,256]{2,1,0:T(8,128)(2,1)S(1)} async-done(((bf16[8,80,256]{2,1,0:T(8,128)(2,1)}), bf16[8,80,256]{2,1,0:T(8,128)(2,1)S(1)}, u32[]{:S(2)}, u32[]{:S(2)}) %all-to-all-start) | async-done | bytes 327712 | tf_op jit(solution)/shard_map/all_to_all | solution.py:94
  73.9 13.9 %all_to_all.20 = bf16[8,112,256]{2,1,0:T(8,128)(2,1)S(1)} all-to-all(bf16[8,112,256]{2,1,0:T(8,128)(2,1)S(1)} %broadcast_in_dim.2), channel_id=1, replica_groups={{0,1,2,3,4,5,6,7},{8,9,10,11,12,13,14,15},{16,17,18,19,20,21,22,23},{24..., dimensions={0} | all-to-all | bytes 917504 | tf_op jit(solution)/shard_map/all_to_all | solution.py:94
  89.3 1.9 collective-permute-start.14
  95.8 2.4 %collective-permute-done.13 = bf16[448,256]{1,0:T(8,128)(2,1)S(1)} collective-permute-done((bf16[448,256]{1,0:T(8,128)(2,1)S(1)}, bf16[448,256]{1,0:T(8,128)(2,1)S(1)}, u32[]{:S(2)}, u32[]{:S(2)}) %collective-permute-start.13) | collective-permute-done | bytes 229408 | tf_op jit(solution)/shard_map/ppermute | solution.py:74
  99.8 2.6 %collective-permute-done.16 = bf16[448,256]{1,0:T(8,128)(2,1)S(1)} collective-permute-done((bf16[448,256]{1,0:T(8,128)(2,1)S(1)}, bf16[448,256]{1,0:T(8,128)(2,1)S(1)}, u32[]{:S(2)}, u32[]{:S(2)}) %collective-permute-start.16) | collective-permute-done | bytes 229408 | tf_op jit(solution)/shard_map/ppermute | solution.py:83
  102.7 7.0 %collective-permute-start.23 = (bf16[8,448,256]{2,1,0:T(8,128)(2,1)S(1)}, bf16[8,448,256]{2,1,0:T(8,128)(2,1)}, u32[]{:S(2)}, u32[]{:S(2)}) collective-permute-start(bf16[8,448,256]{2,1,0:T(8,128)(2,1)S(1)} %pad_maximum_fusion.1), channel_id=1, source_target_pairs={{0,32},{32,0},{64,96},{96,64},{128,160},{160,128},{192,224},{224,1... | collective-permute-start | bytes 5505032 | tf_op jit(solution)/shard_map/ppermute | solution.py:90
  111.0 2.7 %collective-permute-start.21 = (bf16[4,448,256]{2,1,0:T(8,128)(2,1)S(1)}, bf16[4,448,256]{2,1,0:T(8,128)(2,1)S(1)}, u32[]{:S(2)}, u32[]{:S(2)}) collective-permute-start(bf16[4,448,256]{2,1,0:T(8,128)(2,1)S(1)} %pad_maximum_fusion.2.refs_0_), channel_id=1, source_target_pairs={{0,192},{32,224},{64,0},{96,32},{128,64},{160,96},{192,128},{224,1... | collective-permute-start | bytes 2752520 | tf_op jit(solution)/shard_map/ppermute | solution.py:83
  115.0 17.8 %collective-permute-done.19.refs_2_ = bf16[4,448,256]{2,1,0:T(8,128)(2,1)S(1)} collective-permute-done((bf16[4,448,256]{2,1,0:T(8,128)(2,1)S(1)}, bf16[4,448,256]{2,1,0:T(8,128)(2,1)S(1)}, u32[]{:S(2)}, u32[]{:S(2)}) %collective-permute-start.19) | collective-permute-done | bytes 917536 | tf_op jit(solution)/shard_map/ppermute | solution.py:83
  133.0 1.7 collective-permute-done.22.refs_5_
  135.6 1.8 collective-permute-start.28
  137.4 2.7 %collective-permute-start.25 = (bf16[2,448,256]{2,1,0:T(8,128)(2,1)S(1)}, bf16[2,448,256]{2,1,0:T(8,128)(2,1)S(1)}, u32[]{:S(2)}, u32[]{:S(2)}) collective-permute-start(bf16[2,448,256]{2,1,0:T(8,128)(2,1)S(1)} %slice.145), channel_id=1, source_target_pairs={{0,192},{32,224},{64,0},{96,32},{128,64},{160,96},{192,128},{224,1... | collective-permute-start | bytes 1376264 | tf_op jit(solution)/shard_map/ppermute | solution.py:83
  141.0 1.8 collective-permute-start.27
  142.8 8.0 %collective-permute-done.24.refs_6_ = bf16[2,448,256]{2,1,0:T(8,128)(2,1)S(1)} collective-permute-done((bf16[2,448,256]{2,1,0:T(8,128)(2,1)S(1)}, bf16[2,448,256]{2,1,0:T(8,128)(2,1)S(1)}, u32[]{:S(2)}, u32[]{:S(2)}) %collective-permute-start.24) | collective-permute-done | bytes 458784 | tf_op jit(solution)/shard_map/ppermute | solution.py:83
  156.4 1.8 copy-done.7
  158.3 64.2 %newton_schulz.1 = bf16[8,48,448]{2,1,0:T(8,128)(2,1)} custom-call(bf16[48,3584]{1,0:T(8,128)(2,1)} %copy-done, bf16[4,448,256]{2,1,0:T(8,128)(2,1)} %copy-done.1, bf16[4,448,256]{2,1,0:T(8,128)(2,1)} %copy-done.2, bf16[4,448,256]{2,1,0:T(8,128)(2,1)} %copy-done.3, bf16[4,448,256]{2,1,0:T(8,128)(2,1)} %copy-done.4, bf16[4,448,256]{2,1,0:T(8,128)(2,1)} %copy-done.5, ...), custom_call_target="tpu_custom_call" | custom-call | tf_op jit(solution)/shard_map/newton_schulz/pallas_call | solution.py:265
  222.5 11.8 %all_to_all.21 = bf16[8,48,448]{2,1,0:T(8,128)(2,1)S(1)} all-to-all(bf16[8,48,448]{2,1,0:T(8,128)(2,1)} %newton_schulz.1), channel_id=1, replica_groups=mesh['row'=8,'col'=32] {'row'}, dimensions={0} | all-to-all | bytes 688128 | tf_op jit(solution)/shard_map/all_to_all | solution.py:332
  (94 shorter events, 26.7 us)
Async XLA Ops:
  2.8 9.3 %collective-permute-start = (bf16[448,384]{1,0:T(8,128)(2,1)S(1)}, bf16[448,384]{1,0:T(8,128)(2,1)S(1)}, u32[]{:S(2)}, u32[]{:S(2)}) collective-permute-start(bf16[448,384]{1,0:T(8,128)(2,1)S(1)} %get-tuple-element.36.refs_0_), channel_id=1, source_target_pairs={{0,64},{32,96},{64,128},{96,160},{128,192},{160,224},{192,0},{224,... | collective-permute-start | bytes 1032200 | tf_op jit(solution)/shard_map/ppermute | solution.py:83
  4.9 17.5 %collective-permute-start.1 = (bf16[448,384]{1,0:T(8,128)(2,1)S(1)}, bf16[448,384]{1,0:T(8,128)(2,1)S(1)}, u32[]{:S(2)}, u32[]{:S(2)}) collective-permute-start(bf16[448,384]{1,0:T(8,128)(2,1)S(1)} %get-tuple-element.36.refs_0_), channel_id=1, source_target_pairs={{0,128},{32,160},{64,192},{96,224},{128,0},{160,32},{192,64},{224,... | collective-permute-start | bytes 1032200 | tf_op jit(solution)/shard_map/ppermute | solution.py:83
  7.6 16.4 %collective-permute-start.2 = (bf16[448,384]{1,0:T(8,128)(2,1)S(1)}, bf16[448,384]{1,0:T(8,128)(2,1)S(1)}, u32[]{:S(2)}, u32[]{:S(2)}) collective-permute-start(bf16[448,384]{1,0:T(8,128)(2,1)S(1)} %get-tuple-element.36.refs_0_), channel_id=1, source_target_pairs={{0,192},{32,224},{64,0},{96,32},{128,64},{160,96},{192,128},{224,1... | collective-permute-start | bytes 1032200 | tf_op jit(solution)/shard_map/ppermute | solution.py:83
  8.6 15.3 %collective-permute-start.3 = (bf16[448,384]{1,0:T(8,128)(2,1)S(1)}, bf16[448,384]{1,0:T(8,128)(2,1)S(1)}, u32[]{:S(2)}, u32[]{:S(2)}) collective-permute-start(bf16[448,384]{1,0:T(8,128)(2,1)S(1)} %get-tuple-element.36.refs_0_), channel_id=1, source_target_pairs={{0,32},{32,0},{64,96},{96,64},{128,160},{160,128},{192,224},{224,1... | collective-permute-start | bytes 1032200 | tf_op jit(solution)/shard_map/ppermute | solution.py:90
  12.1 11.8 %collective-permute-start.4 = (bf16[448,384]{1,0:T(8,128)(2,1)S(1)}, bf16[448,384]{1,0:T(8,128)(2,1)S(1)}, u32[]{:S(2)}, u32[]{:S(2)}) collective-permute-start(bf16[448,384]{1,0:T(8,128)(2,1)S(1)} %collective-permute-done.refs_1_), channel_id=1, source_target_pairs={{0,32},{32,0},{64,96},{96,64},{128,160},{160,128},{192,224},{224,1... | collective-permute-start | bytes 1032200 | tf_op jit(solution)/shard_map/ppermute | solution.py:90
  22.4 2.8 %collective-permute-start.5 = (bf16[448,384]{1,0:T(8,128)(2,1)S(1)}, bf16[448,384]{1,0:T(8,128)(2,1)S(1)}, u32[]{:S(2)}, u32[]{:S(2)}) collective-permute-start(bf16[448,384]{1,0:T(8,128)(2,1)S(1)} %collective-permute-done.1.refs_2_), channel_id=1, source_target_pairs={{0,32},{32,0},{64,96},{96,64},{128,160},{160,128},{192,224},{224,1... | collective-permute-start | bytes 1032200 | tf_op jit(solution)/shard_map/ppermute | solution.py:90
  30.1 27.2 %all-to-all-start.1 = ((bf16[8,128,256]{2,1,0:T(8,128)(2,1)}), bf16[8,128,256]{2,1,0:T(8,128)(2,1)S(1)}, u32[]{:S(2)}, u32[]{:S(2)}) async-start(bf16[8,128,256]{2,1,0:T(8,128)(2,1)} %get-tuple-element.24), calls=%async_computation.1 | async-start | bytes 1048576 | tf_op jit(solution)/shard_map/all_to_all | solution.py:94
  38.3 9.7 %collective-permute-start.9 = (bf16[640,256]{1,0:T(8,128)(2,1)S(1)}, bf16[640,256]{1,0:T(8,128)(2,1)S(1)}, u32[]{:S(2)}, u32[]{:S(2)}) collective-permute-start(bf16[640,256]{1,0:T(8,128)(2,1)S(1)} %get-tuple-element.23), channel_id=1, source_target_pairs={{0,24},{1,25},{2,26},{3,27},{4,28},{5,29},{6,30},{7,31},{8,0},{9,1... | collective-permute-start | bytes 983048 | tf_op jit(solution)/shard_map/ppermute | solution.py:74
  40.7 10.4 %collective-permute-start.8 = (bf16[640,256]{1,0:T(8,128)(2,1)S(1)}, bf16[640,256]{1,0:T(8,128)(2,1)S(1)}, u32[]{:S(2)}, u32[]{:S(2)}) collective-permute-start(bf16[640,256]{1,0:T(8,128)(2,1)S(1)} %get-tuple-element.22), channel_id=1, source_target_pairs={{0,8},{1,9},{2,10},{3,11},{4,12},{5,13},{6,14},{7,15},{8,16},{9,17... | collective-permute-start | bytes 983048 | tf_op jit(solution)/shard_map/ppermute | solution.py:74
  40.7 15.6 %collective-permute-start.7 = (bf16[640,256]{1,0:T(8,128)(2,1)S(1)}, bf16[640,256]{1,0:T(8,128)(2,1)S(1)}, u32[]{:S(2)}, u32[]{:S(2)}) collective-permute-start(bf16[640,256]{1,0:T(8,128)(2,1)S(1)} %get-tuple-element.21), channel_id=1, source_target_pairs={{0,16},{1,17},{2,18},{3,19},{4,20},{5,21},{6,22},{7,23},{8,24},{9,... | collective-permute-start | bytes 983048 | tf_op jit(solution)/shard_map/ppermute | solution.py:74
  57.3 16.5 %all-to-all-start = ((bf16[8,80,256]{2,1,0:T(8,128)(2,1)}), bf16[8,80,256]{2,1,0:T(8,128)(2,1)S(1)}, u32[]{:S(2)}, u32[]{:S(2)}) async-start(bf16[8,80,256]{2,1,0:T(8,128)(2,1)} %bitcast), calls=%async_computation | async-start | bytes 655360 | tf_op jit(solution)/shard_map/all_to_all | solution.py:94
  63.7 10.1 %collective-permute-start.12 = (bf16[32,256]{1,0:T(8,128)(2,1)S(1)}, bf16[32,256]{1,0:T(8,128)(2,1)S(1)}, u32[]{:S(2)}, u32[]{:S(2)}) collective-permute-start(bf16[32,256]{1,0:T(8,128)(2,1)S(1)} %get-tuple-element.43), channel_id=1, source_target_pairs={{0,24},{1,25},{2,26},{3,27},{4,28},{5,29},{6,30},{7,31},{8,0},{9,1... | collective-permute-start | bytes 49160 | tf_op jit(solution)/shard_map/ppermute | solution.py:74
  63.8 10.0 %collective-permute-start.11 = (bf16[32,256]{1,0:T(8,128)(2,1)S(1)}, bf16[32,256]{1,0:T(8,128)(2,1)S(1)}, u32[]{:S(2)}, u32[]{:S(2)}) collective-permute-start(bf16[32,256]{1,0:T(8,128)(2,1)S(1)} %get-tuple-element.42), channel_id=1, source_target_pairs={{0,8},{1,9},{2,10},{3,11},{4,12},{5,13},{6,14},{7,15},{8,16},{9,17... | collective-permute-start | bytes 49160 | tf_op jit(solution)/shard_map/ppermute | solution.py:74
  65.3 8.6 %collective-permute-start.10 = (bf16[32,256]{1,0:T(8,128)(2,1)S(1)}, bf16[32,256]{1,0:T(8,128)(2,1)S(1)}, u32[]{:S(2)}, u32[]{:S(2)}) collective-permute-start(bf16[32,256]{1,0:T(8,128)(2,1)S(1)} %get-tuple-element.41), channel_id=1, source_target_pairs={{0,16},{1,17},{2,18},{3,19},{4,20},{5,21},{6,22},{7,23},{8,24},{9,... | collective-permute-start | bytes 49160 | tf_op jit(solution)/shard_map/ppermute | solution.py:74
  87.9 6.3 %collective-permute-start.15 = (bf16[448,256]{1,0:T(8,128)(2,1)S(1)}, bf16[448,256]{1,0:T(8,128)(2,1)S(1)}, u32[]{:S(2)}, u32[]{:S(2)}) collective-permute-start(bf16[448,256]{1,0:T(8,128)(2,1)S(1)} %get-tuple-element.40), channel_id=1, source_target_pairs={{0,24},{1,25},{2,26},{3,27},{4,28},{5,29},{6,30},{7,31},{8,0},{9,1... | collective-permute-start | bytes 688136 | tf_op jit(solution)/shard_map/ppermute | solution.py:74
  89.3 6.5 %collective-permute-start.14 = (bf16[448,256]{1,0:T(8,128)(2,1)S(1)}, bf16[448,256]{1,0:T(8,128)(2,1)S(1)}, u32[]{:S(2)}, u32[]{:S(2)}) collective-permute-start(bf16[448,256]{1,0:T(8,128)(2,1)S(1)} %get-tuple-element.40), channel_id=1, source_target_pairs={{0,16},{1,17},{2,18},{3,19},{4,20},{5,21},{6,22},{7,23},{8,24},{9,... | collective-permute-start | bytes 688136 | tf_op jit(solution)/shard_map/ppermute | solution.py:74
  91.2 6.9 %collective-permute-start.13 = (bf16[448,256]{1,0:T(8,128)(2,1)S(1)}, bf16[448,256]{1,0:T(8,128)(2,1)S(1)}, u32[]{:S(2)}, u32[]{:S(2)}) collective-permute-start(bf16[448,256]{1,0:T(8,128)(2,1)S(1)} %get-tuple-element.40), channel_id=1, source_target_pairs={{0,8},{1,9},{2,10},{3,11},{4,12},{5,13},{6,14},{7,15},{8,16},{9,17... | collective-permute-start | bytes 688136 | tf_op jit(solution)/shard_map/ppermute | solution.py:74
  92.0 6.3 %collective-permute-start.18 = (bf16[448,256]{1,0:T(8,128)(2,1)S(1)}, bf16[448,256]{1,0:T(8,128)(2,1)S(1)}, u32[]{:S(2)}, u32[]{:S(2)}) collective-permute-start(bf16[448,256]{1,0:T(8,128)(2,1)S(1)} %get-tuple-element.38), channel_id=1, source_target_pairs={{0,192},{32,224},{64,0},{96,32},{128,64},{160,96},{192,128},{224,1... | collective-permute-start | bytes 688136 | tf_op jit(solution)/shard_map/ppermute | solution.py:83
  93.3 6.5 %collective-permute-start.17 = (bf16[448,256]{1,0:T(8,128)(2,1)S(1)}, bf16[448,256]{1,0:T(8,128)(2,1)S(1)}, u32[]{:S(2)}, u32[]{:S(2)}) collective-permute-start(bf16[448,256]{1,0:T(8,128)(2,1)S(1)} %get-tuple-element.38), channel_id=1, source_target_pairs={{0,128},{32,160},{64,192},{96,224},{128,0},{160,32},{192,64},{224,... | collective-permute-start | bytes 688136 | tf_op jit(solution)/shard_map/ppermute | solution.py:83
  94.2 8.3 %collective-permute-start.16 = (bf16[448,256]{1,0:T(8,128)(2,1)S(1)}, bf16[448,256]{1,0:T(8,128)(2,1)S(1)}, u32[]{:S(2)}, u32[]{:S(2)}) collective-permute-start(bf16[448,256]{1,0:T(8,128)(2,1)S(1)} %get-tuple-element.38), channel_id=1, source_target_pairs={{0,64},{32,96},{64,128},{96,160},{128,192},{160,224},{192,0},{224,... | collective-permute-start | bytes 688136 | tf_op jit(solution)/shard_map/ppermute | solution.py:83
  102.7 32.0 %collective-permute-start.23 = (bf16[8,448,256]{2,1,0:T(8,128)(2,1)S(1)}, bf16[8,448,256]{2,1,0:T(8,128)(2,1)}, u32[]{:S(2)}, u32[]{:S(2)}) collective-permute-start(bf16[8,448,256]{2,1,0:T(8,128)(2,1)S(1)} %pad_maximum_fusion.1), channel_id=1, source_target_pairs={{0,32},{32,0},{64,96},{96,64},{128,160},{160,128},{192,224},{224,1... | collective-permute-start | bytes 5505032 | tf_op jit(solution)/shard_map/ppermute | solution.py:90
  109.7 23.1 %collective-permute-start.19 = (bf16[4,448,256]{2,1,0:T(8,128)(2,1)S(1)}, bf16[4,448,256]{2,1,0:T(8,128)(2,1)S(1)}, u32[]{:S(2)}, u32[]{:S(2)}) collective-permute-start(bf16[4,448,256]{2,1,0:T(8,128)(2,1)S(1)} %pad_maximum_fusion.2.refs_0_), channel_id=1, source_target_pairs={{0,64},{32,96},{64,128},{96,160},{128,192},{160,224},{192,0},{224,... | collective-permute-start | bytes 2752520 | tf_op jit(solution)/shard_map/ppermute | solution.py:83
  109.7 23.2 %collective-permute-start.20 = (bf16[4,448,256]{2,1,0:T(8,128)(2,1)S(1)}, bf16[4,448,256]{2,1,0:T(8,128)(2,1)S(1)}, u32[]{:S(2)}, u32[]{:S(2)}) collective-permute-start(bf16[4,448,256]{2,1,0:T(8,128)(2,1)S(1)} %pad_maximum_fusion.3.refs_1_), channel_id=1, source_target_pairs={{0,8},{1,9},{2,10},{3,11},{4,12},{5,13},{6,14},{7,15},{8,16},{9,17... | collective-permute-start | bytes 2752520 | tf_op jit(solution)/shard_map/ppermute | solution.py:74
  111.0 21.9 %collective-permute-start.21 = (bf16[4,448,256]{2,1,0:T(8,128)(2,1)S(1)}, bf16[4,448,256]{2,1,0:T(8,128)(2,1)S(1)}, u32[]{:S(2)}, u32[]{:S(2)}) collective-permute-start(bf16[4,448,256]{2,1,0:T(8,128)(2,1)S(1)} %pad_maximum_fusion.2.refs_0_), channel_id=1, source_target_pairs={{0,192},{32,224},{64,0},{96,32},{128,64},{160,96},{192,128},{224,1... | collective-permute-start | bytes 2752520 | tf_op jit(solution)/shard_map/ppermute | solution.py:83
  113.7 20.9 %collective-permute-start.22 = (bf16[4,448,256]{2,1,0:T(8,128)(2,1)S(1)}, bf16[4,448,256]{2,1,0:T(8,128)(2,1)S(1)}, u32[]{:S(2)}, u32[]{:S(2)}) collective-permute-start(bf16[4,448,256]{2,1,0:T(8,128)(2,1)S(1)} %pad_maximum_fusion.3.refs_1_), channel_id=1, source_target_pairs={{0,24},{1,25},{2,26},{3,27},{4,28},{5,29},{6,30},{7,31},{8,0},{9,1... | collective-permute-start | bytes 2752520 | tf_op jit(solution)/shard_map/ppermute | solution.py:74
  135.6 20.8 %collective-permute-start.28 = (bf16[16,448,256]{2,1,0:T(8,128)(2,1)S(1)}, bf16[16,448,256]{2,1,0:T(8,128)(2,1)S(1)}, u32[]{:S(2)}, u32[]{:S(2)}) collective-permute-start(bf16[16,448,256]{2,1,0:T(8,128)(2,1)S(1)} %pad_maximum_fusion), channel_id=1, source_target_pairs={{0,32},{32,0},{64,96},{96,64},{128,160},{160,128},{192,224},{224,1... | collective-permute-start | bytes 11010056 | tf_op jit(solution)/shard_map/ppermute | solution.py:90
  137.4 13.4 %collective-permute-start.24 = (bf16[2,448,256]{2,1,0:T(8,128)(2,1)S(1)}, bf16[2,448,256]{2,1,0:T(8,128)(2,1)S(1)}, u32[]{:S(2)}, u32[]{:S(2)}) collective-permute-start(bf16[2,448,256]{2,1,0:T(8,128)(2,1)S(1)} %slice.143), channel_id=1, source_target_pairs={{0,64},{32,96},{64,128},{96,160},{128,192},{160,224},{192,0},{224,... | collective-permute-start | bytes 1376264 | tf_op jit(solution)/shard_map/ppermute | solution.py:83
  137.4 14.1 %collective-permute-start.25 = (bf16[2,448,256]{2,1,0:T(8,128)(2,1)S(1)}, bf16[2,448,256]{2,1,0:T(8,128)(2,1)S(1)}, u32[]{:S(2)}, u32[]{:S(2)}) collective-permute-start(bf16[2,448,256]{2,1,0:T(8,128)(2,1)S(1)} %slice.145), channel_id=1, source_target_pairs={{0,192},{32,224},{64,0},{96,32},{128,64},{160,96},{192,128},{224,1... | collective-permute-start | bytes 1376264 | tf_op jit(solution)/shard_map/ppermute | solution.py:83
  140.1 12.7 %collective-permute-start.26 = (bf16[2,448,256]{2,1,0:T(8,128)(2,1)S(1)}, bf16[2,448,256]{2,1,0:T(8,128)(2,1)S(1)}, u32[]{:S(2)}, u32[]{:S(2)}) collective-permute-start(bf16[2,448,256]{2,1,0:T(8,128)(2,1)S(1)} %slice.144), channel_id=1, source_target_pairs={{0,8},{1,9},{2,10},{3,11},{4,12},{5,13},{6,14},{7,15},{8,16},{9,17... | collective-permute-start | bytes 1376264 | tf_op jit(solution)/shard_map/ppermute | solution.py:74
  141.0 13.3 %collective-permute-start.27 = (bf16[2,448,256]{2,1,0:T(8,128)(2,1)S(1)}, bf16[2,448,256]{2,1,0:T(8,128)(2,1)S(1)}, u32[]{:S(2)}, u32[]{:S(2)}) collective-permute-start(bf16[2,448,256]{2,1,0:T(8,128)(2,1)S(1)} %slice.146), channel_id=1, source_target_pairs={{0,24},{1,25},{2,26},{3,27},{4,28},{5,29},{6,30},{7,31},{8,0},{9,1... | collective-permute-start | bytes 1376264 | tf_op jit(solution)/shard_map/ppermute | solution.py:74
  150.8 3.6 %collective-permute-start.29 = (bf16[2,448,256]{2,1,0:T(8,128)(2,1)S(1)}, bf16[2,448,256]{2,1,0:T(8,128)(2,1)S(1)}, u32[]{:S(2)}, u32[]{:S(2)}) collective-permute-start(bf16[2,448,256]{2,1,0:T(8,128)(2,1)S(1)} %collective-permute-done.24.refs_6_), channel_id=1, source_target_pairs={{0,32},{32,0},{64,96},{96,64},{128,160},{160,128},{192,224},{224,1... | collective-permute-start | bytes 1376264 | tf_op jit(solution)/shard_map/ppermute | solution.py:90
  152.8 2.9 %collective-permute-start.31 = (bf16[2,448,256]{2,1,0:T(8,128)(2,1)S(1)}, bf16[2,448,256]{2,1,0:T(8,128)(2,1)S(1)}, u32[]{:S(2)}, u32[]{:S(2)}) collective-permute-start(bf16[2,448,256]{2,1,0:T(8,128)(2,1)S(1)} %collective-permute-done.26.refs_8_), channel_id=1, source_target_pairs={{0,32},{32,0},{64,96},{96,64},{128,160},{160,128},{192,224},{224,1... | collective-permute-start | bytes 1376264 | tf_op jit(solution)/shard_map/ppermute | solution.py:90
  (19 other events, 119.6 us)

commit v7 on v6

--- a/solution.py
+++ b/solution.py
@@ -54,7 +54,7 @@
 NEAR = [line(half, last, ALL_FOUR) for last in (0, 1, 3) for half in (0, 1)]
 FAR = [line(half, 2, others) for half in (0, 1) for others in ((0, 1), (2, 3))]
 OWN_PARTS = len(NEAR) + len(FAR)
-PARTS = NEAR + FAR + [sum(NEAR[:2], []), sum(NEAR[2:], [])] + FAR
+PARTS = NEAR + FAR + [sum(NEAR, [])] + FAR
 
 Z_GROUPS = [[x * Z_CHIPS + z for z in range(Z_CHIPS)] for x in range(X_CHIPS)]
 
@@ -236,9 +236,13 @@
         from_state = jnp.where(cubic, 0.0, 1.0)
         for strip in range(M // STRIP):
             cut = pl.ds(strip * STRIP, STRIP)
-            product = square * jnp.dot(
-                value[now], gram[:, cut], preferred_element_type=jnp.float32
-            )
+            upper = jnp.dot(
+                value[now, :, : M // 2], gram[: M // 2, cut], preferred_element_type=jnp.float32
+            )
+            lower = jnp.dot(
+                value[now, :, M // 2 :], gram[M // 2 :, cut], preferred_element_type=jnp.float32
+            )
+            product = square * (upper + lower)
             result = keep * state[:, cut] + add * product
             state[:, cut] = result
             value[1 - now, :, cut] = (from_product * product + from_state * result).astype(
@@ -308,15 +312,15 @@
     second = jnp.stack([second] + [from_y[k] for k in (1, 2, 3)])
     first, second = lax.optimization_barrier((first, second))
     ups, downs = [over_y(first, 1), over_x(second, 1)], [over_y(first, 3), over_x(second, 3)]
-    swapped = over_cores(jnp.concatenate([first, second]))
     onward = [up[:2] for up in ups], [down[2:] for down in downs]
-    ups, downs, onward, swapped = lax.optimization_barrier((ups, downs, onward, swapped))
+    ups, downs, onward = lax.optimization_barrier((ups, downs, onward))
     far = []
     for over, up, down in zip((over_y, over_x), *onward):
         far += [over(up, 1), over(down, 3)]
-    near = over_cores(jnp.concatenate(ups + downs))
+    near = over_cores(jnp.concatenate([first, second] + ups + downs))
+    sent, near = lax.optimization_barrier((far, near))
     own_core = [first, second] + ups + downs + far
-    return own_core + [swapped, near] + [over_cores(part) for part in far]
+    return own_core + [near] + [over_cores(part) for part in sent]
 
 
 def per_device(gradient, momentum):

time: 236 us -> 234 us (level)
  waiting for transfers between devices: 69.9 us -> 76.3 us
  starting transfers between devices: 62.6 us -> 57.4 us
    ppermute x10 -> x9, starting transfers between devices: 17.5 us -> 11.8 us  [over_cores(): return lax.ppermute(value, 'row', pairs)]
    ppermute x10, waiting for transfers between devices: 38.9 us -> 43.1 us  [over_y(): return lax.ppermute(value, 'row', pairs)]
  transfers between devices with their start and end apart: 35 -> 34, of which waited for: 18 -> 18; matrix products, arithmetic and copies ran while one was open for 1% -> 1% of each run, Pallas kernels for 0% -> 0%
where the time goes in v7:
time: 234 us
  waiting for transfers between devices  76.3 us (33%)
  Pallas kernels  65.5 us (28%)
  starting transfers between devices  57.4 us (25%)
  blocking collectives  27.2 us (12%)
  other arithmetic  3.49 us (1%)
  local copies, waits for them, and re-layouts  3.03 us (1%)
    pallas_call x1, Pallas kernels, newton_schulz(): pl.pallas_call(newton_schulz_kernel, out_shape=jax.ShapeDtypeStruct((ROWS...  61.9 us
    ppermute x10, waiting for transfers between devices, over_y(): return lax.ppermute(value, 'row', pairs)  43.1 us
    ppermute x13, waiting for transfers between devices, over_x(): return lax.ppermute(value, 'col', pairs)  21.1 us
    ppermute x13, starting transfers between devices, over_x(): return lax.ppermute(value, 'col', pairs)  18.9 us
    all_to_all x1, blocking collectives, over_z(): lax.all_to_all(value, 'col', split_axis=0, concat_axis=0, axis_index_grou...  15.4 us
    all_to_all x2, starting transfers between devices, over_z(): lax.all_to_all(value, 'col', split_axis=0, concat_axis=0, axis_index_grou...  14.8 us
    ppermute x10, starting transfers between devices, over_y(): return lax.ppermute(value, 'row', pairs)  11.8 us
    all_to_all x1, blocking collectives, per_device(): update = lax.all_to_all(update, 'row', split_axis=0, concat_axis=0)  11.8 us
  transfers between devices with their start and end apart: 34, of which 18 were waited for; matrix products, arithmetic and copies ran while one was open for 1% of the time, Pallas kernels for 0%

profile of v7, /device:TPU:1, one launch (start us, length us, event | category | flops | bytes accessed | tf_op | source)
XLA Modules:
  0.0 233.8 jit_solution(13816561071183760011)
XLA Ops:
  0.6 2.2 fusion
  2.8 3.6 %collective-permute-start.2 = (bf16[448,384]{1,0:T(8,128)(2,1)S(1)}, bf16[448,384]{1,0:T(8,128)(2,1)S(1)}, u32[]{:S(2)}, u32[]{:S(2)}) collective-permute-start(bf16[448,384]{1,0:T(8,128)(2,1)S(1)} %get-tuple-element.44.refs_0_), channel_id=1, source_target_pairs={{0,192},{32,224},{64,0},{96,32},{128,64},{160,96},{192,128},{224,1... | collective-permute-start | bytes 1032200 | tf_op jit(solution)/shard_map/ppermute | solution.py:83
  7.4 1.5 collective-permute-start.3
  8.9 11.4 %collective-permute-done.2.refs_3_ = bf16[448,384]{1,0:T(8,128)(2,1)S(1)} collective-permute-done((bf16[448,384]{1,0:T(8,128)(2,1)S(1)}, bf16[448,384]{1,0:T(8,128)(2,1)S(1)}, u32[]{:S(2)}, u32[]{:S(2)}) %collective-permute-start.2) | collective-permute-done | bytes 344096 | tf_op jit(solution)/shard_map/ppermute | solution.py:83
  20.3 1.7 collective-permute-start.6
  22.0 3.2 %collective-permute-done.refs_1_ = bf16[448,384]{1,0:T(8,128)(2,1)S(1)} collective-permute-done((bf16[448,384]{1,0:T(8,128)(2,1)S(1)}, bf16[448,384]{1,0:T(8,128)(2,1)S(1)}, u32[]{:S(2)}, u32[]{:S(2)}) %collective-permute-start) | collective-permute-done | bytes 344096 | tf_op jit(solution)/shard_map/ppermute | solution.py:83
  25.7 1.3 collective-permute-done.4.refs_5_
  27.0 3.6 %partial_gram.1 = (bf16[640,256]{1,0:T(8,128)(2,1)S(1)}, bf16[640,256]{1,0:T(8,128)(2,1)S(1)}, bf16[640,256]{1,0:T(8,128)(2,1)S(1)}, bf16[640,256]{1,0:T(8,128)(...) custom-call(bf16[448,384]{1,0:T(8,128)(2,1)S(1)} %get-tuple-element.44.refs_0_, ...), custom_call_target="tpu_custom_call" | custom-call | tf_op jit(solution)/shard_map/partial_gram/pallas_call | solution.py:151
  31.4 8.2 %all-to-all-start.1 = ((bf16[8,128,256]{2,1,0:T(8,128)(2,1)}), bf16[8,128,256]{2,1,0:T(8,128)(2,1)S(1)}, u32[]{:S(2)}, u32[]{:S(2)}) async-start(bf16[8,128,256]{2,1,0:T(8,128)(2,1)} %get-tuple-element.28), calls=%async_computation.1 | async-start | bytes 1048576 | tf_op jit(solution)/shard_map/all_to_all | solution.py:94
  39.5 2.7 %collective-permute-start.7 = (bf16[640,256]{1,0:T(8,128)(2,1)S(1)}, bf16[640,256]{1,0:T(8,128)(2,1)S(1)}, u32[]{:S(2)}, u32[]{:S(2)}) collective-permute-start(bf16[640,256]{1,0:T(8,128)(2,1)S(1)} %get-tuple-element.25), channel_id=1, source_target_pairs={{0,16},{1,17},{2,18},{3,19},{4,20},{5,21},{6,22},{7,23},{8,24},{9,... | collective-permute-start | bytes 983048 | tf_op jit(solution)/shard_map/ppermute | solution.py:74
  42.6 2.4 %collective-permute-start.9 = (bf16[640,256]{1,0:T(8,128)(2,1)S(1)}, bf16[640,256]{1,0:T(8,128)(2,1)S(1)}, u32[]{:S(2)}, u32[]{:S(2)}) collective-permute-start(bf16[640,256]{1,0:T(8,128)(2,1)S(1)} %get-tuple-element.27), channel_id=1, source_target_pairs={{0,24},{1,25},{2,26},{3,27},{4,28},{5,29},{6,30},{7,31},{8,0},{9,1... | collective-permute-start | bytes 983048 | tf_op jit(solution)/shard_map/ppermute | solution.py:74
  45.0 4.7 %collective-permute-done.7 = bf16[640,256]{1,0:T(8,128)(2,1)S(1)} collective-permute-done((bf16[640,256]{1,0:T(8,128)(2,1)S(1)}, bf16[640,256]{1,0:T(8,128)(2,1)S(1)}, u32[]{:S(2)}, u32[]{:S(2)}) %collective-permute-start.7) | collective-permute-done | bytes 327712 | tf_op jit(solution)/shard_map/ppermute | solution.py:74
  49.7 8.0 %collective-permute-done.8 = bf16[640,256]{1,0:T(8,128)(2,1)S(1)} collective-permute-done((bf16[640,256]{1,0:T(8,128)(2,1)S(1)}, bf16[640,256]{1,0:T(8,128)(2,1)S(1)}, u32[]{:S(2)}, u32[]{:S(2)}) %collective-permute-start.8) | collective-permute-done | bytes 327712 | tf_op jit(solution)/shard_map/ppermute | solution.py:74
  58.6 6.6 %all-to-all-start = ((bf16[8,80,256]{2,1,0:T(8,128)(2,1)}), bf16[8,80,256]{2,1,0:T(8,128)(2,1)S(1)}, u32[]{:S(2)}, u32[]{:S(2)}) async-start(bf16[8,80,256]{2,1,0:T(8,128)(2,1)} %bitcast), calls=%async_computation | async-start | bytes 655360 | tf_op jit(solution)/shard_map/all_to_all | solution.py:94
  66.4 2.1 collective-permute-start.11
  69.1 8.2 %all-to-all-done = bf16[8,80,256]{2,1,0:T(8,128)(2,1)S(1)} async-done(((bf16[8,80,256]{2,1,0:T(8,128)(2,1)}), bf16[8,80,256]{2,1,0:T(8,128)(2,1)S(1)}, u32[]{:S(2)}, u32[]{:S(2)}) %all-to-all-start) | async-done | bytes 327712 | tf_op jit(solution)/shard_map/all_to_all | solution.py:94
  77.4 15.4 %all_to_all.20 = bf16[8,112,256]{2,1,0:T(8,128)(2,1)S(1)} all-to-all(bf16[8,112,256]{2,1,0:T(8,128)(2,1)S(1)} %broadcast_in_dim.2), channel_id=1, replica_groups={{0,1,2,3,4,5,6,7},{8,9,10,11,12,13,14,15},{16,17,18,19,20,21,22,23},{24..., dimensions={0} | all-to-all | bytes 917504 | tf_op jit(solution)/shard_map/all_to_all | solution.py:94
  93.4 5.1 %collective-permute-start.13 = (bf16[448,256]{1,0:T(8,128)(2,1)S(1)}, bf16[448,256]{1,0:T(8,128)(2,1)S(1)}, u32[]{:S(2)}, u32[]{:S(2)}) collective-permute-start(bf16[448,256]{1,0:T(8,128)(2,1)S(1)} %get-tuple-element.48), channel_id=1, source_target_pairs={{0,8},{1,9},{2,10},{3,11},{4,12},{5,13},{6,14},{7,15},{8,16},{9,17... | collective-permute-start | bytes 688136 | tf_op jit(solution)/shard_map/ppermute | solution.py:74
  99.8 1.7 collective-permute-start.18
  101.5 2.4 %collective-permute-done.13 = bf16[448,256]{1,0:T(8,128)(2,1)S(1)} collective-permute-done((bf16[448,256]{1,0:T(8,128)(2,1)S(1)}, bf16[448,256]{1,0:T(8,128)(2,1)S(1)}, u32[]{:S(2)}, u32[]{:S(2)}) %collective-permute-start.13) | collective-permute-done | bytes 229408 | tf_op jit(solution)/shard_map/ppermute | solution.py:74
  103.9 3.3 %collective-permute-done.15 = bf16[448,256]{1,0:T(8,128)(2,1)S(1)} collective-permute-done((bf16[448,256]{1,0:T(8,128)(2,1)S(1)}, bf16[448,256]{1,0:T(8,128)(2,1)S(1)}, u32[]{:S(2)}, u32[]{:S(2)}) %collective-permute-start.15) | collective-permute-done | bytes 229408 | tf_op jit(solution)/shard_map/ppermute | solution.py:74
  107.4 3.5 %collective-permute-done.16 = bf16[448,256]{1,0:T(8,128)(2,1)S(1)} collective-permute-done((bf16[448,256]{1,0:T(8,128)(2,1)S(1)}, bf16[448,256]{1,0:T(8,128)(2,1)S(1)}, u32[]{:S(2)}, u32[]{:S(2)}) %collective-permute-start.16) | collective-permute-done | bytes 229408 | tf_op jit(solution)/shard_map/ppermute | solution.py:83
  111.2 1.5 collective-permute-start.19
  114.2 16.8 %collective-permute-done.21.refs_4_ = bf16[4,448,256]{2,1,0:T(8,128)(2,1)S(1)} collective-permute-done((bf16[4,448,256]{2,1,0:T(8,128)(2,1)S(1)}, bf16[4,448,256]{2,1,0:T(8,128)(2,1)S(1)}, u32[]{:S(2)}, u32[]{:S(2)}) %collective-permute-start.21) | collective-permute-done | bytes 917536 | tf_op jit(solution)/shard_map/ppermute | solution.py:83
  132.3 5.7 %collective-permute-start.27 = (bf16[24,448,256]{2,1,0:T(8,128)(2,1)S(1)}, bf16[24,448,256]{2,1,0:T(8,128)(2,1)}, u32[]{:S(2)}, u32[]{:S(2)}) collective-permute-start(bf16[24,448,256]{2,1,0:T(8,128)(2,1)S(1)} %constant_dynamic-update-slice_fusion), channel_id=1, source_target_pairs={{0,32},{32,0},{64,96},{96,64},{128,160},{160,128},{192,224},{224,1... | collective-permute-start | bytes 16515080 | tf_op jit(solution)/shard_map/ppermute | solution.py:90
  138.0 2.7 %collective-permute-start.24 = (bf16[2,448,256]{2,1,0:T(8,128)(2,1)S(1)}, bf16[2,448,256]{2,1,0:T(8,128)(2,1)S(1)}, u32[]{:S(2)}, u32[]{:S(2)}) collective-permute-start(bf16[2,448,256]{2,1,0:T(8,128)(2,1)S(1)} %slice.145), channel_id=1, source_target_pairs={{0,192},{32,224},{64,0},{96,32},{128,64},{160,96},{192,128},{224,1... | collective-permute-start | bytes 1376264 | tf_op jit(solution)/shard_map/ppermute | solution.py:83
  140.7 2.7 %collective-permute-start.26 = (bf16[2,448,256]{2,1,0:T(8,128)(2,1)S(1)}, bf16[2,448,256]{2,1,0:T(8,128)(2,1)S(1)}, u32[]{:S(2)}, u32[]{:S(2)}) collective-permute-start(bf16[2,448,256]{2,1,0:T(8,128)(2,1)S(1)} %slice.146), channel_id=1, source_target_pairs={{0,24},{1,25},{2,26},{3,27},{4,28},{5,29},{6,30},{7,31},{8,0},{9,1... | collective-permute-start | bytes 1376264 | tf_op jit(solution)/shard_map/ppermute | solution.py:74
  143.4 7.9 %collective-permute-done.23.refs_6_ = bf16[2,448,256]{2,1,0:T(8,128)(2,1)S(1)} collective-permute-done((bf16[2,448,256]{2,1,0:T(8,128)(2,1)S(1)}, bf16[2,448,256]{2,1,0:T(8,128)(2,1)S(1)}, u32[]{:S(2)}, u32[]{:S(2)}) %collective-permute-start.23) | collective-permute-done | bytes 458784 | tf_op jit(solution)/shard_map/ppermute | solution.py:83
  151.3 2.0 collective-permute-done.25.refs_8_
  153.4 1.6 collective-permute-start.28
  159.2 61.9 %newton_schulz.1 = bf16[8,48,448]{2,1,0:T(8,128)(2,1)} custom-call(bf16[48,3584]{1,0:T(8,128)(2,1)} %copy-done, bf16[4,448,256]{2,1,0:T(8,128)(2,1)} %copy-done.1, bf16[4,448,256]{2,1,0:T(8,128)(2,1)} %copy-done.2, bf16[4,448,256]{2,1,0:T(8,128)(2,1)} %copy-done.4, bf16[4,448,256]{2,1,0:T(8,128)(2,1)} %copy-done.6, bf16[4,448,256]{2,1,0:T(8,128)(2,1)} %copy-done.3, ...), custom_call_target="tpu_custom_call" | custom-call | tf_op jit(solution)/shard_map/newton_schulz/pallas_call | solution.py:269
  221.1 11.8 %all_to_all.21 = bf16[8,48,448]{2,1,0:T(8,128)(2,1)S(1)} all-to-all(bf16[8,48,448]{2,1,0:T(8,128)(2,1)} %newton_schulz.1), channel_id=1, replica_groups=mesh['row'=8,'col'=32] {'row'}, dimensions={0} | all-to-all | bytes 688128 | tf_op jit(solution)/shard_map/all_to_all | solution.py:336
  (94 shorter events, 15.4 us)
Async XLA Ops:
  2.8 17.5 %collective-permute-start.2 = (bf16[448,384]{1,0:T(8,128)(2,1)S(1)}, bf16[448,384]{1,0:T(8,128)(2,1)S(1)}, u32[]{:S(2)}, u32[]{:S(2)}) collective-permute-start(bf16[448,384]{1,0:T(8,128)(2,1)S(1)} %get-tuple-element.44.refs_0_), channel_id=1, source_target_pairs={{0,192},{32,224},{64,0},{96,32},{128,64},{160,96},{192,128},{224,1... | collective-permute-start | bytes 1032200 | tf_op jit(solution)/shard_map/ppermute | solution.py:83
  6.4 15.7 %collective-permute-start.1 = (bf16[448,384]{1,0:T(8,128)(2,1)S(1)}, bf16[448,384]{1,0:T(8,128)(2,1)S(1)}, u32[]{:S(2)}, u32[]{:S(2)}) collective-permute-start(bf16[448,384]{1,0:T(8,128)(2,1)S(1)} %get-tuple-element.44.refs_0_), channel_id=1, source_target_pairs={{0,128},{32,160},{64,192},{96,224},{128,0},{160,32},{192,64},{224,... | collective-permute-start | bytes 1032200 | tf_op jit(solution)/shard_map/ppermute | solution.py:83
  6.7 18.5 %collective-permute-start = (bf16[448,384]{1,0:T(8,128)(2,1)S(1)}, bf16[448,384]{1,0:T(8,128)(2,1)S(1)}, u32[]{:S(2)}, u32[]{:S(2)}) collective-permute-start(bf16[448,384]{1,0:T(8,128)(2,1)S(1)} %get-tuple-element.44.refs_0_), channel_id=1, source_target_pairs={{0,64},{32,96},{64,128},{96,160},{128,192},{160,224},{192,0},{224,... | collective-permute-start | bytes 1032200 | tf_op jit(solution)/shard_map/ppermute | solution.py:83
  7.4 18.3 %collective-permute-start.3 = (bf16[448,384]{1,0:T(8,128)(2,1)S(1)}, bf16[448,384]{1,0:T(8,128)(2,1)S(1)}, u32[]{:S(2)}, u32[]{:S(2)}) collective-permute-start(bf16[448,384]{1,0:T(8,128)(2,1)S(1)} %get-tuple-element.44.refs_0_), channel_id=1, source_target_pairs={{0,32},{32,0},{64,96},{96,64},{128,160},{160,128},{192,224},{224,1... | collective-permute-start | bytes 1032200 | tf_op jit(solution)/shard_map/ppermute | solution.py:90
  20.3 5.4 %collective-permute-start.6 = (bf16[448,384]{1,0:T(8,128)(2,1)S(1)}, bf16[448,384]{1,0:T(8,128)(2,1)S(1)}, u32[]{:S(2)}, u32[]{:S(2)}) collective-permute-start(bf16[448,384]{1,0:T(8,128)(2,1)S(1)} %collective-permute-done.2.refs_3_), channel_id=1, source_target_pairs={{0,32},{32,0},{64,96},{96,64},{128,160},{160,128},{192,224},{224,1... | collective-permute-start | bytes 1032200 | tf_op jit(solution)/shard_map/ppermute | solution.py:90
  22.0 3.7 %collective-permute-start.5 = (bf16[448,384]{1,0:T(8,128)(2,1)S(1)}, bf16[448,384]{1,0:T(8,128)(2,1)S(1)}, u32[]{:S(2)}, u32[]{:S(2)}) collective-permute-start(bf16[448,384]{1,0:T(8,128)(2,1)S(1)} %collective-permute-done.1.refs_2_), channel_id=1, source_target_pairs={{0,32},{32,0},{64,96},{96,64},{128,160},{160,128},{192,224},{224,1... | collective-permute-start | bytes 1032200 | tf_op jit(solution)/shard_map/ppermute | solution.py:90
  31.4 27.2 %all-to-all-start.1 = ((bf16[8,128,256]{2,1,0:T(8,128)(2,1)}), bf16[8,128,256]{2,1,0:T(8,128)(2,1)S(1)}, u32[]{:S(2)}, u32[]{:S(2)}) async-start(bf16[8,128,256]{2,1,0:T(8,128)(2,1)} %get-tuple-element.28), calls=%async_computation.1 | async-start | bytes 1048576 | tf_op jit(solution)/shard_map/all_to_all | solution.py:94
  39.5 10.1 %collective-permute-start.7 = (bf16[640,256]{1,0:T(8,128)(2,1)S(1)}, bf16[640,256]{1,0:T(8,128)(2,1)S(1)}, u32[]{:S(2)}, u32[]{:S(2)}) collective-permute-start(bf16[640,256]{1,0:T(8,128)(2,1)S(1)} %get-tuple-element.25), channel_id=1, source_target_pairs={{0,16},{1,17},{2,18},{3,19},{4,20},{5,21},{6,22},{7,23},{8,24},{9,... | collective-permute-start | bytes 983048 | tf_op jit(solution)/shard_map/ppermute | solution.py:74
  42.3 15.4 %collective-permute-start.8 = (bf16[640,256]{1,0:T(8,128)(2,1)S(1)}, bf16[640,256]{1,0:T(8,128)(2,1)S(1)}, u32[]{:S(2)}, u32[]{:S(2)}) collective-permute-start(bf16[640,256]{1,0:T(8,128)(2,1)S(1)} %get-tuple-element.26), channel_id=1, source_target_pairs={{0,8},{1,9},{2,10},{3,11},{4,12},{5,13},{6,14},{7,15},{8,16},{9,17... | collective-permute-start | bytes 983048 | tf_op jit(solution)/shard_map/ppermute | solution.py:74
  42.6 15.1 %collective-permute-start.9 = (bf16[640,256]{1,0:T(8,128)(2,1)S(1)}, bf16[640,256]{1,0:T(8,128)(2,1)S(1)}, u32[]{:S(2)}, u32[]{:S(2)}) collective-permute-start(bf16[640,256]{1,0:T(8,128)(2,1)S(1)} %get-tuple-element.27), channel_id=1, source_target_pairs={{0,24},{1,25},{2,26},{3,27},{4,28},{5,29},{6,30},{7,31},{8,0},{9,1... | collective-permute-start | bytes 983048 | tf_op jit(solution)/shard_map/ppermute | solution.py:74
  58.6 18.7 %all-to-all-start = ((bf16[8,80,256]{2,1,0:T(8,128)(2,1)}), bf16[8,80,256]{2,1,0:T(8,128)(2,1)S(1)}, u32[]{:S(2)}, u32[]{:S(2)}) async-start(bf16[8,80,256]{2,1,0:T(8,128)(2,1)} %bitcast), calls=%async_computation | async-start | bytes 655360 | tf_op jit(solution)/shard_map/all_to_all | solution.py:94
  65.3 12.0 %collective-permute-start.10 = (bf16[32,256]{1,0:T(8,128)(2,1)S(1)}, bf16[32,256]{1,0:T(8,128)(2,1)S(1)}, u32[]{:S(2)}, u32[]{:S(2)}) collective-permute-start(bf16[32,256]{1,0:T(8,128)(2,1)S(1)} %get-tuple-element.49), channel_id=1, source_target_pairs={{0,16},{1,17},{2,18},{3,19},{4,20},{5,21},{6,22},{7,23},{8,24},{9,... | collective-permute-start | bytes 49160 | tf_op jit(solution)/shard_map/ppermute | solution.py:74
  66.4 11.0 %collective-permute-start.11 = (bf16[32,256]{1,0:T(8,128)(2,1)S(1)}, bf16[32,256]{1,0:T(8,128)(2,1)S(1)}, u32[]{:S(2)}, u32[]{:S(2)}) collective-permute-start(bf16[32,256]{1,0:T(8,128)(2,1)S(1)} %get-tuple-element.50), channel_id=1, source_target_pairs={{0,8},{1,9},{2,10},{3,11},{4,12},{5,13},{6,14},{7,15},{8,16},{9,17... | collective-permute-start | bytes 49160 | tf_op jit(solution)/shard_map/ppermute | solution.py:74
  68.5 8.9 %collective-permute-start.12 = (bf16[32,256]{1,0:T(8,128)(2,1)S(1)}, bf16[32,256]{1,0:T(8,128)(2,1)S(1)}, u32[]{:S(2)}, u32[]{:S(2)}) collective-permute-start(bf16[32,256]{1,0:T(8,128)(2,1)S(1)} %get-tuple-element.51), channel_id=1, source_target_pairs={{0,24},{1,25},{2,26},{3,27},{4,28},{5,29},{6,30},{7,31},{8,0},{9,1... | collective-permute-start | bytes 49160 | tf_op jit(solution)/shard_map/ppermute | solution.py:74
  92.9 6.9 %collective-permute-start.14 = (bf16[448,256]{1,0:T(8,128)(2,1)S(1)}, bf16[448,256]{1,0:T(8,128)(2,1)S(1)}, u32[]{:S(2)}, u32[]{:S(2)}) collective-permute-start(bf16[448,256]{1,0:T(8,128)(2,1)S(1)} %get-tuple-element.48), channel_id=1, source_target_pairs={{0,16},{1,17},{2,18},{3,19},{4,20},{5,21},{6,22},{7,23},{8,24},{9,... | collective-permute-start | bytes 688136 | tf_op jit(solution)/shard_map/ppermute | solution.py:74
  93.4 10.5 %collective-permute-start.13 = (bf16[448,256]{1,0:T(8,128)(2,1)S(1)}, bf16[448,256]{1,0:T(8,128)(2,1)S(1)}, u32[]{:S(2)}, u32[]{:S(2)}) collective-permute-start(bf16[448,256]{1,0:T(8,128)(2,1)S(1)} %get-tuple-element.48), channel_id=1, source_target_pairs={{0,8},{1,9},{2,10},{3,11},{4,12},{5,13},{6,14},{7,15},{8,16},{9,17... | collective-permute-start | bytes 688136 | tf_op jit(solution)/shard_map/ppermute | solution.py:74
  98.5 8.8 %collective-permute-start.15 = (bf16[448,256]{1,0:T(8,128)(2,1)S(1)}, bf16[448,256]{1,0:T(8,128)(2,1)S(1)}, u32[]{:S(2)}, u32[]{:S(2)}) collective-permute-start(bf16[448,256]{1,0:T(8,128)(2,1)S(1)} %get-tuple-element.48), channel_id=1, source_target_pairs={{0,24},{1,25},{2,26},{3,27},{4,28},{5,29},{6,30},{7,31},{8,0},{9,1... | collective-permute-start | bytes 688136 | tf_op jit(solution)/shard_map/ppermute | solution.py:74
  98.5 8.9 %collective-permute-start.17 = (bf16[448,256]{1,0:T(8,128)(2,1)S(1)}, bf16[448,256]{1,0:T(8,128)(2,1)S(1)}, u32[]{:S(2)}, u32[]{:S(2)}) collective-permute-start(bf16[448,256]{1,0:T(8,128)(2,1)S(1)} %get-tuple-element.46), channel_id=1, source_target_pairs={{0,128},{32,160},{64,192},{96,224},{128,0},{160,32},{192,64},{224,... | collective-permute-start | bytes 688136 | tf_op jit(solution)/shard_map/ppermute | solution.py:83
  98.9 12.1 %collective-permute-start.16 = (bf16[448,256]{1,0:T(8,128)(2,1)S(1)}, bf16[448,256]{1,0:T(8,128)(2,1)S(1)}, u32[]{:S(2)}, u32[]{:S(2)}) collective-permute-start(bf16[448,256]{1,0:T(8,128)(2,1)S(1)} %get-tuple-element.46), channel_id=1, source_target_pairs={{0,64},{32,96},{64,128},{96,160},{128,192},{160,224},{192,0},{224,... | collective-permute-start | bytes 688136 | tf_op jit(solution)/shard_map/ppermute | solution.py:83
  99.8 11.2 %collective-permute-start.18 = (bf16[448,256]{1,0:T(8,128)(2,1)S(1)}, bf16[448,256]{1,0:T(8,128)(2,1)S(1)}, u32[]{:S(2)}, u32[]{:S(2)}) collective-permute-start(bf16[448,256]{1,0:T(8,128)(2,1)S(1)} %get-tuple-element.46), channel_id=1, source_target_pairs={{0,192},{32,224},{64,0},{96,32},{128,64},{160,96},{192,128},{224,1... | collective-permute-start | bytes 688136 | tf_op jit(solution)/shard_map/ppermute | solution.py:83
  111.1 19.9 %collective-permute-start.21 = (bf16[4,448,256]{2,1,0:T(8,128)(2,1)S(1)}, bf16[4,448,256]{2,1,0:T(8,128)(2,1)S(1)}, u32[]{:S(2)}, u32[]{:S(2)}) collective-permute-start(bf16[4,448,256]{2,1,0:T(8,128)(2,1)S(1)} %pad_maximum_fusion.refs_0_), channel_id=1, source_target_pairs={{0,192},{32,224},{64,0},{96,32},{128,64},{160,96},{192,128},{224,1... | collective-permute-start | bytes 2752520 | tf_op jit(solution)/shard_map/ppermute | solution.py:83
  111.2 20.1 %collective-permute-start.19 = (bf16[4,448,256]{2,1,0:T(8,128)(2,1)S(1)}, bf16[4,448,256]{2,1,0:T(8,128)(2,1)S(1)}, u32[]{:S(2)}, u32[]{:S(2)}) collective-permute-start(bf16[4,448,256]{2,1,0:T(8,128)(2,1)S(1)} %pad_maximum_fusion.refs_0_), channel_id=1, source_target_pairs={{0,64},{32,96},{64,128},{96,160},{128,192},{160,224},{192,0},{224,... | collective-permute-start | bytes 2752520 | tf_op jit(solution)/shard_map/ppermute | solution.py:83
  112.6 19.3 %collective-permute-start.22 = (bf16[4,448,256]{2,1,0:T(8,128)(2,1)S(1)}, bf16[4,448,256]{2,1,0:T(8,128)(2,1)S(1)}, u32[]{:S(2)}, u32[]{:S(2)}) collective-permute-start(bf16[4,448,256]{2,1,0:T(8,128)(2,1)S(1)} %pad_maximum_fusion.1.refs_1_), channel_id=1, source_target_pairs={{0,24},{1,25},{2,26},{3,27},{4,28},{5,29},{6,30},{7,31},{8,0},{9,1... | collective-permute-start | bytes 2752520 | tf_op jit(solution)/shard_map/ppermute | solution.py:74
  113.6 18.4 %collective-permute-start.20 = (bf16[4,448,256]{2,1,0:T(8,128)(2,1)S(1)}, bf16[4,448,256]{2,1,0:T(8,128)(2,1)S(1)}, u32[]{:S(2)}, u32[]{:S(2)}) collective-permute-start(bf16[4,448,256]{2,1,0:T(8,128)(2,1)S(1)} %pad_maximum_fusion.1.refs_1_), channel_id=1, source_target_pairs={{0,8},{1,9},{2,10},{3,11},{4,12},{5,13},{6,14},{7,15},{8,16},{9,17... | collective-permute-start | bytes 2752520 | tf_op jit(solution)/shard_map/ppermute | solution.py:74
  132.3 21.0 %collective-permute-start.27 = (bf16[24,448,256]{2,1,0:T(8,128)(2,1)S(1)}, bf16[24,448,256]{2,1,0:T(8,128)(2,1)}, u32[]{:S(2)}, u32[]{:S(2)}) collective-permute-start(bf16[24,448,256]{2,1,0:T(8,128)(2,1)S(1)} %constant_dynamic-update-slice_fusion), channel_id=1, source_target_pairs={{0,32},{32,0},{64,96},{96,64},{128,160},{160,128},{192,224},{224,1... | collective-permute-start | bytes 16515080 | tf_op jit(solution)/shard_map/ppermute | solution.py:90
  138.0 13.3 %collective-permute-start.23 = (bf16[2,448,256]{2,1,0:T(8,128)(2,1)S(1)}, bf16[2,448,256]{2,1,0:T(8,128)(2,1)S(1)}, u32[]{:S(2)}, u32[]{:S(2)}) collective-permute-start(bf16[2,448,256]{2,1,0:T(8,128)(2,1)S(1)} %slice.143), channel_id=1, source_target_pairs={{0,64},{32,96},{64,128},{96,160},{128,192},{160,224},{192,0},{224,... | collective-permute-start | bytes 1376264 | tf_op jit(solution)/shard_map/ppermute | solution.py:83
  138.0 13.3 %collective-permute-start.24 = (bf16[2,448,256]{2,1,0:T(8,128)(2,1)S(1)}, bf16[2,448,256]{2,1,0:T(8,128)(2,1)S(1)}, u32[]{:S(2)}, u32[]{:S(2)}) collective-permute-start(bf16[2,448,256]{2,1,0:T(8,128)(2,1)S(1)} %slice.145), channel_id=1, source_target_pairs={{0,192},{32,224},{64,0},{96,32},{128,64},{160,96},{192,128},{224,1... | collective-permute-start | bytes 1376264 | tf_op jit(solution)/shard_map/ppermute | solution.py:83
  140.7 12.6 %collective-permute-start.25 = (bf16[2,448,256]{2,1,0:T(8,128)(2,1)S(1)}, bf16[2,448,256]{2,1,0:T(8,128)(2,1)S(1)}, u32[]{:S(2)}, u32[]{:S(2)}) collective-permute-start(bf16[2,448,256]{2,1,0:T(8,128)(2,1)S(1)} %slice.144), channel_id=1, source_target_pairs={{0,8},{1,9},{2,10},{3,11},{4,12},{5,13},{6,14},{7,15},{8,16},{9,17... | collective-permute-start | bytes 1376264 | tf_op jit(solution)/shard_map/ppermute | solution.py:74
  140.7 12.6 %collective-permute-start.26 = (bf16[2,448,256]{2,1,0:T(8,128)(2,1)S(1)}, bf16[2,448,256]{2,1,0:T(8,128)(2,1)S(1)}, u32[]{:S(2)}, u32[]{:S(2)}) collective-permute-start(bf16[2,448,256]{2,1,0:T(8,128)(2,1)S(1)} %slice.146), channel_id=1, source_target_pairs={{0,24},{1,25},{2,26},{3,27},{4,28},{5,29},{6,30},{7,31},{8,0},{9,1... | collective-permute-start | bytes 1376264 | tf_op jit(solution)/shard_map/ppermute | solution.py:74
  153.4 3.0 %collective-permute-start.28 = (bf16[2,448,256]{2,1,0:T(8,128)(2,1)S(1)}, bf16[2,448,256]{2,1,0:T(8,128)(2,1)S(1)}, u32[]{:S(2)}, u32[]{:S(2)}) collective-permute-start(bf16[2,448,256]{2,1,0:T(8,128)(2,1)S(1)} %collective-permute-done.23.refs_6_), channel_id=1, source_target_pairs={{0,32},{32,0},{64,96},{96,64},{128,160},{160,128},{192,224},{224,1... | collective-permute-start | bytes 1376264 | tf_op jit(solution)/shard_map/ppermute | solution.py:90
  155.3 2.4 %collective-permute-start.30 = (bf16[2,448,256]{2,1,0:T(8,128)(2,1)S(1)}, bf16[2,448,256]{2,1,0:T(8,128)(2,1)S(1)}, u32[]{:S(2)}, u32[]{:S(2)}) collective-permute-start(bf16[2,448,256]{2,1,0:T(8,128)(2,1)S(1)} %collective-permute-done.25.refs_8_), channel_id=1, source_target_pairs={{0,32},{32,0},{64,96},{96,64},{128,160},{160,128},{192,224},{224,1... | collective-permute-start | bytes 1376264 | tf_op jit(solution)/shard_map/ppermute | solution.py:90
  155.5 2.9 %collective-permute-start.31 = (bf16[2,448,256]{2,1,0:T(8,128)(2,1)S(1)}, bf16[2,448,256]{2,1,0:T(8,128)(2,1)S(1)}, u32[]{:S(2)}, u32[]{:S(2)}) collective-permute-start(bf16[2,448,256]{2,1,0:T(8,128)(2,1)S(1)} %collective-permute-done.26.refs_9_), channel_id=1, source_target_pairs={{0,32},{32,0},{64,96},{96,64},{128,160},{160,128},{192,224},{224,1... | collective-permute-start | bytes 1376264 | tf_op jit(solution)/shard_map/ppermute | solution.py:90
  (17 other events, 168.5 us)

commit v8 on v7

--- a/solution.py
+++ b/solution.py
@@ -38,7 +38,7 @@
 HALF_CHUNK = CHUNK // 2
 PIECE = TILE // 2
 CHUNK_PIECES = CHUNK // PIECE
-FIRST_PIECES = 5
+FIRST_PIECES = 4
 FIRST_SHARE = FIRST_PIECES * PIECE // Z_CHIPS
 OTHER_SHARE = SHARE - FIRST_SHARE
 STEPS = 12
@@ -122,6 +122,7 @@
     pick = jnp.where(wanted == column, 1.0, 0.0).astype(jnp.bfloat16)
     for shift in range(X_CHIPS):
         owner = lax.rem(x + shift, X_CHIPS)
+        rest = []
         for k in range(CHUNK_PIECES):
             piece = owner * CHUNK_PIECES + k
             tile = row * ROW_TILES + piece // 2
@@ -136,11 +137,12 @@
             if k < FIRST_PIECES:
                 chunk_refs[shift][k * PIECE : (k + 1) * PIECE, :] = piece
             else:
-                for part in range(PIECE // OTHER_SHARE):
-                    z = (k - FIRST_PIECES) * (PIECE // OTHER_SHARE) + part
-                    others_ref[z, shift * OTHER_SHARE : (shift + 1) * OTHER_SHARE, :] = piece[
-                        part * OTHER_SHARE : (part + 1) * OTHER_SHARE, :
-                    ]
+                rest.append(piece)
+        rest = jnp.concatenate(rest)
+        for z in range(Z_CHIPS):
+            others_ref[z, shift * OTHER_SHARE : (shift + 1) * OTHER_SHARE, :] = rest[
+                z * OTHER_SHARE : (z + 1) * OTHER_SHARE, :
+            ]
     for b in range(BLOCKS):
         rows = panel_ref[b * BLOCK : (b + 1) * BLOCK, :]
         columns_ref[:, b * BLOCK : (b + 1) * BLOCK] = dot_nt(pick, rows).astype(jnp.bfloat16)

time: 234 us -> 234 us (level)
    ppermute x13, waiting for transfers between devices: 21.1 us -> 14 us  [over_x(): return lax.ppermute(value, 'col', pairs)]
    all_to_all x2, waiting for transfers between devices: 8.22 us -> 13.8 us  [over_z(): lax.all_to_all(value, 'col', split_axis=0, concat_axis=0, axis_index_grou...]
    all_to_all x2, starting transfers between devices: 14.8 us -> 11.6 us  [over_z(): lax.all_to_all(value, 'col', split_axis=0, concat_axis=0, axis_index_grou...]
where the time goes in v8:
time: 234 us; the launch traced here: 233 us
  waiting for transfers between devices  74.1 us (32%)
  Pallas kernels  65.6 us (28%)
  starting transfers between devices  57.4 us (25%)
  blocking collectives  28.5 us (12%)
  other arithmetic  3.44 us (1%)
  local copies, waits for them, and re-layouts  3.05 us (1%)
    pallas_call x1, Pallas kernels, newton_schulz(): pl.pallas_call(newton_schulz_kernel, out_shape=jax.ShapeDtypeStruct((ROWS...  61.9 us
    ppermute x10, waiting for transfers between devices, over_y(): return lax.ppermute(value, 'row', pairs)  42.3 us
    ppermute x13, starting transfers between devices, over_x(): return lax.ppermute(value, 'col', pairs)  20.9 us
    all_to_all x1, blocking collectives, over_z(): lax.all_to_all(value, 'col', split_axis=0, concat_axis=0, axis_index_grou...  16.7 us
    ppermute x13, waiting for transfers between devices, over_x(): return lax.ppermute(value, 'col', pairs)  14 us
    all_to_all x2, waiting for transfers between devices, over_z(): lax.all_to_all(value, 'col', split_axis=0, concat_axis=0, axis_index_grou...  13.8 us
    ppermute x9, starting transfers between devices, over_cores(): return lax.ppermute(value, 'row', pairs)  12.8 us
    ppermute x10, starting transfers between devices, over_y(): return lax.ppermute(value, 'row', pairs)  12.1 us
  transfers between devices with their start and end apart: 34, of which 18 were waited for; matrix products, arithmetic and copies ran while one was open for 1% of the time, Pallas kernels for 0%

profile of v8, /device:TPU:1, one launch (start us, length us, event | category | flops | bytes accessed | tf_op | source)
XLA Modules:
  0.0 233.1 jit_solution(10518547441335267821)
XLA Ops:
  0.6 2.2 fusion
  2.8 3.6 %collective-permute-start.2 = (bf16[448,384]{1,0:T(8,128)(2,1)S(1)}, bf16[448,384]{1,0:T(8,128)(2,1)S(1)}, u32[]{:S(2)}, u32[]{:S(2)}) collective-permute-start(bf16[448,384]{1,0:T(8,128)(2,1)S(1)} %get-tuple-element.44.refs_0_), channel_id=1, source_target_pairs={{0,192},{32,224},{64,0},{96,32},{128,64},{160,96},{192,128},{224,1... | collective-permute-start | bytes 1032200 | tf_op jit(solution)/shard_map/ppermute | solution.py:83
  8.9 11.4 %collective-permute-done.2.refs_3_ = bf16[448,384]{1,0:T(8,128)(2,1)S(1)} collective-permute-done((bf16[448,384]{1,0:T(8,128)(2,1)S(1)}, bf16[448,384]{1,0:T(8,128)(2,1)S(1)}, u32[]{:S(2)}, u32[]{:S(2)}) %collective-permute-start.2) | collective-permute-done | bytes 344096 | tf_op jit(solution)/shard_map/ppermute | solution.py:83
  20.3 1.7 collective-permute-start.6
  22.0 3.2 %collective-permute-done.refs_1_ = bf16[448,384]{1,0:T(8,128)(2,1)S(1)} collective-permute-done((bf16[448,384]{1,0:T(8,128)(2,1)S(1)}, bf16[448,384]{1,0:T(8,128)(2,1)S(1)}, u32[]{:S(2)}, u32[]{:S(2)}) %collective-permute-start) | collective-permute-done | bytes 344096 | tf_op jit(solution)/shard_map/ppermute | solution.py:83
  27.0 3.7 %partial_gram.1 = (bf16[512,256]{1,0:T(8,128)(2,1)S(1)}, bf16[512,256]{1,0:T(8,128)(2,1)S(1)}, bf16[512,256]{1,0:T(8,128)(2,1)S(1)}, bf16[512,256]{1,0:T(8,128)(...) custom-call(bf16[448,384]{1,0:T(8,128)(2,1)S(1)} %get-tuple-element.44.refs_0_, ...), custom_call_target="tpu_custom_call" | custom-call | tf_op jit(solution)/shard_map/partial_gram/pallas_call | solution.py:153
  31.5 8.2 %all-to-all-start.1 = ((bf16[8,192,256]{2,1,0:T(8,128)(2,1)}), bf16[8,192,256]{2,1,0:T(8,128)(2,1)S(1)}, u32[]{:S(2)}, u32[]{:S(2)}) async-start(bf16[8,192,256]{2,1,0:T(8,128)(2,1)} %get-tuple-element.28), calls=%async_computation.1 | async-start | bytes 1572864 | tf_op jit(solution)/shard_map/all_to_all | solution.py:94
  39.6 2.7 %collective-permute-start.7 = (bf16[512,256]{1,0:T(8,128)(2,1)S(1)}, bf16[512,256]{1,0:T(8,128)(2,1)S(1)}, u32[]{:S(2)}, u32[]{:S(2)}) collective-permute-start(bf16[512,256]{1,0:T(8,128)(2,1)S(1)} %get-tuple-element.25), channel_id=1, source_target_pairs={{0,16},{1,17},{2,18},{3,19},{4,20},{5,21},{6,22},{7,23},{8,24},{9,... | collective-permute-start | bytes 786440 | tf_op jit(solution)/shard_map/ppermute | solution.py:74
  42.7 2.4 %collective-permute-start.9 = (bf16[512,256]{1,0:T(8,128)(2,1)S(1)}, bf16[512,256]{1,0:T(8,128)(2,1)S(1)}, u32[]{:S(2)}, u32[]{:S(2)}) collective-permute-start(bf16[512,256]{1,0:T(8,128)(2,1)S(1)} %get-tuple-element.27), channel_id=1, source_target_pairs={{0,24},{1,25},{2,26},{3,27},{4,28},{5,29},{6,30},{7,31},{8,0},{9,1... | collective-permute-start | bytes 786440 | tf_op jit(solution)/shard_map/ppermute | solution.py:74
  45.1 3.3 %collective-permute-done.7 = bf16[512,256]{1,0:T(8,128)(2,1)S(1)} collective-permute-done((bf16[512,256]{1,0:T(8,128)(2,1)S(1)}, bf16[512,256]{1,0:T(8,128)(2,1)S(1)}, u32[]{:S(2)}, u32[]{:S(2)}) %collective-permute-start.7) | collective-permute-done | bytes 262176 | tf_op jit(solution)/shard_map/ppermute | solution.py:74
  48.4 6.6 %collective-permute-done.8 = bf16[512,256]{1,0:T(8,128)(2,1)S(1)} collective-permute-done((bf16[512,256]{1,0:T(8,128)(2,1)S(1)}, bf16[512,256]{1,0:T(8,128)(2,1)S(1)}, u32[]{:S(2)}, u32[]{:S(2)}) %collective-permute-start.8) | collective-permute-done | bytes 262176 | tf_op jit(solution)/shard_map/ppermute | solution.py:74
  55.8 7.4 %all-to-all-done.1 = bf16[8,192,256]{2,1,0:T(8,128)(2,1)S(1)} async-done(((bf16[8,192,256]{2,1,0:T(8,128)(2,1)}), bf16[8,192,256]{2,1,0:T(8,128)(2,1)S(1)}, u32[]{:S(2)}, u32[]{:S(2)}) %all-to-all-start.1) | async-done | bytes 786464 | tf_op jit(solution)/shard_map/all_to_all | solution.py:94
  63.2 3.4 %all-to-all-start = ((bf16[8,64,256]{2,1,0:T(8,128)(2,1)}), bf16[8,64,256]{2,1,0:T(8,128)(2,1)S(1)}, u32[]{:S(2)}, u32[]{:S(2)}) async-start(bf16[8,64,256]{2,1,0:T(8,128)(2,1)} %bitcast), calls=%async_computation | async-start | bytes 524288 | tf_op jit(solution)/shard_map/all_to_all | solution.py:94
  66.8 2.8 %collective-permute-start.10 = (bf16[48,256]{1,0:T(8,128)(2,1)S(1)}, bf16[48,256]{1,0:T(8,128)(2,1)S(1)}, u32[]{:S(2)}, u32[]{:S(2)}) collective-permute-start(bf16[48,256]{1,0:T(8,128)(2,1)S(1)} %get-tuple-element.46), channel_id=1, source_target_pairs={{0,16},{1,17},{2,18},{3,19},{4,20},{5,21},{6,22},{7,23},{8,24},{9,... | collective-permute-start | bytes 73736 | tf_op jit(solution)/shard_map/ppermute | solution.py:74
  69.9 2.4 %collective-permute-start.12 = (bf16[48,256]{1,0:T(8,128)(2,1)S(1)}, bf16[48,256]{1,0:T(8,128)(2,1)S(1)}, u32[]{:S(2)}, u32[]{:S(2)}) collective-permute-start(bf16[48,256]{1,0:T(8,128)(2,1)S(1)} %get-tuple-element.48), channel_id=1, source_target_pairs={{0,24},{1,25},{2,26},{3,27},{4,28},{5,29},{6,30},{7,31},{8,0},{9,1... | collective-permute-start | bytes 73736 | tf_op jit(solution)/shard_map/ppermute | solution.py:74
  72.3 6.4 %all-to-all-done = bf16[8,64,256]{2,1,0:T(8,128)(2,1)S(1)} async-done(((bf16[8,64,256]{2,1,0:T(8,128)(2,1)}), bf16[8,64,256]{2,1,0:T(8,128)(2,1)S(1)}, u32[]{:S(2)}, u32[]{:S(2)}) %all-to-all-start) | async-done | bytes 262176 | tf_op jit(solution)/shard_map/all_to_all | solution.py:94
  78.8 16.7 %all_to_all.20 = bf16[8,112,256]{2,1,0:T(8,128)(2,1)S(1)} all-to-all(bf16[8,112,256]{2,1,0:T(8,128)(2,1)S(1)} %broadcast_in_dim.2), channel_id=1, replica_groups={{0,1,2,3,4,5,6,7},{8,9,10,11,12,13,14,15},{16,17,18,19,20,21,22,23},{24..., dimensions={0} | all-to-all | bytes 917504 | tf_op jit(solution)/shard_map/all_to_all | solution.py:94
  97.1 1.8 collective-permute-start.18
  98.9 2.4 %collective-permute-start.15 = (bf16[448,256]{1,0:T(8,128)(2,1)S(1)}, bf16[448,256]{1,0:T(8,128)(2,1)S(1)}, u32[]{:S(2)}, u32[]{:S(2)}) collective-permute-start(bf16[448,256]{1,0:T(8,128)(2,1)S(1)} %bitcast.29), channel_id=1, source_target_pairs={{0,24},{1,25},{2,26},{3,27},{4,28},{5,29},{6,30},{7,31},{8,0},{9,1... | collective-permute-start | bytes 688136 | tf_op jit(solution)/shard_map/ppermute | solution.py:74
  102.8 1.9 collective-permute-start.13
  104.7 4.1 %collective-permute-done.16 = bf16[448,256]{1,0:T(8,128)(2,1)S(1)} collective-permute-done((bf16[448,256]{1,0:T(8,128)(2,1)S(1)}, bf16[448,256]{1,0:T(8,128)(2,1)S(1)}, u32[]{:S(2)}, u32[]{:S(2)}) %collective-permute-start.16) | collective-permute-done | bytes 229408 | tf_op jit(solution)/shard_map/ppermute | solution.py:83
  109.0 1.7 collective-permute-done.13
  114.0 13.8 %collective-permute-done.21.refs_4_ = bf16[4,448,256]{2,1,0:T(8,128)(2,1)S(1)} collective-permute-done((bf16[4,448,256]{2,1,0:T(8,128)(2,1)S(1)}, bf16[4,448,256]{2,1,0:T(8,128)(2,1)S(1)}, u32[]{:S(2)}, u32[]{:S(2)}) %collective-permute-start.21) | collective-permute-done | bytes 917536 | tf_op jit(solution)/shard_map/ppermute | solution.py:83
  127.8 1.8 collective-permute-done.19.refs_2_
  130.4 6.9 %collective-permute-start.27 = (bf16[24,448,256]{2,1,0:T(8,128)(2,1)S(1)}, bf16[24,448,256]{2,1,0:T(8,128)(2,1)}, u32[]{:S(2)}, u32[]{:S(2)}) collective-permute-start(bf16[24,448,256]{2,1,0:T(8,128)(2,1)S(1)} %constant_dynamic-update-slice_fusion), channel_id=1, source_target_pairs={{0,32},{32,0},{64,96},{96,64},{128,160},{160,128},{192,224},{224,1... | collective-permute-start | bytes 16515080 | tf_op jit(solution)/shard_map/ppermute | solution.py:90
  137.3 2.7 %collective-permute-start.24 = (bf16[2,448,256]{2,1,0:T(8,128)(2,1)S(1)}, bf16[2,448,256]{2,1,0:T(8,128)(2,1)S(1)}, u32[]{:S(2)}, u32[]{:S(2)}) collective-permute-start(bf16[2,448,256]{2,1,0:T(8,128)(2,1)S(1)} %slice.150), channel_id=1, source_target_pairs={{0,192},{32,224},{64,0},{96,32},{128,64},{160,96},{192,128},{224,1... | collective-permute-start | bytes 1376264 | tf_op jit(solution)/shard_map/ppermute | solution.py:83
  140.0 2.7 %collective-permute-start.26 = (bf16[2,448,256]{2,1,0:T(8,128)(2,1)S(1)}, bf16[2,448,256]{2,1,0:T(8,128)(2,1)S(1)}, u32[]{:S(2)}, u32[]{:S(2)}) collective-permute-start(bf16[2,448,256]{2,1,0:T(8,128)(2,1)S(1)} %slice.151), channel_id=1, source_target_pairs={{0,24},{1,25},{2,26},{3,27},{4,28},{5,29},{6,30},{7,31},{8,0},{9,1... | collective-permute-start | bytes 1376264 | tf_op jit(solution)/shard_map/ppermute | solution.py:74
  142.7 7.9 %collective-permute-done.23.refs_6_ = bf16[2,448,256]{2,1,0:T(8,128)(2,1)S(1)} collective-permute-done((bf16[2,448,256]{2,1,0:T(8,128)(2,1)S(1)}, bf16[2,448,256]{2,1,0:T(8,128)(2,1)S(1)}, u32[]{:S(2)}, u32[]{:S(2)}) %collective-permute-start.23) | collective-permute-done | bytes 458784 | tf_op jit(solution)/shard_map/ppermute | solution.py:83
  150.6 2.0 collective-permute-done.25.refs_8_
  152.6 1.6 collective-permute-start.28
  158.5 61.9 %newton_schulz.1 = bf16[8,48,448]{2,1,0:T(8,128)(2,1)} custom-call(bf16[48,3584]{1,0:T(8,128)(2,1)} %copy-done, bf16[4,448,256]{2,1,0:T(8,128)(2,1)} %copy-done.2, bf16[4,448,256]{2,1,0:T(8,128)(2,1)} %copy-done.1, bf16[4,448,256]{2,1,0:T(8,128)(2,1)} %copy-done.4, bf16[4,448,256]{2,1,0:T(8,128)(2,1)} %copy-done.6, bf16[4,448,256]{2,1,0:T(8,128)(2,1)} %copy-done.3, ...), custom_call_target="tpu_custom_call" | custom-call | tf_op jit(solution)/shard_map/newton_schulz/pallas_call | solution.py:271
  220.4 11.8 %all_to_all.21 = bf16[8,48,448]{2,1,0:T(8,128)(2,1)S(1)} all-to-all(bf16[8,48,448]{2,1,0:T(8,128)(2,1)} %newton_schulz.1), channel_id=1, replica_groups=mesh['row'=8,'col'=32] {'row'}, dimensions={0} | all-to-all | bytes 688128 | tf_op jit(solution)/shard_map/all_to_all | solution.py:338
  (95 shorter events, 19.2 us)
Async XLA Ops:
  2.8 17.5 %collective-permute-start.2 = (bf16[448,384]{1,0:T(8,128)(2,1)S(1)}, bf16[448,384]{1,0:T(8,128)(2,1)S(1)}, u32[]{:S(2)}, u32[]{:S(2)}) collective-permute-start(bf16[448,384]{1,0:T(8,128)(2,1)S(1)} %get-tuple-element.44.refs_0_), channel_id=1, source_target_pairs={{0,192},{32,224},{64,0},{96,32},{128,64},{160,96},{192,128},{224,1... | collective-permute-start | bytes 1032200 | tf_op jit(solution)/shard_map/ppermute | solution.py:83
  6.4 15.7 %collective-permute-start.1 = (bf16[448,384]{1,0:T(8,128)(2,1)S(1)}, bf16[448,384]{1,0:T(8,128)(2,1)S(1)}, u32[]{:S(2)}, u32[]{:S(2)}) collective-permute-start(bf16[448,384]{1,0:T(8,128)(2,1)S(1)} %get-tuple-element.44.refs_0_), channel_id=1, source_target_pairs={{0,128},{32,160},{64,192},{96,224},{128,0},{160,32},{192,64},{224,... | collective-permute-start | bytes 1032200 | tf_op jit(solution)/shard_map/ppermute | solution.py:83
  6.7 18.5 %collective-permute-start = (bf16[448,384]{1,0:T(8,128)(2,1)S(1)}, bf16[448,384]{1,0:T(8,128)(2,1)S(1)}, u32[]{:S(2)}, u32[]{:S(2)}) collective-permute-start(bf16[448,384]{1,0:T(8,128)(2,1)S(1)} %get-tuple-element.44.refs_0_), channel_id=1, source_target_pairs={{0,64},{32,96},{64,128},{96,160},{128,192},{160,224},{192,0},{224,... | collective-permute-start | bytes 1032200 | tf_op jit(solution)/shard_map/ppermute | solution.py:83
  7.4 18.3 %collective-permute-start.3 = (bf16[448,384]{1,0:T(8,128)(2,1)S(1)}, bf16[448,384]{1,0:T(8,128)(2,1)S(1)}, u32[]{:S(2)}, u32[]{:S(2)}) collective-permute-start(bf16[448,384]{1,0:T(8,128)(2,1)S(1)} %get-tuple-element.44.refs_0_), channel_id=1, source_target_pairs={{0,32},{32,0},{64,96},{96,64},{128,160},{160,128},{192,224},{224,1... | collective-permute-start | bytes 1032200 | tf_op jit(solution)/shard_map/ppermute | solution.py:90
  20.3 5.4 %collective-permute-start.6 = (bf16[448,384]{1,0:T(8,128)(2,1)S(1)}, bf16[448,384]{1,0:T(8,128)(2,1)S(1)}, u32[]{:S(2)}, u32[]{:S(2)}) collective-permute-start(bf16[448,384]{1,0:T(8,128)(2,1)S(1)} %collective-permute-done.2.refs_3_), channel_id=1, source_target_pairs={{0,32},{32,0},{64,96},{96,64},{128,160},{160,128},{192,224},{224,1... | collective-permute-start | bytes 1032200 | tf_op jit(solution)/shard_map/ppermute | solution.py:90
  22.0 3.7 %collective-permute-start.5 = (bf16[448,384]{1,0:T(8,128)(2,1)S(1)}, bf16[448,384]{1,0:T(8,128)(2,1)S(1)}, u32[]{:S(2)}, u32[]{:S(2)}) collective-permute-start(bf16[448,384]{1,0:T(8,128)(2,1)S(1)} %collective-permute-done.1.refs_2_), channel_id=1, source_target_pairs={{0,32},{32,0},{64,96},{96,64},{128,160},{160,128},{192,224},{224,1... | collective-permute-start | bytes 1032200 | tf_op jit(solution)/shard_map/ppermute | solution.py:90
  31.5 31.7 %all-to-all-start.1 = ((bf16[8,192,256]{2,1,0:T(8,128)(2,1)}), bf16[8,192,256]{2,1,0:T(8,128)(2,1)S(1)}, u32[]{:S(2)}, u32[]{:S(2)}) async-start(bf16[8,192,256]{2,1,0:T(8,128)(2,1)} %get-tuple-element.28), calls=%async_computation.1 | async-start | bytes 1572864 | tf_op jit(solution)/shard_map/all_to_all | solution.py:94
  39.6 8.7 %collective-permute-start.7 = (bf16[512,256]{1,0:T(8,128)(2,1)S(1)}, bf16[512,256]{1,0:T(8,128)(2,1)S(1)}, u32[]{:S(2)}, u32[]{:S(2)}) collective-permute-start(bf16[512,256]{1,0:T(8,128)(2,1)S(1)} %get-tuple-element.25), channel_id=1, source_target_pairs={{0,16},{1,17},{2,18},{3,19},{4,20},{5,21},{6,22},{7,23},{8,24},{9,... | collective-permute-start | bytes 786440 | tf_op jit(solution)/shard_map/ppermute | solution.py:74
  42.4 12.6 %collective-permute-start.8 = (bf16[512,256]{1,0:T(8,128)(2,1)S(1)}, bf16[512,256]{1,0:T(8,128)(2,1)S(1)}, u32[]{:S(2)}, u32[]{:S(2)}) collective-permute-start(bf16[512,256]{1,0:T(8,128)(2,1)S(1)} %get-tuple-element.26), channel_id=1, source_target_pairs={{0,8},{1,9},{2,10},{3,11},{4,12},{5,13},{6,14},{7,15},{8,16},{9,17... | collective-permute-start | bytes 786440 | tf_op jit(solution)/shard_map/ppermute | solution.py:74
  42.7 12.3 %collective-permute-start.9 = (bf16[512,256]{1,0:T(8,128)(2,1)S(1)}, bf16[512,256]{1,0:T(8,128)(2,1)S(1)}, u32[]{:S(2)}, u32[]{:S(2)}) collective-permute-start(bf16[512,256]{1,0:T(8,128)(2,1)S(1)} %get-tuple-element.27), channel_id=1, source_target_pairs={{0,24},{1,25},{2,26},{3,27},{4,28},{5,29},{6,30},{7,31},{8,0},{9,1... | collective-permute-start | bytes 786440 | tf_op jit(solution)/shard_map/ppermute | solution.py:74
  63.2 15.4 %all-to-all-start = ((bf16[8,64,256]{2,1,0:T(8,128)(2,1)}), bf16[8,64,256]{2,1,0:T(8,128)(2,1)S(1)}, u32[]{:S(2)}, u32[]{:S(2)}) async-start(bf16[8,64,256]{2,1,0:T(8,128)(2,1)} %bitcast), calls=%async_computation | async-start | bytes 524288 | tf_op jit(solution)/shard_map/all_to_all | solution.py:94
  66.8 11.9 %collective-permute-start.10 = (bf16[48,256]{1,0:T(8,128)(2,1)S(1)}, bf16[48,256]{1,0:T(8,128)(2,1)S(1)}, u32[]{:S(2)}, u32[]{:S(2)}) collective-permute-start(bf16[48,256]{1,0:T(8,128)(2,1)S(1)} %get-tuple-element.46), channel_id=1, source_target_pairs={{0,16},{1,17},{2,18},{3,19},{4,20},{5,21},{6,22},{7,23},{8,24},{9,... | collective-permute-start | bytes 73736 | tf_op jit(solution)/shard_map/ppermute | solution.py:74
  69.6 9.1 %collective-permute-start.11 = (bf16[48,256]{1,0:T(8,128)(2,1)S(1)}, bf16[48,256]{1,0:T(8,128)(2,1)S(1)}, u32[]{:S(2)}, u32[]{:S(2)}) collective-permute-start(bf16[48,256]{1,0:T(8,128)(2,1)S(1)} %get-tuple-element.47), channel_id=1, source_target_pairs={{0,8},{1,9},{2,10},{3,11},{4,12},{5,13},{6,14},{7,15},{8,16},{9,17... | collective-permute-start | bytes 73736 | tf_op jit(solution)/shard_map/ppermute | solution.py:74
  69.9 8.8 %collective-permute-start.12 = (bf16[48,256]{1,0:T(8,128)(2,1)S(1)}, bf16[48,256]{1,0:T(8,128)(2,1)S(1)}, u32[]{:S(2)}, u32[]{:S(2)}) collective-permute-start(bf16[48,256]{1,0:T(8,128)(2,1)S(1)} %get-tuple-element.48), channel_id=1, source_target_pairs={{0,24},{1,25},{2,26},{3,27},{4,28},{5,29},{6,30},{7,31},{8,0},{9,1... | collective-permute-start | bytes 73736 | tf_op jit(solution)/shard_map/ppermute | solution.py:74
  95.6 7.3 %collective-permute-start.17 = (bf16[448,256]{1,0:T(8,128)(2,1)S(1)}, bf16[448,256]{1,0:T(8,128)(2,1)S(1)}, u32[]{:S(2)}, u32[]{:S(2)}) collective-permute-start(bf16[448,256]{1,0:T(8,128)(2,1)S(1)} %pad_maximum_fusion.2), channel_id=1, source_target_pairs={{0,128},{32,160},{64,192},{96,224},{128,0},{160,32},{192,64},{224,... | collective-permute-start | bytes 688136 | tf_op jit(solution)/shard_map/ppermute | solution.py:83
  96.2 12.7 %collective-permute-start.16 = (bf16[448,256]{1,0:T(8,128)(2,1)S(1)}, bf16[448,256]{1,0:T(8,128)(2,1)S(1)}, u32[]{:S(2)}, u32[]{:S(2)}) collective-permute-start(bf16[448,256]{1,0:T(8,128)(2,1)S(1)} %pad_maximum_fusion.2), channel_id=1, source_target_pairs={{0,64},{32,96},{64,128},{96,160},{128,192},{160,224},{192,0},{224,... | collective-permute-start | bytes 688136 | tf_op jit(solution)/shard_map/ppermute | solution.py:83
  97.1 11.7 %collective-permute-start.18 = (bf16[448,256]{1,0:T(8,128)(2,1)S(1)}, bf16[448,256]{1,0:T(8,128)(2,1)S(1)}, u32[]{:S(2)}, u32[]{:S(2)}) collective-permute-start(bf16[448,256]{1,0:T(8,128)(2,1)S(1)} %pad_maximum_fusion.2), channel_id=1, source_target_pairs={{0,192},{32,224},{64,0},{96,32},{128,64},{160,96},{192,128},{224,1... | collective-permute-start | bytes 688136 | tf_op jit(solution)/shard_map/ppermute | solution.py:83
  98.9 10.1 %collective-permute-start.15 = (bf16[448,256]{1,0:T(8,128)(2,1)S(1)}, bf16[448,256]{1,0:T(8,128)(2,1)S(1)}, u32[]{:S(2)}, u32[]{:S(2)}) collective-permute-start(bf16[448,256]{1,0:T(8,128)(2,1)S(1)} %bitcast.29), channel_id=1, source_target_pairs={{0,24},{1,25},{2,26},{3,27},{4,28},{5,29},{6,30},{7,31},{8,0},{9,1... | collective-permute-start | bytes 688136 | tf_op jit(solution)/shard_map/ppermute | solution.py:74
  101.3 7.7 %collective-permute-start.14 = (bf16[448,256]{1,0:T(8,128)(2,1)S(1)}, bf16[448,256]{1,0:T(8,128)(2,1)S(1)}, u32[]{:S(2)}, u32[]{:S(2)}) collective-permute-start(bf16[448,256]{1,0:T(8,128)(2,1)S(1)} %bitcast.30), channel_id=1, source_target_pairs={{0,16},{1,17},{2,18},{3,19},{4,20},{5,21},{6,22},{7,23},{8,24},{9,... | collective-permute-start | bytes 688136 | tf_op jit(solution)/shard_map/ppermute | solution.py:74
  102.8 7.9 %collective-permute-start.13 = (bf16[448,256]{1,0:T(8,128)(2,1)S(1)}, bf16[448,256]{1,0:T(8,128)(2,1)S(1)}, u32[]{:S(2)}, u32[]{:S(2)}) collective-permute-start(bf16[448,256]{1,0:T(8,128)(2,1)S(1)} %bitcast.31), channel_id=1, source_target_pairs={{0,8},{1,9},{2,10},{3,11},{4,12},{5,13},{6,14},{7,15},{8,16},{9,17... | collective-permute-start | bytes 688136 | tf_op jit(solution)/shard_map/ppermute | solution.py:74
  110.9 17.0 %collective-permute-start.21 = (bf16[4,448,256]{2,1,0:T(8,128)(2,1)S(1)}, bf16[4,448,256]{2,1,0:T(8,128)(2,1)S(1)}, u32[]{:S(2)}, u32[]{:S(2)}) collective-permute-start(bf16[4,448,256]{2,1,0:T(8,128)(2,1)S(1)} %pad_maximum_fusion.refs_0_), channel_id=1, source_target_pairs={{0,192},{32,224},{64,0},{96,32},{128,64},{160,96},{192,128},{224,1... | collective-permute-start | bytes 2752520 | tf_op jit(solution)/shard_map/ppermute | solution.py:83
  111.5 18.1 %collective-permute-start.19 = (bf16[4,448,256]{2,1,0:T(8,128)(2,1)S(1)}, bf16[4,448,256]{2,1,0:T(8,128)(2,1)S(1)}, u32[]{:S(2)}, u32[]{:S(2)}) collective-permute-start(bf16[4,448,256]{2,1,0:T(8,128)(2,1)S(1)} %pad_maximum_fusion.refs_0_), channel_id=1, source_target_pairs={{0,64},{32,96},{64,128},{96,160},{128,192},{160,224},{192,0},{224,... | collective-permute-start | bytes 2752520 | tf_op jit(solution)/shard_map/ppermute | solution.py:83
  112.4 17.3 %collective-permute-start.22 = (bf16[4,448,256]{2,1,0:T(8,128)(2,1)S(1)}, bf16[4,448,256]{2,1,0:T(8,128)(2,1)S(1)}, u32[]{:S(2)}, u32[]{:S(2)}) collective-permute-start(bf16[4,448,256]{2,1,0:T(8,128)(2,1)S(1)} %pad_maximum_fusion.1.refs_1_), channel_id=1, source_target_pairs={{0,24},{1,25},{2,26},{3,27},{4,28},{5,29},{6,30},{7,31},{8,0},{9,1... | collective-permute-start | bytes 2752520 | tf_op jit(solution)/shard_map/ppermute | solution.py:74
  112.9 17.2 %collective-permute-start.20 = (bf16[4,448,256]{2,1,0:T(8,128)(2,1)S(1)}, bf16[4,448,256]{2,1,0:T(8,128)(2,1)S(1)}, u32[]{:S(2)}, u32[]{:S(2)}) collective-permute-start(bf16[4,448,256]{2,1,0:T(8,128)(2,1)S(1)} %pad_maximum_fusion.1.refs_1_), channel_id=1, source_target_pairs={{0,8},{1,9},{2,10},{3,11},{4,12},{5,13},{6,14},{7,15},{8,16},{9,17... | collective-permute-start | bytes 2752520 | tf_op jit(solution)/shard_map/ppermute | solution.py:74
  130.4 22.2 %collective-permute-start.27 = (bf16[24,448,256]{2,1,0:T(8,128)(2,1)S(1)}, bf16[24,448,256]{2,1,0:T(8,128)(2,1)}, u32[]{:S(2)}, u32[]{:S(2)}) collective-permute-start(bf16[24,448,256]{2,1,0:T(8,128)(2,1)S(1)} %constant_dynamic-update-slice_fusion), channel_id=1, source_target_pairs={{0,32},{32,0},{64,96},{96,64},{128,160},{160,128},{192,224},{224,1... | collective-permute-start | bytes 16515080 | tf_op jit(solution)/shard_map/ppermute | solution.py:90
  137.3 13.3 %collective-permute-start.23 = (bf16[2,448,256]{2,1,0:T(8,128)(2,1)S(1)}, bf16[2,448,256]{2,1,0:T(8,128)(2,1)S(1)}, u32[]{:S(2)}, u32[]{:S(2)}) collective-permute-start(bf16[2,448,256]{2,1,0:T(8,128)(2,1)S(1)} %slice.148), channel_id=1, source_target_pairs={{0,64},{32,96},{64,128},{96,160},{128,192},{160,224},{192,0},{224,... | collective-permute-start | bytes 1376264 | tf_op jit(solution)/shard_map/ppermute | solution.py:83
  137.3 13.3 %collective-permute-start.24 = (bf16[2,448,256]{2,1,0:T(8,128)(2,1)S(1)}, bf16[2,448,256]{2,1,0:T(8,128)(2,1)S(1)}, u32[]{:S(2)}, u32[]{:S(2)}) collective-permute-start(bf16[2,448,256]{2,1,0:T(8,128)(2,1)S(1)} %slice.150), channel_id=1, source_target_pairs={{0,192},{32,224},{64,0},{96,32},{128,64},{160,96},{192,128},{224,1... | collective-permute-start | bytes 1376264 | tf_op jit(solution)/shard_map/ppermute | solution.py:83
  140.0 12.6 %collective-permute-start.25 = (bf16[2,448,256]{2,1,0:T(8,128)(2,1)S(1)}, bf16[2,448,256]{2,1,0:T(8,128)(2,1)S(1)}, u32[]{:S(2)}, u32[]{:S(2)}) collective-permute-start(bf16[2,448,256]{2,1,0:T(8,128)(2,1)S(1)} %slice.149), channel_id=1, source_target_pairs={{0,8},{1,9},{2,10},{3,11},{4,12},{5,13},{6,14},{7,15},{8,16},{9,17... | collective-permute-start | bytes 1376264 | tf_op jit(solution)/shard_map/ppermute | solution.py:74
  140.0 12.6 %collective-permute-start.26 = (bf16[2,448,256]{2,1,0:T(8,128)(2,1)S(1)}, bf16[2,448,256]{2,1,0:T(8,128)(2,1)S(1)}, u32[]{:S(2)}, u32[]{:S(2)}) collective-permute-start(bf16[2,448,256]{2,1,0:T(8,128)(2,1)S(1)} %slice.151), channel_id=1, source_target_pairs={{0,24},{1,25},{2,26},{3,27},{4,28},{5,29},{6,30},{7,31},{8,0},{9,1... | collective-permute-start | bytes 1376264 | tf_op jit(solution)/shard_map/ppermute | solution.py:74
  152.6 3.0 %collective-permute-start.28 = (bf16[2,448,256]{2,1,0:T(8,128)(2,1)S(1)}, bf16[2,448,256]{2,1,0:T(8,128)(2,1)S(1)}, u32[]{:S(2)}, u32[]{:S(2)}) collective-permute-start(bf16[2,448,256]{2,1,0:T(8,128)(2,1)S(1)} %collective-permute-done.23.refs_6_), channel_id=1, source_target_pairs={{0,32},{32,0},{64,96},{96,64},{128,160},{160,128},{192,224},{224,1... | collective-permute-start | bytes 1376264 | tf_op jit(solution)/shard_map/ppermute | solution.py:90
  154.3 2.7 %collective-permute-start.30 = (bf16[2,448,256]{2,1,0:T(8,128)(2,1)S(1)}, bf16[2,448,256]{2,1,0:T(8,128)(2,1)S(1)}, u32[]{:S(2)}, u32[]{:S(2)}) collective-permute-start(bf16[2,448,256]{2,1,0:T(8,128)(2,1)S(1)} %collective-permute-done.25.refs_8_), channel_id=1, source_target_pairs={{0,32},{32,0},{64,96},{96,64},{128,160},{160,128},{192,224},{224,1... | collective-permute-start | bytes 1376264 | tf_op jit(solution)/shard_map/ppermute | solution.py:90
  154.7 2.9 %collective-permute-start.31 = (bf16[2,448,256]{2,1,0:T(8,128)(2,1)S(1)}, bf16[2,448,256]{2,1,0:T(8,128)(2,1)S(1)}, u32[]{:S(2)}, u32[]{:S(2)}) collective-permute-start(bf16[2,448,256]{2,1,0:T(8,128)(2,1)S(1)} %collective-permute-done.26.refs_9_), channel_id=1, source_target_pairs={{0,32},{32,0},{64,96},{96,64},{128,160},{160,128},{192,224},{224,1... | collective-permute-start | bytes 1376264 | tf_op jit(solution)/shard_map/ppermute | solution.py:90
  (17 other events, 168.3 us)

commit v9 on v8

--- a/solution.py
+++ b/solution.py
@@ -54,7 +54,7 @@
 NEAR = [line(half, last, ALL_FOUR) for last in (0, 1, 3) for half in (0, 1)]
 FAR = [line(half, 2, others) for half in (0, 1) for others in ((0, 1), (2, 3))]
 OWN_PARTS = len(NEAR) + len(FAR)
-PARTS = NEAR + FAR + [sum(NEAR, [])] + FAR
+PARTS = NEAR + FAR + [sum(NEAR, []), sum(FAR, [])]
 
 Z_GROUPS = [[x * Z_CHIPS + z for z in range(Z_CHIPS)] for x in range(X_CHIPS)]
 
@@ -322,7 +322,7 @@
     near = over_cores(jnp.concatenate([first, second] + ups + downs))
     sent, near = lax.optimization_barrier((far, near))
     own_core = [first, second] + ups + downs + far
-    return own_core + [near] + [over_cores(part) for part in sent]
+    return own_core + [near, over_cores(jnp.concatenate(sent))]
 
 
 def per_device(gradient, momentum):
@@ -337,6 +337,8 @@
     update = newton_schulz(columns, parts)
     update = lax.all_to_all(update, "row", split_axis=0, concat_axis=0)
     update_matrix = update.reshape(PANEL_COLS, OWN_ROWS).T
+    gradient, momentum = lax.optimization_barrier((gradient, momentum))
+    buffer = MOMENTUM_DECAY * momentum + gradient.astype(jnp.float32)
     return (update_matrix, buffer)
 
 

time: 234 us -> 235 us (level)
  blocking collectives: 28.5 us -> 16.7 us
  waiting for transfers between devices: 74.1 us -> 80.4 us
  starting transfers between devices: 57.4 us -> 62.9 us
    all_to_all x1 -> x0, blocking collectives: 11.8 us -> none  [per_device(): update = lax.all_to_all(update, 'row', split_axis=0, concat_axis=0)]
    ppermute x10, waiting for transfers between devices: 42.3 us -> 31.3 us  [over_y(): return lax.ppermute(value, 'row', pairs)]
    ppermute x13, waiting for transfers between devices: 14 us -> 21.7 us  [over_x(): return lax.ppermute(value, 'col', pairs)]
    all_to_all x0 -> x1, waiting for transfers between devices: none -> 7.16 us  [per_device(): update = lax.all_to_all(update, 'row', split_axis=0, concat_axis=0)]
    all_to_all x0 -> x1, starting transfers between devices: none -> 3.74 us  [per_device(): update = lax.all_to_all(update, 'row', split_axis=0, concat_axis=0)]
    ppermute x9 -> x6, starting transfers between devices: 12.8 us -> 14.2 us  [over_cores(): return lax.ppermute(value, 'row', pairs)]
    ppermute x9 -> x6, waiting for transfers between devices: 4.07 us -> 5.17 us  [over_cores(): return lax.ppermute(value, 'row', pairs)]
  transfers between devices with their start and end apart: 34 -> 32, of which waited for: 18 -> 17; matrix products, arithmetic and copies ran while one was open for 1% -> 1% of each run, Pallas kernels for 0% -> 0%
where the time goes in v9:
time: 235 us; the launch traced here: 234 us
  waiting for transfers between devices  80.4 us (34%)
  Pallas kernels  65.6 us (28%)
  starting transfers between devices  62.9 us (27%)
  blocking collectives  16.7 us (7%)
  local copies, waits for them, and re-layouts  3.92 us (2%)
  other arithmetic  3.76 us (2%)
    pallas_call x1, Pallas kernels, newton_schulz(): pl.pallas_call(newton_schulz_kernel, out_shape=jax.ShapeDtypeStruct((ROWS...  61.9 us
    ppermute x10, waiting for transfers between devices, over_y(): return lax.ppermute(value, 'row', pairs)  31.3 us
    ppermute x13, waiting for transfers between devices, over_x(): return lax.ppermute(value, 'col', pairs)  21.7 us
    ppermute x13, starting transfers between devices, over_x(): return lax.ppermute(value, 'col', pairs)  19.4 us
    all_to_all x1, blocking collectives, over_z(): lax.all_to_all(value, 'col', split_axis=0, concat_axis=0, axis_index_grou...  16.7 us
    all_to_all x2, waiting for transfers between devices, over_z(): lax.all_to_all(value, 'col', split_axis=0, concat_axis=0, axis_index_grou...  15.1 us
    ppermute x6, starting transfers between devices, over_cores(): return lax.ppermute(value, 'row', pairs)  14.2 us
    ppermute x10, starting transfers between devices, over_y(): return lax.ppermute(value, 'row', pairs)  14 us
  transfers between devices with their start and end apart: 32, of which 17 were waited for; matrix products, arithmetic and copies ran while one was open for 1% of the time, Pallas kernels for 0%

profile of v9, /device:TPU:1, one launch (start us, length us, event | category | flops | bytes accessed | tf_op | source)
XLA Modules:
  0.0 234.3 jit_solution(3128338895167052111)
XLA Ops:
  2.0 2.2 collective-permute-start
  4.2 2.6 %collective-permute-start.1 = (bf16[448,384]{1,0:T(8,128)(2,1)S(1)}, bf16[448,384]{1,0:T(8,128)(2,1)S(1)}, u32[]{:S(2)}, u32[]{:S(2)}) collective-permute-start(bf16[448,384]{1,0:T(8,128)(2,1)S(1)} %fusion.1.refs_0_), channel_id=1, source_target_pairs={{0,128},{32,160},{64,192},{96,224},{128,0},{160,32},{192,64},{224,... | collective-permute-start | bytes 1032200 | tf_op jit(solution)/shard_map/ppermute | solution.py:83
  9.4 2.0 collective-permute-done.refs_1_
  11.4 3.3 %collective-permute-start.4 = (bf16[448,384]{1,0:T(8,128)(2,1)S(1)}, bf16[448,384]{1,0:T(8,128)(2,1)S(1)}, u32[]{:S(2)}, u32[]{:S(2)}) collective-permute-start(bf16[448,384]{1,0:T(8,128)(2,1)S(1)} %collective-permute-done.refs_1_), channel_id=1, source_target_pairs={{0,32},{32,0},{64,96},{96,64},{128,160},{160,128},{192,224},{224,1... | collective-permute-start | bytes 1032200 | tf_op jit(solution)/shard_map/ppermute | solution.py:90
  14.6 7.0 %collective-permute-done.1.refs_2_ = bf16[448,384]{1,0:T(8,128)(2,1)S(1)} collective-permute-done((bf16[448,384]{1,0:T(8,128)(2,1)S(1)}, bf16[448,384]{1,0:T(8,128)(2,1)S(1)}, u32[]{:S(2)}, u32[]{:S(2)}) %collective-permute-start.1) | collective-permute-done | bytes 344096 | tf_op jit(solution)/shard_map/ppermute | solution.py:83
  25.0 3.7 %partial_gram.1 = (bf16[512,256]{1,0:T(8,128)(2,1)S(1)}, bf16[512,256]{1,0:T(8,128)(2,1)S(1)}, bf16[512,256]{1,0:T(8,128)(2,1)S(1)}, bf16[512,256]{1,0:T(8,128)(...) custom-call(bf16[448,384]{1,0:T(8,128)(2,1)S(1)} %fusion.1.refs_0_, ...), custom_call_target="tpu_custom_call" | custom-call | tf_op jit(solution)/shard_map/partial_gram/pallas_call | solution.py:153
  29.4 8.2 %all-to-all-start.1 = ((bf16[8,192,256]{2,1,0:T(8,128)(2,1)}), bf16[8,192,256]{2,1,0:T(8,128)(2,1)S(1)}, u32[]{:S(2)}, u32[]{:S(2)}) async-start(bf16[8,192,256]{2,1,0:T(8,128)(2,1)} %get-tuple-element.30), calls=%async_computation.1 | async-start | bytes 1572864 | tf_op jit(solution)/shard_map/all_to_all | solution.py:94
  37.6 2.5 %collective-permute-start.9 = (bf16[512,256]{1,0:T(8,128)(2,1)S(1)}, bf16[512,256]{1,0:T(8,128)(2,1)S(1)}, u32[]{:S(2)}, u32[]{:S(2)}) collective-permute-start(bf16[512,256]{1,0:T(8,128)(2,1)S(1)} %get-tuple-element.29), channel_id=1, source_target_pairs={{0,24},{1,25},{2,26},{3,27},{4,28},{5,29},{6,30},{7,31},{8,0},{9,1... | collective-permute-start | bytes 786440 | tf_op jit(solution)/shard_map/ppermute | solution.py:74
  40.1 1.7 collective-permute-start.7
  41.8 4.0 %collective-permute-done.9 = bf16[512,256]{1,0:T(8,128)(2,1)S(1)} collective-permute-done((bf16[512,256]{1,0:T(8,128)(2,1)S(1)}, bf16[512,256]{1,0:T(8,128)(2,1)S(1)}, u32[]{:S(2)}, u32[]{:S(2)}) %collective-permute-start.9) | collective-permute-done | bytes 262176 | tf_op jit(solution)/shard_map/ppermute | solution.py:74
  45.8 3.2 %collective-permute-done.8 = bf16[512,256]{1,0:T(8,128)(2,1)S(1)} collective-permute-done((bf16[512,256]{1,0:T(8,128)(2,1)S(1)}, bf16[512,256]{1,0:T(8,128)(2,1)S(1)}, u32[]{:S(2)}, u32[]{:S(2)}) %collective-permute-start.8) | collective-permute-done | bytes 262176 | tf_op jit(solution)/shard_map/ppermute | solution.py:74
  49.1 3.8 %collective-permute-done.7 = bf16[512,256]{1,0:T(8,128)(2,1)S(1)} collective-permute-done((bf16[512,256]{1,0:T(8,128)(2,1)S(1)}, bf16[512,256]{1,0:T(8,128)(2,1)S(1)}, u32[]{:S(2)}, u32[]{:S(2)}) %collective-permute-start.7) | collective-permute-done | bytes 262176 | tf_op jit(solution)/shard_map/ppermute | solution.py:74
  53.7 7.5 %all-to-all-done.1 = bf16[8,192,256]{2,1,0:T(8,128)(2,1)S(1)} async-done(((bf16[8,192,256]{2,1,0:T(8,128)(2,1)}), bf16[8,192,256]{2,1,0:T(8,128)(2,1)S(1)}, u32[]{:S(2)}, u32[]{:S(2)}) %all-to-all-start.1) | async-done | bytes 786464 | tf_op jit(solution)/shard_map/all_to_all | solution.py:94
  61.2 3.4 %all-to-all-start = ((bf16[8,64,256]{2,1,0:T(8,128)(2,1)}), bf16[8,64,256]{2,1,0:T(8,128)(2,1)S(1)}, u32[]{:S(2)}, u32[]{:S(2)}) async-start(bf16[8,64,256]{2,1,0:T(8,128)(2,1)} %bitcast), calls=%async_computation | async-start | bytes 524288 | tf_op jit(solution)/shard_map/all_to_all | solution.py:94
  64.7 2.6 %collective-permute-start.12 = (bf16[48,256]{1,0:T(8,128)(2,1)S(1)}, bf16[48,256]{1,0:T(8,128)(2,1)S(1)}, u32[]{:S(2)}, u32[]{:S(2)}) collective-permute-start(bf16[48,256]{1,0:T(8,128)(2,1)S(1)} %get-tuple-element.50), channel_id=1, source_target_pairs={{0,24},{1,25},{2,26},{3,27},{4,28},{5,29},{6,30},{7,31},{8,0},{9,1... | collective-permute-start | bytes 73736 | tf_op jit(solution)/shard_map/ppermute | solution.py:74
  67.3 1.7 collective-permute-start.10
  69.0 7.6 %all-to-all-done = bf16[8,64,256]{2,1,0:T(8,128)(2,1)S(1)} async-done(((bf16[8,64,256]{2,1,0:T(8,128)(2,1)}), bf16[8,64,256]{2,1,0:T(8,128)(2,1)S(1)}, u32[]{:S(2)}, u32[]{:S(2)}) %all-to-all-start) | async-done | bytes 262176 | tf_op jit(solution)/shard_map/all_to_all | solution.py:94
  76.8 16.7 %all_to_all.20 = bf16[8,112,256]{2,1,0:T(8,128)(2,1)S(1)} all-to-all(bf16[8,112,256]{2,1,0:T(8,128)(2,1)S(1)} %broadcast_in_dim.2), channel_id=1, replica_groups={{0,1,2,3,4,5,6,7},{8,9,10,11,12,13,14,15},{16,17,18,19,20,21,22,23},{24..., dimensions={0} | all-to-all | bytes 917504 | tf_op jit(solution)/shard_map/all_to_all | solution.py:94
  93.5 2.6 %collective-permute-start.15 = (bf16[448,256]{1,0:T(8,128)(2,1)S(1)}, bf16[448,256]{1,0:T(8,128)(2,1)S(1)}, u32[]{:S(2)}, u32[]{:S(2)}) collective-permute-start(bf16[448,256]{1,0:T(8,128)(2,1)S(1)} %bitcast.29), channel_id=1, source_target_pairs={{0,24},{1,25},{2,26},{3,27},{4,28},{5,29},{6,30},{7,31},{8,0},{9,1... | collective-permute-start | bytes 688136 | tf_op jit(solution)/shard_map/ppermute | solution.py:74
  102.5 6.0 %collective-permute-done.13 = bf16[448,256]{1,0:T(8,128)(2,1)S(1)} collective-permute-done((bf16[448,256]{1,0:T(8,128)(2,1)S(1)}, bf16[448,256]{1,0:T(8,128)(2,1)S(1)}, u32[]{:S(2)}, u32[]{:S(2)}) %collective-permute-start.13) | collective-permute-done | bytes 229408 | tf_op jit(solution)/shard_map/ppermute | solution.py:74
  110.5 2.6 %collective-permute-start.21 = (bf16[4,448,256]{2,1,0:T(8,128)(2,1)S(1)}, bf16[4,448,256]{2,1,0:T(8,128)(2,1)S(1)}, u32[]{:S(2)}, u32[]{:S(2)}) collective-permute-start(bf16[4,448,256]{2,1,0:T(8,128)(2,1)S(1)} %pad_maximum_fusion.1.refs_0_), channel_id=1, source_target_pairs={{0,192},{32,224},{64,0},{96,32},{128,64},{160,96},{192,128},{224,1... | collective-permute-start | bytes 2752520 | tf_op jit(solution)/shard_map/ppermute | solution.py:83
  113.1 2.7 %collective-permute-start.22 = (bf16[4,448,256]{2,1,0:T(8,128)(2,1)S(1)}, bf16[4,448,256]{2,1,0:T(8,128)(2,1)S(1)}, u32[]{:S(2)}, u32[]{:S(2)}) collective-permute-start(bf16[4,448,256]{2,1,0:T(8,128)(2,1)S(1)} %pad_maximum_fusion.2.refs_1_), channel_id=1, source_target_pairs={{0,24},{1,25},{2,26},{3,27},{4,28},{5,29},{6,30},{7,31},{8,0},{9,1... | collective-permute-start | bytes 2752520 | tf_op jit(solution)/shard_map/ppermute | solution.py:74
  115.9 13.6 %collective-permute-done.19.refs_2_ = bf16[4,448,256]{2,1,0:T(8,128)(2,1)S(1)} collective-permute-done((bf16[4,448,256]{2,1,0:T(8,128)(2,1)S(1)}, bf16[4,448,256]{2,1,0:T(8,128)(2,1)S(1)}, u32[]{:S(2)}, u32[]{:S(2)}) %collective-permute-start.19) | collective-permute-done | bytes 917536 | tf_op jit(solution)/shard_map/ppermute | solution.py:83
  130.5 6.3 %collective-permute-start.27 = (bf16[24,448,256]{2,1,0:T(8,128)(2,1)S(1)}, bf16[24,448,256]{2,1,0:T(8,128)(2,1)}, u32[]{:S(2)}, u32[]{:S(2)}) collective-permute-start(bf16[24,448,256]{2,1,0:T(8,128)(2,1)S(1)} %constant_dynamic-update-slice_fusion), channel_id=1, source_target_pairs={{0,32},{32,0},{64,96},{96,64},{128,160},{160,128},{192,224},{224,1... | collective-permute-start | bytes 16515080 | tf_op jit(solution)/shard_map/ppermute | solution.py:90
  136.8 2.7 %collective-permute-start.24 = (bf16[2,448,256]{2,1,0:T(8,128)(2,1)S(1)}, bf16[2,448,256]{2,1,0:T(8,128)(2,1)S(1)}, u32[]{:S(2)}, u32[]{:S(2)}) collective-permute-start(bf16[2,448,256]{2,1,0:T(8,128)(2,1)S(1)} %slice.150), channel_id=1, source_target_pairs={{0,192},{32,224},{64,0},{96,32},{128,64},{160,96},{192,128},{224,1... | collective-permute-start | bytes 1376264 | tf_op jit(solution)/shard_map/ppermute | solution.py:83
  140.5 2.4 %collective-permute-start.26 = (bf16[2,448,256]{2,1,0:T(8,128)(2,1)S(1)}, bf16[2,448,256]{2,1,0:T(8,128)(2,1)S(1)}, u32[]{:S(2)}, u32[]{:S(2)}) collective-permute-start(bf16[2,448,256]{2,1,0:T(8,128)(2,1)S(1)} %slice.151), channel_id=1, source_target_pairs={{0,24},{1,25},{2,26},{3,27},{4,28},{5,29},{6,30},{7,31},{8,0},{9,1... | collective-permute-start | bytes 1376264 | tf_op jit(solution)/shard_map/ppermute | solution.py:74
  142.9 7.2 %collective-permute-done.23.refs_6_ = bf16[2,448,256]{2,1,0:T(8,128)(2,1)S(1)} collective-permute-done((bf16[2,448,256]{2,1,0:T(8,128)(2,1)S(1)}, bf16[2,448,256]{2,1,0:T(8,128)(2,1)S(1)}, u32[]{:S(2)}, u32[]{:S(2)}) %collective-permute-start.23) | collective-permute-done | bytes 458784 | tf_op jit(solution)/shard_map/ppermute | solution.py:83
  150.1 3.1 %collective-permute-done.25.refs_8_ = bf16[2,448,256]{2,1,0:T(8,128)(2,1)S(1)} collective-permute-done((bf16[2,448,256]{2,1,0:T(8,128)(2,1)S(1)}, bf16[2,448,256]{2,1,0:T(8,128)(2,1)S(1)}, u32[]{:S(2)}, u32[]{:S(2)}) %collective-permute-start.25) | collective-permute-done | bytes 458784 | tf_op jit(solution)/shard_map/ppermute | solution.py:74
  155.0 3.4 %collective-permute-done.28.refs_11_ = bf16[8,448,256]{2,1,0:T(8,128)(2,1)S(1)} collective-permute-done((bf16[8,448,256]{2,1,0:T(8,128)(2,1)S(1)}, bf16[8,448,256]{2,1,0:T(8,128)(2,1)S(1)}, u32[]{:S(2)}, u32[]{:S(2)}) %collective-permute-start.28) | collective-permute-done | bytes 1835040 | tf_op jit(solution)/shard_map/ppermute | solution.py:90
  159.6 61.9 %newton_schulz.1 = bf16[8,48,448]{2,1,0:T(8,128)(2,1)} custom-call(bf16[48,3584]{1,0:T(8,128)(2,1)} %copy-done, bf16[4,448,256]{2,1,0:T(8,128)(2,1)} %copy-done.1, bf16[4,448,256]{2,1,0:T(8,128)(2,1)} %copy-done.2, bf16[4,448,256]{2,1,0:T(8,128)(2,1)} %copy-done.3, bf16[4,448,256]{2,1,0:T(8,128)(2,1)} %copy-done.4, bf16[4,448,256]{2,1,0:T(8,128)(2,1)} %copy-done.5, ...), custom_call_target="tpu_custom_call" | custom-call | tf_op jit(solution)/shard_map/newton_schulz/pallas_call | solution.py:271
  221.5 3.7 %all-to-all-start.3 = ((bf16[8,48,448]{2,1,0:T(8,128)(2,1)}), bf16[8,48,448]{2,1,0:T(8,128)(2,1)S(1)}, u32[]{:S(2)}, u32[]{:S(2)}) async-start(bf16[8,48,448]{2,1,0:T(8,128)(2,1)} %newton_schulz.1), calls=%async_computation.3 | async-start | bytes 786432 | tf_op jit(solution)/shard_map/all_to_all | solution.py:338
  226.2 7.2 %all-to-all-done.3 = bf16[8,48,448]{2,1,0:T(8,128)(2,1)S(1)} async-done(((bf16[8,48,448]{2,1,0:T(8,128)(2,1)}), bf16[8,48,448]{2,1,0:T(8,128)(2,1)S(1)}, u32[]{:S(2)}, u32[]{:S(2)}) %all-to-all-start.3) | async-done | bytes 344096 | tf_op jit(solution)/shard_map/all_to_all | solution.py:338
  (90 shorter events, 24.3 us)
Async XLA Ops:
  2.0 9.4 %collective-permute-start = (bf16[448,384]{1,0:T(8,128)(2,1)S(1)}, bf16[448,384]{1,0:T(8,128)(2,1)S(1)}, u32[]{:S(2)}, u32[]{:S(2)}) collective-permute-start(bf16[448,384]{1,0:T(8,128)(2,1)S(1)} %fusion.1.refs_0_), channel_id=1, source_target_pairs={{0,64},{32,96},{64,128},{96,160},{128,192},{160,224},{192,0},{224,... | collective-permute-start | bytes 1032200 | tf_op jit(solution)/shard_map/ppermute | solution.py:83
  4.2 17.5 %collective-permute-start.1 = (bf16[448,384]{1,0:T(8,128)(2,1)S(1)}, bf16[448,384]{1,0:T(8,128)(2,1)S(1)}, u32[]{:S(2)}, u32[]{:S(2)}) collective-permute-start(bf16[448,384]{1,0:T(8,128)(2,1)S(1)} %fusion.1.refs_0_), channel_id=1, source_target_pairs={{0,128},{32,160},{64,192},{96,224},{128,0},{160,32},{192,64},{224,... | collective-permute-start | bytes 1032200 | tf_op jit(solution)/shard_map/ppermute | solution.py:83
  6.8 16.4 %collective-permute-start.2 = (bf16[448,384]{1,0:T(8,128)(2,1)S(1)}, bf16[448,384]{1,0:T(8,128)(2,1)S(1)}, u32[]{:S(2)}, u32[]{:S(2)}) collective-permute-start(bf16[448,384]{1,0:T(8,128)(2,1)S(1)} %fusion.1.refs_0_), channel_id=1, source_target_pairs={{0,192},{32,224},{64,0},{96,32},{128,64},{160,96},{192,128},{224,1... | collective-permute-start | bytes 1032200 | tf_op jit(solution)/shard_map/ppermute | solution.py:83
  7.9 15.3 %collective-permute-start.3 = (bf16[448,384]{1,0:T(8,128)(2,1)S(1)}, bf16[448,384]{1,0:T(8,128)(2,1)S(1)}, u32[]{:S(2)}, u32[]{:S(2)}) collective-permute-start(bf16[448,384]{1,0:T(8,128)(2,1)S(1)} %fusion.1.refs_0_), channel_id=1, source_target_pairs={{0,32},{32,0},{64,96},{96,64},{128,160},{160,128},{192,224},{224,1... | collective-permute-start | bytes 1032200 | tf_op jit(solution)/shard_map/ppermute | solution.py:90
  11.4 11.8 %collective-permute-start.4 = (bf16[448,384]{1,0:T(8,128)(2,1)S(1)}, bf16[448,384]{1,0:T(8,128)(2,1)S(1)}, u32[]{:S(2)}, u32[]{:S(2)}) collective-permute-start(bf16[448,384]{1,0:T(8,128)(2,1)S(1)} %collective-permute-done.refs_1_), channel_id=1, source_target_pairs={{0,32},{32,0},{64,96},{96,64},{128,160},{160,128},{192,224},{224,1... | collective-permute-start | bytes 1032200 | tf_op jit(solution)/shard_map/ppermute | solution.py:90
  21.6 2.8 %collective-permute-start.5 = (bf16[448,384]{1,0:T(8,128)(2,1)S(1)}, bf16[448,384]{1,0:T(8,128)(2,1)S(1)}, u32[]{:S(2)}, u32[]{:S(2)}) collective-permute-start(bf16[448,384]{1,0:T(8,128)(2,1)S(1)} %collective-permute-done.1.refs_2_), channel_id=1, source_target_pairs={{0,32},{32,0},{64,96},{96,64},{128,160},{160,128},{192,224},{224,1... | collective-permute-start | bytes 1032200 | tf_op jit(solution)/shard_map/ppermute | solution.py:90
  23.2 1.8 collective-permute-start.6
  29.4 31.8 %all-to-all-start.1 = ((bf16[8,192,256]{2,1,0:T(8,128)(2,1)}), bf16[8,192,256]{2,1,0:T(8,128)(2,1)S(1)}, u32[]{:S(2)}, u32[]{:S(2)}) async-start(bf16[8,192,256]{2,1,0:T(8,128)(2,1)} %get-tuple-element.30), calls=%async_computation.1 | async-start | bytes 1572864 | tf_op jit(solution)/shard_map/all_to_all | solution.py:94
  37.6 8.3 %collective-permute-start.9 = (bf16[512,256]{1,0:T(8,128)(2,1)S(1)}, bf16[512,256]{1,0:T(8,128)(2,1)S(1)}, u32[]{:S(2)}, u32[]{:S(2)}) collective-permute-start(bf16[512,256]{1,0:T(8,128)(2,1)S(1)} %get-tuple-element.29), channel_id=1, source_target_pairs={{0,24},{1,25},{2,26},{3,27},{4,28},{5,29},{6,30},{7,31},{8,0},{9,1... | collective-permute-start | bytes 786440 | tf_op jit(solution)/shard_map/ppermute | solution.py:74
  40.1 9.0 %collective-permute-start.8 = (bf16[512,256]{1,0:T(8,128)(2,1)S(1)}, bf16[512,256]{1,0:T(8,128)(2,1)S(1)}, u32[]{:S(2)}, u32[]{:S(2)}) collective-permute-start(bf16[512,256]{1,0:T(8,128)(2,1)S(1)} %get-tuple-element.28), channel_id=1, source_target_pairs={{0,8},{1,9},{2,10},{3,11},{4,12},{5,13},{6,14},{7,15},{8,16},{9,17... | collective-permute-start | bytes 786440 | tf_op jit(solution)/shard_map/ppermute | solution.py:74
  40.1 12.8 %collective-permute-start.7 = (bf16[512,256]{1,0:T(8,128)(2,1)S(1)}, bf16[512,256]{1,0:T(8,128)(2,1)S(1)}, u32[]{:S(2)}, u32[]{:S(2)}) collective-permute-start(bf16[512,256]{1,0:T(8,128)(2,1)S(1)} %get-tuple-element.27), channel_id=1, source_target_pairs={{0,16},{1,17},{2,18},{3,19},{4,20},{5,21},{6,22},{7,23},{8,24},{9,... | collective-permute-start | bytes 786440 | tf_op jit(solution)/shard_map/ppermute | solution.py:74
  61.2 15.4 %all-to-all-start = ((bf16[8,64,256]{2,1,0:T(8,128)(2,1)}), bf16[8,64,256]{2,1,0:T(8,128)(2,1)S(1)}, u32[]{:S(2)}, u32[]{:S(2)}) async-start(bf16[8,64,256]{2,1,0:T(8,128)(2,1)} %bitcast), calls=%async_computation | async-start | bytes 524288 | tf_op jit(solution)/shard_map/all_to_all | solution.py:94
  64.7 11.9 %collective-permute-start.12 = (bf16[48,256]{1,0:T(8,128)(2,1)S(1)}, bf16[48,256]{1,0:T(8,128)(2,1)S(1)}, u32[]{:S(2)}, u32[]{:S(2)}) collective-permute-start(bf16[48,256]{1,0:T(8,128)(2,1)S(1)} %get-tuple-element.50), channel_id=1, source_target_pairs={{0,24},{1,25},{2,26},{3,27},{4,28},{5,29},{6,30},{7,31},{8,0},{9,1... | collective-permute-start | bytes 73736 | tf_op jit(solution)/shard_map/ppermute | solution.py:74
  67.3 9.4 %collective-permute-start.11 = (bf16[48,256]{1,0:T(8,128)(2,1)S(1)}, bf16[48,256]{1,0:T(8,128)(2,1)S(1)}, u32[]{:S(2)}, u32[]{:S(2)}) collective-permute-start(bf16[48,256]{1,0:T(8,128)(2,1)S(1)} %get-tuple-element.49), channel_id=1, source_target_pairs={{0,8},{1,9},{2,10},{3,11},{4,12},{5,13},{6,14},{7,15},{8,16},{9,17... | collective-permute-start | bytes 73736 | tf_op jit(solution)/shard_map/ppermute | solution.py:74
  67.3 9.4 %collective-permute-start.10 = (bf16[48,256]{1,0:T(8,128)(2,1)S(1)}, bf16[48,256]{1,0:T(8,128)(2,1)S(1)}, u32[]{:S(2)}, u32[]{:S(2)}) collective-permute-start(bf16[48,256]{1,0:T(8,128)(2,1)S(1)} %get-tuple-element.48), channel_id=1, source_target_pairs={{0,16},{1,17},{2,18},{3,19},{4,20},{5,21},{6,22},{7,23},{8,24},{9,... | collective-permute-start | bytes 73736 | tf_op jit(solution)/shard_map/ppermute | solution.py:74
  93.5 7.1 %collective-permute-start.15 = (bf16[448,256]{1,0:T(8,128)(2,1)S(1)}, bf16[448,256]{1,0:T(8,128)(2,1)S(1)}, u32[]{:S(2)}, u32[]{:S(2)}) collective-permute-start(bf16[448,256]{1,0:T(8,128)(2,1)S(1)} %bitcast.29), channel_id=1, source_target_pairs={{0,24},{1,25},{2,26},{3,27},{4,28},{5,29},{6,30},{7,31},{8,0},{9,1... | collective-permute-start | bytes 688136 | tf_op jit(solution)/shard_map/ppermute | solution.py:74
  96.0 6.5 %collective-permute-start.14 = (bf16[448,256]{1,0:T(8,128)(2,1)S(1)}, bf16[448,256]{1,0:T(8,128)(2,1)S(1)}, u32[]{:S(2)}, u32[]{:S(2)}) collective-permute-start(bf16[448,256]{1,0:T(8,128)(2,1)S(1)} %bitcast.30), channel_id=1, source_target_pairs={{0,16},{1,17},{2,18},{3,19},{4,20},{5,21},{6,22},{7,23},{8,24},{9,... | collective-permute-start | bytes 688136 | tf_op jit(solution)/shard_map/ppermute | solution.py:74
  97.6 10.9 %collective-permute-start.13 = (bf16[448,256]{1,0:T(8,128)(2,1)S(1)}, bf16[448,256]{1,0:T(8,128)(2,1)S(1)}, u32[]{:S(2)}, u32[]{:S(2)}) collective-permute-start(bf16[448,256]{1,0:T(8,128)(2,1)S(1)} %bitcast.31), channel_id=1, source_target_pairs={{0,8},{1,9},{2,10},{3,11},{4,12},{5,13},{6,14},{7,15},{8,16},{9,17... | collective-permute-start | bytes 688136 | tf_op jit(solution)/shard_map/ppermute | solution.py:74
  98.3 10.4 %collective-permute-start.18 = (bf16[448,256]{1,0:T(8,128)(2,1)S(1)}, bf16[448,256]{1,0:T(8,128)(2,1)S(1)}, u32[]{:S(2)}, u32[]{:S(2)}) collective-permute-start(bf16[448,256]{1,0:T(8,128)(2,1)S(1)} %pad_maximum_fusion.3), channel_id=1, source_target_pairs={{0,192},{32,224},{64,0},{96,32},{128,64},{160,96},{192,128},{224,1... | collective-permute-start | bytes 688136 | tf_op jit(solution)/shard_map/ppermute | solution.py:83
  99.7 8.9 %collective-permute-start.17 = (bf16[448,256]{1,0:T(8,128)(2,1)S(1)}, bf16[448,256]{1,0:T(8,128)(2,1)S(1)}, u32[]{:S(2)}, u32[]{:S(2)}) collective-permute-start(bf16[448,256]{1,0:T(8,128)(2,1)S(1)} %pad_maximum_fusion.3), channel_id=1, source_target_pairs={{0,128},{32,160},{64,192},{96,224},{128,0},{160,32},{192,64},{224,... | collective-permute-start | bytes 688136 | tf_op jit(solution)/shard_map/ppermute | solution.py:83
  100.6 9.6 %collective-permute-start.16 = (bf16[448,256]{1,0:T(8,128)(2,1)S(1)}, bf16[448,256]{1,0:T(8,128)(2,1)S(1)}, u32[]{:S(2)}, u32[]{:S(2)}) collective-permute-start(bf16[448,256]{1,0:T(8,128)(2,1)S(1)} %pad_maximum_fusion.3), channel_id=1, source_target_pairs={{0,64},{32,96},{64,128},{96,160},{128,192},{160,224},{192,0},{224,... | collective-permute-start | bytes 688136 | tf_op jit(solution)/shard_map/ppermute | solution.py:83
  110.4 19.1 %collective-permute-start.19 = (bf16[4,448,256]{2,1,0:T(8,128)(2,1)S(1)}, bf16[4,448,256]{2,1,0:T(8,128)(2,1)S(1)}, u32[]{:S(2)}, u32[]{:S(2)}) collective-permute-start(bf16[4,448,256]{2,1,0:T(8,128)(2,1)S(1)} %pad_maximum_fusion.1.refs_0_), channel_id=1, source_target_pairs={{0,64},{32,96},{64,128},{96,160},{128,192},{160,224},{192,0},{224,... | collective-permute-start | bytes 2752520 | tf_op jit(solution)/shard_map/ppermute | solution.py:83
  110.4 19.1 %collective-permute-start.20 = (bf16[4,448,256]{2,1,0:T(8,128)(2,1)S(1)}, bf16[4,448,256]{2,1,0:T(8,128)(2,1)S(1)}, u32[]{:S(2)}, u32[]{:S(2)}) collective-permute-start(bf16[4,448,256]{2,1,0:T(8,128)(2,1)S(1)} %pad_maximum_fusion.2.refs_1_), channel_id=1, source_target_pairs={{0,8},{1,9},{2,10},{3,11},{4,12},{5,13},{6,14},{7,15},{8,16},{9,17... | collective-permute-start | bytes 2752520 | tf_op jit(solution)/shard_map/ppermute | solution.py:74
  110.5 19.1 %collective-permute-start.21 = (bf16[4,448,256]{2,1,0:T(8,128)(2,1)S(1)}, bf16[4,448,256]{2,1,0:T(8,128)(2,1)S(1)}, u32[]{:S(2)}, u32[]{:S(2)}) collective-permute-start(bf16[4,448,256]{2,1,0:T(8,128)(2,1)S(1)} %pad_maximum_fusion.1.refs_0_), channel_id=1, source_target_pairs={{0,192},{32,224},{64,0},{96,32},{128,64},{160,96},{192,128},{224,1... | collective-permute-start | bytes 2752520 | tf_op jit(solution)/shard_map/ppermute | solution.py:83
  113.1 16.6 %collective-permute-start.22 = (bf16[4,448,256]{2,1,0:T(8,128)(2,1)S(1)}, bf16[4,448,256]{2,1,0:T(8,128)(2,1)S(1)}, u32[]{:S(2)}, u32[]{:S(2)}) collective-permute-start(bf16[4,448,256]{2,1,0:T(8,128)(2,1)S(1)} %pad_maximum_fusion.2.refs_1_), channel_id=1, source_target_pairs={{0,24},{1,25},{2,26},{3,27},{4,28},{5,29},{6,30},{7,31},{8,0},{9,1... | collective-permute-start | bytes 2752520 | tf_op jit(solution)/shard_map/ppermute | solution.py:74
  130.5 22.7 %collective-permute-start.27 = (bf16[24,448,256]{2,1,0:T(8,128)(2,1)S(1)}, bf16[24,448,256]{2,1,0:T(8,128)(2,1)}, u32[]{:S(2)}, u32[]{:S(2)}) collective-permute-start(bf16[24,448,256]{2,1,0:T(8,128)(2,1)S(1)} %constant_dynamic-update-slice_fusion), channel_id=1, source_target_pairs={{0,32},{32,0},{64,96},{96,64},{128,160},{160,128},{192,224},{224,1... | collective-permute-start | bytes 16515080 | tf_op jit(solution)/shard_map/ppermute | solution.py:90
  136.8 13.3 %collective-permute-start.23 = (bf16[2,448,256]{2,1,0:T(8,128)(2,1)S(1)}, bf16[2,448,256]{2,1,0:T(8,128)(2,1)S(1)}, u32[]{:S(2)}, u32[]{:S(2)}) collective-permute-start(bf16[2,448,256]{2,1,0:T(8,128)(2,1)S(1)} %slice.148), channel_id=1, source_target_pairs={{0,64},{32,96},{64,128},{96,160},{128,192},{160,224},{192,0},{224,... | collective-permute-start | bytes 1376264 | tf_op jit(solution)/shard_map/ppermute | solution.py:83
  136.8 13.3 %collective-permute-start.24 = (bf16[2,448,256]{2,1,0:T(8,128)(2,1)S(1)}, bf16[2,448,256]{2,1,0:T(8,128)(2,1)S(1)}, u32[]{:S(2)}, u32[]{:S(2)}) collective-permute-start(bf16[2,448,256]{2,1,0:T(8,128)(2,1)S(1)} %slice.150), channel_id=1, source_target_pairs={{0,192},{32,224},{64,0},{96,32},{128,64},{160,96},{192,128},{224,1... | collective-permute-start | bytes 1376264 | tf_op jit(solution)/shard_map/ppermute | solution.py:83
  139.5 13.7 %collective-permute-start.25 = (bf16[2,448,256]{2,1,0:T(8,128)(2,1)S(1)}, bf16[2,448,256]{2,1,0:T(8,128)(2,1)S(1)}, u32[]{:S(2)}, u32[]{:S(2)}) collective-permute-start(bf16[2,448,256]{2,1,0:T(8,128)(2,1)S(1)} %slice.149), channel_id=1, source_target_pairs={{0,8},{1,9},{2,10},{3,11},{4,12},{5,13},{6,14},{7,15},{8,16},{9,17... | collective-permute-start | bytes 1376264 | tf_op jit(solution)/shard_map/ppermute | solution.py:74
  140.5 12.7 %collective-permute-start.26 = (bf16[2,448,256]{2,1,0:T(8,128)(2,1)S(1)}, bf16[2,448,256]{2,1,0:T(8,128)(2,1)S(1)}, u32[]{:S(2)}, u32[]{:S(2)}) collective-permute-start(bf16[2,448,256]{2,1,0:T(8,128)(2,1)S(1)} %slice.151), channel_id=1, source_target_pairs={{0,24},{1,25},{2,26},{3,27},{4,28},{5,29},{6,30},{7,31},{8,0},{9,1... | collective-permute-start | bytes 1376264 | tf_op jit(solution)/shard_map/ppermute | solution.py:74
  153.5 4.9 %collective-permute-start.28 = (bf16[8,448,256]{2,1,0:T(8,128)(2,1)S(1)}, bf16[8,448,256]{2,1,0:T(8,128)(2,1)S(1)}, u32[]{:S(2)}, u32[]{:S(2)}) collective-permute-start(bf16[8,448,256]{2,1,0:T(8,128)(2,1)S(1)} %pad_maximum_fusion), channel_id=1, source_target_pairs={{0,32},{32,0},{64,96},{96,64},{128,160},{160,128},{192,224},{224,1... | collective-permute-start | bytes 5505032 | tf_op jit(solution)/shard_map/ppermute | solution.py:90
  221.5 11.8 %all-to-all-start.3 = ((bf16[8,48,448]{2,1,0:T(8,128)(2,1)}), bf16[8,48,448]{2,1,0:T(8,128)(2,1)S(1)}, u32[]{:S(2)}, u32[]{:S(2)}) async-start(bf16[8,48,448]{2,1,0:T(8,128)(2,1)} %newton_schulz.1), calls=%async_computation.3 | async-start | bytes 786432 | tf_op jit(solution)/shard_map/all_to_all | solution.py:338
  (14 other events, 273.4 us)
